TPU v7x, 512 devices: a whole 4x8x8 slice. The times are simulated.
512 devices in a mesh: section: 8 (over z_lo, core), table: 64 (over x, y, z_hi).
Axes of the slice: x: 4, y: 8, z: 8 (z_hi: 2, z_lo: 4; z = z_hi * 4 + z_lo), core: 2. Of those that a mesh axis runs over, the one named last changes fastest.
Arguments:
- gate_a: bfloat16 [8, 4096, 4096], P('section', 'table'), may hold values from -6 to 6
- cotangent_a: bfloat16 [8, 4096, 4096], P('section', 'table'), may hold values from -6 to 6
- gate_b: bfloat16 [8, 4096, 4096], P('section', 'table'), may hold values from -6 to 6
- table: bfloat16 [4096, 4096], P('table'), may hold values from -6 to 6
- row_ids: int32 [8, 2, 64, 128], P('section', None, 'table'), may hold values from 0 to 4095, as said below
- slots: int32 [8, 2, 4096, 128], P('section', None, 'table'), may hold values from 0 to 127, as said below
- weights: float32 [8, 2, 4096, 128], P('section', None, 'table'), may hold values from 0.02 to 0.2
Outputs:
- mixed_b: bfloat16 [8, 4096, 4096], P('section', 'table')
- grad_gate_a: bfloat16 [8, 4096, 4096], P('section', 'table')
- grad_weights_a: float32 [8, 4096, 128], P('section', 'table')
- grad_table: float32 [4096, 4096], P('table', 'section')
Inputs may be any that keep to these rules, and one draw needn't show every extreme that they name: `row_ids`: row r is held by index r // 64 of table. The 128 ids of one list are distinct, and at most 8 of them are held by one index of table; in every section and micro-batch some index of table holds 8 ids of every device's list. `slots`: the 32 picks of one token and head are distinct, and every position of a device's list is picked by some token of that device and micro-batch.
All inputs are finite; a program needn't handle non-finite values.
Results may differ from a plain program's by a relative error of at most 0.0057.
Values may be sent and summed in bfloat16 or wider, within the bound.
No kernel may reach another device: no remote copies, remote signals or barrier semaphores. Data moves between devices by JAX's collectives and lax.ppermute only.
A program may use at most 128 MiB of HBM per device.

v0:
```python
import jax
import jax.numpy as jnp
from jax import lax
from jax.sharding import Mesh
from jax.sharding import PartitionSpec as P

ROW_LIMIT = 8
TABLE = ("table_0", "table_1", "table_2")
SECTION = ("section_0", "section_1")


def reduced_to_own(tiles, axes, turns):
    inside = tiles.shape[1:]
    tiles = tiles.reshape(*(lax.axis_size(a) for a in axes), *inside)
    tiles = jnp.moveaxis(tiles, turns, range(len(axes))).reshape(-1, *inside)
    for k in turns:
        tiles = lax.psum_scatter(tiles, axes[k], scatter_dimension=0, tiled=True)
    return tiles[0]


def in_blocks(shard, dim, count):
    lengths = shard.shape
    tiles = shard.reshape(*lengths[:dim], count, lengths[dim] // count, *lengths[dim + 1 :])
    return jnp.moveaxis(tiles, dim, 0)


def summed_rows(shard, axes, turns, dim):
    count = lax.axis_size(axes)
    return reduced_to_own(in_blocks(shard, dim, count), axes, turns)


def laid_out(tiles, dim):
    lengths = list(tiles.shape[1:])
    lengths[dim] *= tiles.shape[0]
    return jnp.moveaxis(tiles, 0, dim).reshape(lengths)


def exchange_in_order(tiles, axes, turns):
    lengths = [lax.axis_size(a) for a in axes]
    tiles = tiles.reshape(*lengths, *tiles.shape[1:])
    for k in turns:
        tiles = lax.all_to_all(tiles, axes[k], split_axis=k, concat_axis=k, tiled=True)
    return tiles.reshape(-1, *tiles.shape[len(axes) :])


def stepwise_exchange(shard, axes, turns, split_dim, concat_dim):
    tiles = in_blocks(shard, split_dim, lax.axis_size(axes))
    return laid_out(exchange_in_order(tiles, axes, turns), concat_dim)


def bucket_rows(row_list, rows_dev, owners, capacity):
    owner_of = row_list // rows_dev
    offset = row_list - owner_of * rows_dev
    member = (owner_of[:, None] == jnp.arange(owners, dtype=jnp.int32)[None, :]).astype(jnp.int32)
    earlier = jnp.cumsum(member, axis=0) - member
    position = jnp.sum(earlier * member, axis=1)
    slot_place = owner_of * capacity + position
    requests = jnp.full((owners * capacity,), -1, jnp.int32).at[slot_place].set(offset)
    return (requests.reshape(owners, capacity), slot_place)


def combine_table(slot_rows, weight_rows, listed):
    matches = slot_rows[:, :, None] == jnp.arange(listed, dtype=jnp.int32)[None, None, :]
    return jnp.sum(
        jnp.where(matches, weight_rows[:, :, None], jnp.zeros_like(weight_rows[:, :, None])), axis=1
    ).astype(jnp.bfloat16)


def local(gate_a, cotangent_a, gate_b, table, row_ids, slots, weights):
    owners = lax.axis_size(TABLE)
    rows_dev = table.shape[0]
    features = table.shape[1]
    listed = row_ids.shape[-1]
    requests_a, place_a = bucket_rows(row_ids[0, 0, 0], rows_dev, owners, ROW_LIMIT)
    requests_b, place_b = bucket_rows(row_ids[0, 1, 0], rows_dev, owners, ROW_LIMIT)

    def serve_rows(received):
        present = received >= 0
        picked = jnp.take(table, jnp.maximum(received, 0), axis=0)
        return jnp.where(present[..., None], picked, jnp.zeros_like(picked))

    received = (
        stepwise_exchange(requests_a, TABLE, (0, 1, 2), 0, 0),
        stepwise_exchange(requests_b, TABLE, (0, 1, 2), 0, 0),
    )
    fetched_a = lax.all_to_all(
        serve_rows(received[0]), TABLE, split_axis=0, concat_axis=0, tiled=True
    )
    fetched_b = lax.all_to_all(
        serve_rows(received[1]), TABLE, split_axis=0, concat_axis=0, tiled=True
    )
    kept_a = received[0]
    fetched_rows = fetched_a.reshape(-1, features)[place_a]
    mixing = combine_table(slots[0, 0], weights[0, 0], listed)
    memory = jnp.dot(mixing, fetched_rows, preferred_element_type=jnp.float32)
    gate_value = gate_a[0].astype(jnp.float32)
    incoming = cotangent_a[0].astype(jnp.float32)
    logistic = jax.nn.sigmoid(gate_value)
    grad_gate = (incoming * memory * logistic * (1.0 + gate_value * (1.0 - logistic))).astype(
        jnp.bfloat16
    )
    grad_memory = (incoming * gate_value * logistic).astype(jnp.bfloat16)
    row_scores = lax.dot_general(
        grad_memory, fetched_rows, (((1,), (1,)), ((), ())), preferred_element_type=jnp.float32
    )
    grad_weights = jnp.take_along_axis(row_scores, slots[0, 0], axis=1)
    grad_rows = lax.dot_general(
        mixing, grad_memory, (((0,), (0,)), ((), ())), preferred_element_type=jnp.float32
    ).astype(jnp.bfloat16)
    outgoing = (
        jnp.zeros((owners * ROW_LIMIT, features), jnp.bfloat16)
        .at[place_a]
        .set(grad_rows)
        .reshape(owners, ROW_LIMIT, features)
    )
    arrived = lax.all_to_all(outgoing, TABLE, split_axis=0, concat_axis=0, tiled=True)
    owner_match = (kept_a.reshape(1, -1) == jnp.arange(rows_dev, dtype=jnp.int32)[:, None]).astype(
        jnp.bfloat16
    )
    owner_sum = jnp.dot(
        owner_match, arrived.reshape(-1, features), preferred_element_type=jnp.float32
    )
    grad_table = summed_rows(owner_sum, SECTION, (1, 0), 1)
    grad_gate_a, grad_weights_a, grad_table = (grad_gate[None], grad_weights[None], grad_table)
    fetched_rows = fetched_b.reshape(-1, features)[place_b]
    mixing = combine_table(slots[0, 1], weights[0, 1], listed)
    memory = jnp.dot(mixing, fetched_rows, preferred_element_type=jnp.float32)
    gate_value = gate_b[0].astype(jnp.float32)
    mixed_b = (gate_value * jax.nn.sigmoid(gate_value) * memory).astype(jnp.bfloat16)[None]
    return (mixed_b, grad_gate_a, grad_weights_a, grad_table)


def solution(mesh):
    finer = Mesh(
        mesh.devices.reshape(4, 2, 4, 8, 2),
        ("section_0", "section_1", "table_0", "table_1", "table_2"),
    )
    return jax.shard_map(
        local,
        mesh=finer,
        in_specs=(
            P(SECTION, TABLE, None),
            P(SECTION, TABLE, None),
            P(SECTION, TABLE, None),
            P(TABLE, None),
            P(SECTION, None, TABLE, None),
            P(SECTION, None, TABLE, None),
            P(SECTION, None, TABLE, None),
        ),
        out_specs=(
            P(SECTION, TABLE, None),
            P(SECTION, TABLE, None),
            P(SECTION, TABLE, None),
            P(TABLE, SECTION),
        ),
        check_vma=False,
    )
```

profile of v0, /device:TPU:1, one launch (start us, length us, event | category | flops | bytes accessed | tf_op | source)
XLA Modules:
  0.0 413.7 jit_solution(17236063606177621228)
XLA Ops:
  11.1 4.8 %all-to-all-start.4 = ((s32[4,1,128]{2,1,0:T(1,128)}), s32[4,1,128]{2,1,0:T(1,128)S(1)}, u32[]{:S(2)}, u32[]{:S(2)}) async-start(s32[4,1,128]{2,1,0:T(1,128)} %reshape.433), calls=%async_computation.4 | async-start | bytes 4096 | tf_op jit(solution)/shard_map/all_to_all | solution.py:42
  17.7 2.2 all-to-all-done.4
  20.0 3.2 all-to-all-start
  23.2 1.5 fusion.18
  27.2 6.8 %all-to-all-start.5 = ((s32[4,8,2,1,8]{4,2,0,3,1:T(2,128)}), s32[4,8,2,1,8]{4,2,0,3,1:T(2,128)S(1)}, u32[]{:S(2)}, u32[]{:S(2)}) async-start(s32[4,8,2,1,8]{4,2,0,3,1:T(2,128)} %copy.37), calls=%async_computation.5 | async-start | bytes 65536 | tf_op jit(solution)/shard_map/all_to_all | solution.py:42
  36.2 4.7 %all-to-all-done.5 = s32[4,8,2,1,8]{4,2,0,3,1:T(2,128)S(1)} async-done(((s32[4,8,2,1,8]{4,2,0,3,1:T(2,128)}), s32[4,8,2,1,8]{4,2,0,3,1:T(2,128)S(1)}, u32[]{:S(2)}, u32[]{:S(2)}) %all-to-all-start.5) | async-done | bytes 2080 | tf_op jit(solution)/shard_map/all_to_all | solution.py:42
  40.9 3.3 all-to-all-start.1
  45.7 5.3 %all-to-all-done.1 = s32[4,8,2,1,8]{4,2,0,3,1:T(2,128)S(1)} async-done(((s32[4,8,2,1,8]{4,2,0,3,1:T(2,128)}), s32[4,8,2,1,8]{4,2,0,3,1:T(2,128)S(1)}, u32[]{:S(2)}, u32[]{:S(2)}) %all-to-all-start.1) | async-done | bytes 2080 | tf_op jit(solution)/shard_map/all_to_all | solution.py:42
  51.0 10.0 %all-to-all-start.6 = ((s32[2,1,256]{2,1,0:T(1,128)}), s32[2,1,256]{2,1,0:T(1,128)S(1)}, u32[]{:S(2)}, u32[]{:S(2)}) async-start(s32[2,1,256]{2,1,0:T(1,128)} %reshape.435), calls=%async_computation.6 | async-start | bytes 4096 | tf_op jit(solution)/shard_map/all_to_all | solution.py:42
  61.0 2.8 select_reduce_fusion
  64.5 3.1 all-to-all-done.6
  67.6 3.6 all-to-all-start.2
  71.6 4.7 %scatter_custom_fusion.2 = bf16[512,4096]{1,0:T(8,128)(2,1)} fusion(s32[128]{0:T(128)S(1)} %get-tuple-element.13, bf16[128,4096]{1,0:T(8,128)(2,1)S(1)} %convolution_convert_fusion, bf16[]{:T(256)} %constant.68.clone.1), kind=kCustom, calls=%fused_computation.25 | custom fusion | bytes 4194306 | tf_op jit(solution)/shard_map/scatter | solution.py:113
  77.7 8.7 %all-to-all-start.8 = ((bf16[64,8,4096]{2,1,0:T(8,128)(2,1)}), bf16[64,8,4096]{2,1,0:T(8,128)(2,1)}, u32[]{:S(2)}, u32[]{:S(2)}) async-start(bf16[64,8,4096]{2,1,0:T(8,128)(2,1)} %bitcast.146), calls=%async_computation.8 | async-start | bytes 8388608 | tf_op jit(solution)/shard_map/all_to_all | solution.py:116
  87.4 4.4 %gather_fusion.4 = bf16[512,4096]{1,0:T(8,128)(2,1)} fusion(bf16[64,4096]{1,0:T(8,128)(2,1)S(1)} %copy-done, s32[1024]{0:T(1024)S(1)} %pad_clamp_fusion.1), kind=kCustom, calls=%fused_computation.1.clone | custom fusion | bytes 8390656 | tf_op jit(solution)/shard_map/jit(_take)/gather | solution.py:79
  91.8 3.9 fusion.6
  95.7 91.3 %all-to-all-done.8 = bf16[64,8,4096]{2,1,0:T(8,128)(2,1)} async-done(((bf16[64,8,4096]{2,1,0:T(8,128)(2,1)}), bf16[64,8,4096]{2,1,0:T(8,128)(2,1)}, u32[]{:S(2)}, u32[]{:S(2)}) %all-to-all-start.8) | async-done | bytes 4194336 | tf_op jit(solution)/shard_map/all_to_all | solution.py:116
  187.0 8.2 %all-to-all-start.7 = ((bf16[64,8,4096]{2,1,0:T(8,128)(2,1)}), bf16[64,8,4096]{2,1,0:T(8,128)(2,1)}, u32[]{:S(2)}, u32[]{:S(2)}) async-start(bf16[64,8,4096]{2,1,0:T(8,128)(2,1)} %fusion.6), calls=%async_computation.7 | async-start | bytes 8388608 | tf_op jit(solution)/shard_map/all_to_all | solution.py:86
  196.2 4.4 %gather_fusion.3 = bf16[512,4096]{1,0:T(8,128)(2,1)} fusion(bf16[64,4096]{1,0:T(8,128)(2,1)S(1)} %copy-done, s32[1024]{0:T(1024)S(1)} %pad_clamp_fusion.3), kind=kCustom, calls=%fused_computation.clone | custom fusion | bytes 8390656 | tf_op jit(solution)/shard_map/jit(_take)/gather | solution.py:79
  200.5 3.9 fusion.7
  204.5 84.7 %all-to-all-done.7 = bf16[64,8,4096]{2,1,0:T(8,128)(2,1)} async-done(((bf16[64,8,4096]{2,1,0:T(8,128)(2,1)}), bf16[64,8,4096]{2,1,0:T(8,128)(2,1)}, u32[]{:S(2)}, u32[]{:S(2)}) %all-to-all-start.7) | async-done | bytes 4194336 | tf_op jit(solution)/shard_map/all_to_all | solution.py:86
  289.2 11.1 %all-to-all-start.3 = ((bf16[64,8,4096]{2,1,0:T(8,128)(2,1)}), bf16[64,8,4096]{2,1,0:T(8,128)(2,1)}, u32[]{:S(2)}, u32[]{:S(2)}) async-start(bf16[64,8,4096]{2,1,0:T(8,128)(2,1)} %fusion.7), calls=%async_computation.3 | async-start | bytes 8388608 | tf_op jit(solution)/shard_map/all_to_all | solution.py:89
  300.5 6.5 %copy.42 = bf16[4096,512]{1,0:T(8,128)(2,1)} copy(bf16[4096,512]{0,1:T(8,128)(2,1)} %bitcast.33) | data formatting | bytes 8388608 | tf_op jit(solution)/shard_map/dot_general | solution.py:120
  307.0 3.6 fusion.20
  311.8 2.8 select_reduce_fusion.1
  314.7 4.9 %gather_fusion.1 = bf16[128,4096]{1,0:T(8,128)(2,1)S(1)} fusion(bf16[512,4096]{1,0:T(8,128)(2,1)} %bitcast.21, s32[1024]{0:T(1024)S(1)} %pad_clamp_fusion), kind=kCustom, calls=%fused_computation.3 | custom fusion | bytes 2097664 | tf_op jit(solution)/shard_map/gather | solution.py:93
  319.6 13.9 %reduce-scatter.3.cloned.1.call-done = f32[4,64,512]{2,1,0:T(8,128)} async-done(((f32[8,64,512]{2,1,0:T(8,128)}), f32[4,64,512]{2,1,0:T(8,128)}) %reduce-scatter.3.cloned.1.call-update) | async-done | bytes 524304 | tf_op jit(solution)/shard_map/reduce_scatter | solution.py:17
  334.0 50.7 %gather_fusion.2 = f32[8192]{0:T(1024)S(1)} fusion(f32[64,128]{1,0:T(8,128)S(1)} %fusion.38, s32[8192]{0:T(1024)S(1)} %fusion.28), kind=kCustom, calls=%fused_computation.4 | custom fusion | bytes 131072 | tf_op jit(solution)/shard_map/jit(take_along_axis)/gather | solution.py:106
  384.7 12.8 %all-to-all-done.3 = bf16[64,8,4096]{2,1,0:T(8,128)(2,1)} async-done(((bf16[64,8,4096]{2,1,0:T(8,128)(2,1)}), bf16[64,8,4096]{2,1,0:T(8,128)(2,1)}, u32[]{:S(2)}, u32[]{:S(2)}) %all-to-all-start.3) | async-done | bytes 4194336 | tf_op jit(solution)/shard_map/all_to_all | solution.py:89
  397.5 4.9 %gather_fusion = bf16[128,4096]{1,0:T(8,128)(2,1)S(1)} fusion(bf16[512,4096]{1,0:T(8,128)(2,1)} %bitcast.10, s32[1024]{0:T(1024)S(1)} %pad_clamp_fusion.2), kind=kCustom, calls=%fused_computation.2 | custom fusion | bytes 2097664 | tf_op jit(solution)/shard_map/gather | solution.py:125
  403.1 2.3 fusion.4
  405.4 1.4 fusion.5
  (72 shorter events, 18.7 us)
Async XLA Ops:
  7.2 80.2 %copy-start = (bf16[64,4096]{1,0:T(8,128)(2,1)S(1)}, bf16[64,4096]{1,0:T(8,128)(2,1)}, u32[]{:S(2)}) copy-start(bf16[64,4096]{1,0:T(8,128)(2,1)} %param.12) | copy-start | bytes 1572868
  11.1 8.9 %all-to-all-start.4 = ((s32[4,1,128]{2,1,0:T(1,128)}), s32[4,1,128]{2,1,0:T(1,128)S(1)}, u32[]{:S(2)}, u32[]{:S(2)}) async-start(s32[4,1,128]{2,1,0:T(1,128)} %reshape.433), calls=%async_computation.4 | async-start | bytes 4096 | tf_op jit(solution)/shard_map/all_to_all | solution.py:42
  20.0 7.2 %all-to-all-start = ((s32[4,1,128]{2,1,0:T(1,128)}), s32[4,1,128]{2,1,0:T(1,128)S(1)}, u32[]{:S(2)}, u32[]{:S(2)}) async-start(s32[4,1,128]{2,1,0:T(1,128)} %reshape.429), calls=%async_computation | async-start | bytes 4096 | tf_op jit(solution)/shard_map/all_to_all | solution.py:42
  27.2 13.7 %all-to-all-start.5 = ((s32[4,8,2,1,8]{4,2,0,3,1:T(2,128)}), s32[4,8,2,1,8]{4,2,0,3,1:T(2,128)S(1)}, u32[]{:S(2)}, u32[]{:S(2)}) async-start(s32[4,8,2,1,8]{4,2,0,3,1:T(2,128)} %copy.37), calls=%async_computation.5 | async-start | bytes 65536 | tf_op jit(solution)/shard_map/all_to_all | solution.py:42
  40.9 10.1 %all-to-all-start.1 = ((s32[4,8,2,1,8]{4,2,0,3,1:T(2,128)}), s32[4,8,2,1,8]{4,2,0,3,1:T(2,128)S(1)}, u32[]{:S(2)}, u32[]{:S(2)}) async-start(s32[4,8,2,1,8]{4,2,0,3,1:T(2,128)} %copy.33), calls=%async_computation.1 | async-start | bytes 65536 | tf_op jit(solution)/shard_map/all_to_all | solution.py:42
  51.0 16.5 %all-to-all-start.6 = ((s32[2,1,256]{2,1,0:T(1,128)}), s32[2,1,256]{2,1,0:T(1,128)S(1)}, u32[]{:S(2)}, u32[]{:S(2)}) async-start(s32[2,1,256]{2,1,0:T(1,128)} %reshape.435), calls=%async_computation.6 | async-start | bytes 4096 | tf_op jit(solution)/shard_map/all_to_all | solution.py:42
  67.6 10.1 %all-to-all-start.2 = ((s32[2,1,256]{2,1,0:T(1,128)}), s32[2,1,256]{2,1,0:T(1,128)S(1)}, u32[]{:S(2)}, u32[]{:S(2)}) async-start(s32[2,1,256]{2,1,0:T(1,128)} %reshape.431), calls=%async_computation.2 | async-start | bytes 4096 | tf_op jit(solution)/shard_map/all_to_all | solution.py:42
  77.7 109.3 %all-to-all-start.8 = ((bf16[64,8,4096]{2,1,0:T(8,128)(2,1)}), bf16[64,8,4096]{2,1,0:T(8,128)(2,1)}, u32[]{:S(2)}, u32[]{:S(2)}) async-start(bf16[64,8,4096]{2,1,0:T(8,128)(2,1)} %bitcast.146), calls=%async_computation.8 | async-start | bytes 8388608 | tf_op jit(solution)/shard_map/all_to_all | solution.py:116
  187.0 102.2 %all-to-all-start.7 = ((bf16[64,8,4096]{2,1,0:T(8,128)(2,1)}), bf16[64,8,4096]{2,1,0:T(8,128)(2,1)}, u32[]{:S(2)}, u32[]{:S(2)}) async-start(bf16[64,8,4096]{2,1,0:T(8,128)(2,1)} %fusion.6), calls=%async_computation.7 | async-start | bytes 8388608 | tf_op jit(solution)/shard_map/all_to_all | solution.py:86
  289.2 108.3 %all-to-all-start.3 = ((bf16[64,8,4096]{2,1,0:T(8,128)(2,1)}), bf16[64,8,4096]{2,1,0:T(8,128)(2,1)}, u32[]{:S(2)}, u32[]{:S(2)}) async-start(bf16[64,8,4096]{2,1,0:T(8,128)(2,1)} %fusion.7), calls=%async_computation.3 | async-start | bytes 8388608 | tf_op jit(solution)/shard_map/all_to_all | solution.py:89
  300.3 33.2 %reduce-scatter.3.cloned.1.call-start = ((), (), s32[]{:S(2)}) async-start(), calls=%async_computation.11 | async-start | bytes 1572864 | tf_op jit(solution)/shard_map/reduce_scatter | solution.py:17
  307.0 7.6 %copy-start.3 = (s32[1,2,64,128]{3,2,1,0:T(8,128)S(1)}, s32[1,2,64,128]{3,2,1,0:T(8,128)}, u32[]{:S(2)}) copy-start(s32[1,2,64,128]{3,2,1,0:T(8,128)} %param.14) | copy-start | bytes 196612
  311.8 95.1 %reduce-scatter.5.cloned.1.call-start = ((), (), s32[]{:S(2)}) async-start(), calls=%async_computation.12 | async-start | bytes 655360 | tf_op jit(solution)/shard_map/reduce_scatter | solution.py:17
  402.5 2.9 copy-start.1
  402.5 2.9 copy-start.2
Sparse Core Ops, SparseCore 0:
  311.9 21.5 reduce-scatter.2
  337.2 67.2 reduce-scatter.4
where the time goes:
time: 420 us; the launch traced here: 414 us
  waiting for transfers between devices  220 us (52%)
  local copies, waits for them, and re-layouts  90.8 us (22%)
  starting transfers between devices  59.8 us (14%)
  other arithmetic  20.4 us (5%)
  between operations  14.4 us (3%)
  matrix products  8.24 us (2%)
    all_to_all x1, waiting for transfers between devices, local(): lax.all_to_all(outgoing, TABLE, split_axis=0, concat_axis=0, tiled=True)  91.3 us
    all_to_all x1, waiting for transfers between devices, local(): lax.all_to_all(serve_rows(received[0]), TABLE, split_axis=0, concat_axis=...  84.7 us
    gather x1, local copies, waits for them, and re-layouts, local(): grad_weights = jnp.take_along_axis(row_scores, slots[0, 0], axis=1)  50.7 us
    all_to_all x6, starting transfers between devices, exchange_in_order(): lax.all_to_all(tiles, axes[k], split_axis=k, concat_axis=k, tiled=True)  31.8 us
    all_to_all x6, waiting for transfers between devices, exchange_in_order(): lax.all_to_all(tiles, axes[k], split_axis=k, concat_axis=k, tiled=True)  17.2 us
    reduce_scatter x2, waiting for transfers between devices, reduced_to_own(): tiles = lax.psum_scatter(tiles, axes[k], scatter_dimension=0, tiled=True)  13.9 us
    all_to_all x1, waiting for transfers between devices, local(): lax.all_to_all(serve_rows(received[1]), TABLE, split_axis=0, concat_axis=...  12.8 us
    all_to_all x1, starting transfers between devices, local(): lax.all_to_all(serve_rows(received[1]), TABLE, split_axis=0, concat_axis=...  11.1 us
  transfers between devices with their start and end apart: 11, of which 10 were waited for; matrix products, arithmetic and copies ran while one was open for 28% of the time, Pallas kernels for 0%

commit v1 on v0

v1 whole, which is shorter than its diff:
```python
import jax
import jax.numpy as jnp
from jax import lax
from jax.experimental import pallas as pl
from jax.experimental.pallas import tpu as pltpu
from jax.sharding import Mesh
from jax.sharding import PartitionSpec as P

SECTION = ("zl1", "zl0", "c")
TABLE = ("x1", "x0", "y1", "y0", "zh")
GRAD_GROUP = ("x1", "zl0", "c", "x0", "y0")
ROW_GROUP = ("x1", "zl0", "c", "x0")
RING = ("y1", "y0")
ROWS_DEV = 64
F32 = jnp.float32
BF16 = jnp.bfloat16
VMEM = pltpu.CompilerParams(vmem_limit_bytes=40 * 1024 * 1024)


def mixing_of(slots, weights, listed):
    matches = slots[:, :, None] == jnp.arange(listed, dtype=jnp.int32)[None, None, :]
    return jnp.sum(jnp.where(matches, weights[:, :, None], 0.0), axis=1).astype(BF16)


def gated(gate, incoming):
    g = gate.astype(F32)
    sig = 1.0 / (1.0 + jnp.exp(-g))
    return g, sig, incoming.astype(F32)


def outgoing_kernel(gate_ref, cot_ref, mix_ref, ids_ref, out_ref):
    g, sig, inc = gated(gate_ref[...], cot_ref[...])
    grad_memory = (inc * g * sig).astype(BF16)
    rows = lax.dot_general(
        mix_ref[...], grad_memory, (((0,), (0,)), ((), ())), preferred_element_type=F32
    ).astype(BF16)
    listed = rows.shape[0]
    for k in range(out_ref.shape[0]):
        out_ref[k, :listed, :] = rows[:, k * 128 : (k + 1) * 128]
        out_ref[k, listed:, :] = ids_ref[...]


def outgoing(gate, cot, mixing, id_rows, features):
    tokens, width = gate.shape
    listed = mixing.shape[1]
    chunks, step = width // features, 4
    return pl.pallas_call(
        outgoing_kernel,
        grid=(chunks // step,),
        in_specs=[
            pl.BlockSpec((tokens, step * features), lambda i: (0, i)),
            pl.BlockSpec((tokens, step * features), lambda i: (0, i)),
            pl.BlockSpec((tokens, listed), lambda i: (0, 0)),
            pl.BlockSpec((16, listed), lambda i: (0, 0)),
        ],
        out_specs=pl.BlockSpec((step, listed + 16, features), lambda i: (i, 0, 0)),
        out_shape=jax.ShapeDtypeStruct((chunks, listed + 16, features), BF16),
        compiler_params=VMEM,
        name="outgoing_rows",
    )(gate, cot, mixing, id_rows)


def dense_kernel(ids_ref, rows_ref, out_ref):
    tile, features = out_ref.shape
    lists, listed = ids_ref.shape
    row = (lax.broadcasted_iota(jnp.int32, (tile, listed), 0) + pl.program_id(0) * tile).astype(F32)
    total = jnp.zeros((tile, features), F32)
    together = 8
    for first in range(0, lists, together):
        hot = [
            jnp.where(row == ids_ref[pl.ds(k, 1), :], 1.0, 0.0).astype(BF16)
            for k in range(first, first + together)
        ]
        rows = [rows_ref[k, :listed, :] for k in range(first, first + together)]
        total += jnp.dot(
            jnp.concatenate(hot, axis=1), jnp.concatenate(rows, axis=0), preferred_element_type=F32
        )
    out_ref[...] = total.astype(BF16)


def dense_rows(ids, received, rows):
    lists, listed = ids.shape
    features = received.shape[-1]
    tile = 256
    return pl.pallas_call(
        dense_kernel,
        grid=(rows // tile,),
        in_specs=[
            pl.BlockSpec((lists, listed), lambda i: (0, 0)),
            pl.BlockSpec(received.shape, lambda i: (0, 0, 0)),
        ],
        out_specs=pl.BlockSpec((tile, features), lambda i: (i, 0)),
        out_shape=jax.ShapeDtypeStruct((rows, features), BF16),
        compiler_params=VMEM,
        name="dense_rows",
    )(ids, received)


def pick_kernel(ids_ref, place_ref, *refs):
    blocks, out_ref = refs[:-1], refs[-1]
    lists, listed = ids_ref.shape[1:]
    wanted = jnp.concatenate(
        [jnp.transpose(jnp.broadcast_to(ids_ref[0, k : k + 1, :], (128, listed))) for k in range(lists)],
        axis=0,
    )
    total = jnp.zeros(out_ref.shape[1:], F32)
    for b, block in enumerate(blocks):
        rows = block.shape[0]
        hot = [
            jnp.where(wanted == place_ref[b : b + 1, q : q + 128], 1.0, 0.0).astype(BF16)
            for q in range(0, rows, 128)
        ]
        total += jnp.dot(jnp.concatenate(hot, axis=1), block[...], preferred_element_type=F32)
    out_ref[0] = total.astype(BF16)


def picked_rows(ids, places, blocks):
    members, lists, listed = ids.shape
    rows, features = blocks[0].shape
    return pl.pallas_call(
        pick_kernel,
        grid=(members,),
        in_specs=[
            pl.BlockSpec((1, lists, listed), lambda i: (i, 0, 0)),
            pl.BlockSpec(places.shape, lambda i: (0, 0)),
        ]
        + [pl.BlockSpec((rows, features), lambda i: (0, 0))] * len(blocks),
        out_specs=pl.BlockSpec((1, lists * listed, features), lambda i: (i, 0, 0)),
        out_shape=jax.ShapeDtypeStruct((members, lists * listed, features), BF16),
        compiler_params=VMEM,
        name="picked_rows",
    )(ids, places, *blocks)


def final_kernel(
    rows_ref, mix_a_ref, mix_b_ref, gate_a_ref, cot_ref, gate_b_ref, slots_ref,
    mixed_ref, grad_gate_ref, grad_weights_ref, scores_ref,
):
    listed = mix_a_ref.shape[1]
    fetched_a = rows_ref[0, :listed, :]
    fetched_b = rows_ref[0, listed:, :]
    memory_b = jnp.dot(mix_b_ref[...], fetched_b, preferred_element_type=F32)
    gb = gate_b_ref[...].astype(F32)
    mixed_ref[...] = (gb / (1.0 + jnp.exp(-gb)) * memory_b).astype(BF16)
    memory_a = jnp.dot(mix_a_ref[...], fetched_a, preferred_element_type=F32)
    g, sig, inc = gated(gate_a_ref[...], cot_ref[...])
    grad_gate_ref[...] = (inc * memory_a * sig * (1.0 + g * (1.0 - sig))).astype(BF16)
    grad_memory = (inc * g * sig).astype(BF16)
    part = lax.dot_general(
        grad_memory, fetched_a, (((1,), (1,)), ((), ())), preferred_element_type=F32
    )

    @pl.when(pl.program_id(0) == 0)
    def _():
        scores_ref[...] = part

    @pl.when(pl.program_id(0) > 0)
    def _():
        scores_ref[...] += part

    @pl.when(pl.program_id(0) == pl.num_programs(0) - 1)
    def _():
        grad_weights_ref[...] = jnp.take_along_axis(scores_ref[...], slots_ref[...], axis=1)


def final_outputs(fetched, mix_a, mix_b, gate_a, cot, gate_b, slots_a):
    chunks, rows, features = fetched.shape
    tokens, width = gate_a.shape
    listed = mix_a.shape[1]
    whole = pl.BlockSpec((tokens, listed), lambda i: (0, 0))
    part = pl.BlockSpec((tokens, features), lambda i: (0, i))
    return pl.pallas_call(
        final_kernel,
        grid=(chunks,),
        in_specs=[
            pl.BlockSpec((1, rows, features), lambda i: (i, 0, 0)),
            whole, whole, part, part, part, whole,
        ],
        out_specs=[part, part, whole],
        out_shape=[
            jax.ShapeDtypeStruct((tokens, width), BF16),
            jax.ShapeDtypeStruct((tokens, width), BF16),
            jax.ShapeDtypeStruct((tokens, listed), F32),
        ],
        scratch_shapes=[pltpu.VMEM((tokens, listed), F32)],
        compiler_params=VMEM,
        name="final_outputs",
    )(fetched, mix_a, mix_b, gate_a, cot, gate_b, slots_a)


def table_blocks(table):
    rows_dev, width = table.shape
    x1, x0 = lax.axis_index("x1"), lax.axis_index("x0")
    at_x, at_y, at_z = x1 * 2 + x0, lax.axis_index(RING), lax.axis_index("zh")
    n_y = lax.axis_size(RING)
    cut = table.reshape(rows_dev, 2, 4, 2, -1)
    cut = lax.dynamic_index_in_dim(cut, lax.axis_index(("zl0", "c")), 2, keepdims=False)
    cut = jnp.transpose(cut.reshape(rows_dev, 4, -1), (1, 0, 2))
    both = jnp.stack([cut, lax.ppermute(cut, "zh", [(0, 1), (1, 0)])], 1)
    mine = []
    for k in range(4):
        part = lax.dynamic_index_in_dim(both, at_x ^ k, 0, keepdims=False)
        if k:
            part = lax.ppermute(part, ("x1", "x0"), [(i, i ^ k) for i in range(4)])
        mine.append(part)
    block = jnp.stack(mine).reshape(4 * 2 * rows_dev, -1)
    ahead = [(i, (i + 1) % n_y) for i in range(n_y)]
    back = [(i, (i - 1) % n_y) for i in range(n_y)]
    blocks, origin = [block], [at_y]
    forward = backward = block
    for step in range(1, n_y // 2 + 1):
        forward = lax.ppermute(forward, RING, ahead)
        blocks.append(forward)
        origin.append((at_y - step) % n_y)
        if step < n_y - step:
            backward = lax.ppermute(backward, RING, back)
            blocks.append(backward)
            origin.append((at_y + step) % n_y)
    xs = at_x ^ jnp.arange(4, dtype=jnp.int32)
    zs = at_z ^ jnp.arange(2, dtype=jnp.int32)
    holder = (xs[None, :, None] * n_y + jnp.stack(origin)[:, None, None]) * 2 + zs[None, None, :]
    places = holder[..., None] * rows_dev + jnp.arange(rows_dev, dtype=jnp.int32)
    return blocks, places.reshape(len(blocks), -1).astype(F32)


def local(gate_a, cotangent_a, gate_b, table, row_ids, slots, weights):
    rows_dev = table.shape[0]
    owners = lax.axis_size(TABLE)
    listed = row_ids.shape[-1]
    gate_a, cotangent_a, gate_b = gate_a[0], cotangent_a[0], gate_b[0]
    lists = row_ids[0, :, 0]

    mix_a = mixing_of(slots[0, 0], weights[0, 0], listed)
    id_rows = jnp.stack([lists[0] // 64, lists[0] % 64, lists[1] // 64, lists[1] % 64]).astype(BF16)
    id_rows = jnp.concatenate([id_rows, jnp.zeros((12, listed), BF16)])
    sent = outgoing(gate_a, cotangent_a, mix_a, id_rows, 128)
    received = lax.all_to_all(sent, GRAD_GROUP, split_axis=0, concat_axis=0, tiled=True)

    blocks, places = table_blocks(table)

    codes = received[:, listed : listed + 4, :].astype(F32)
    ids = codes[:, 0::2] * 64.0 + codes[:, 1::2]
    dense = dense_rows(ids[:, 0], received, owners * rows_dev)
    arrived = lax.all_to_all(
        dense.reshape(owners, rows_dev, -1), TABLE, split_axis=0, concat_axis=0, tiled=True
    )

    near = ids.reshape(-1, 2, 2, listed)
    near = lax.dynamic_index_in_dim(near, lax.axis_index("y0"), 1, keepdims=False)
    picked = picked_rows(near, places, blocks)
    fetched = lax.all_to_all(picked, ROW_GROUP, split_axis=0, concat_axis=0, tiled=True)

    features = arrived.shape[-1]
    summed = jnp.sum(arrived.reshape(2, 2, -1, 2, 2, rows_dev, features).astype(F32), axis=(2, 4))
    mine = lax.axis_index("zl1")
    kept = lax.dynamic_index_in_dim(summed, mine, 0, keepdims=False)
    given = lax.dynamic_index_in_dim(summed, 1 - mine, 0, keepdims=False)
    total = kept + lax.ppermute(given, "zl1", [(0, 1), (1, 0)])
    grad_table = jnp.transpose(total, (2, 0, 1, 3)).reshape(rows_dev, -1)

    mix_b = mixing_of(slots[0, 1], weights[0, 1], listed)
    mixed_b, grad_gate, grad_weights = final_outputs(
        fetched, mix_a, mix_b, gate_a, cotangent_a, gate_b, slots[0, 0]
    )
    return mixed_b[None], grad_gate[None], grad_weights[None], grad_table


def solution(mesh):
    finer = Mesh(
        mesh.devices.reshape(2, 2, 2, 2, 2, 4, 2, 2),
        ("zl1", "zl0", "c", "x1", "x0", "y1", "y0", "zh"),
    )
    return jax.shard_map(
        local,
        mesh=finer,
        in_specs=(
            P(SECTION, TABLE, None),
            P(SECTION, TABLE, None),
            P(SECTION, TABLE, None),
            P(TABLE, None),
            P(SECTION, None, TABLE, None),
            P(SECTION, None, TABLE, None),
            P(SECTION, None, TABLE, None),
        ),
        out_specs=(
            P(SECTION, TABLE, None),
            P(SECTION, TABLE, None),
            P(SECTION, TABLE, None),
            P(TABLE, SECTION),
        ),
        check_vma=False,
    )
```

time: 420 us -> 208 us (0.50); the launches traced: 414 us -> 207 us
  waiting for transfers between devices: 220 us -> 61.3 us
  local copies, waits for them, and re-layouts: 90.8 us -> 8.99 us
  Pallas kernels: 0 us -> 32.8 us
  blocking collectives: 0 us -> 27.6 us
  between operations: 14.4 us -> 1.1 us
  other arithmetic: 20.4 us -> 8.06 us
  matrix products: 8.24 us -> 0 us
  starting transfers between devices: 59.8 us -> 66.8 us
    all_to_all x9 -> x2, waiting for transfers between devices: 206 us -> 2.23 us  [the longest x1 2.23 us: local(): lax.all_to_all(picked, ROW_GROUP, split_axis=0, concat_axis=0, tiled=True)]
    gather x5 -> x0, local copies, waits for them, and re-layouts: 69.3 us -> none  [the longest x1 50.7 us: local(): grad_weights = jnp.take_along_axis(row_scores, slots[0, 0], axis=1)]
    ppermute x0 -> x12, waiting for transfers between devices: none -> 59.1 us  [the longest x1 26 us: table_blocks(): both = jnp.stack([cut, lax.ppermute(cut, 'zh', [(0, 1), (1, 0)])], 1)]
    ppermute x0 -> x12, starting transfers between devices: none -> 41.8 us  [the longest x3 11.8 us: table_blocks(): backward = lax.ppermute(backward, RING, back)]
    all_to_all x9 -> x2, starting transfers between devices: 59.8 us -> 25 us  [the longest x1 14.1 us: local(): lax.all_to_all(dense.reshape(owners, rows_dev, -1), TABLE, split_axis=0,...]
    pallas_call x0 -> x4, Pallas kernels: none -> 32.8 us  [the longest x1 12.1 us: picked_rows(): pl.pallas_call(pick_kernel, grid=(members,), in_specs=[pl.BlockSpec((1, l...]
    all_to_all x0 -> x1, blocking collectives: none -> 27.6 us  [local(): lax.all_to_all(sent, GRAD_GROUP, split_axis=0, concat_axis=0, tiled=True)]
    reduce_scatter x2 -> x0, waiting for transfers between devices: 13.9 us -> none  [reduced_to_own(): tiles = lax.psum_scatter(tiles, axes[k], scatter_dimension=0, tiled=True)]
  transfers between devices with their start and end apart: 11 -> 14, of which waited for: 10 -> 8; matrix products, arithmetic and copies ran while one was open for 28% -> 3% of each run, Pallas kernels for 0% -> 6%
where the time goes in v1:
time: 208 us; the launch traced here: 207 us
  starting transfers between devices  66.8 us (32%)
  waiting for transfers between devices  61.3 us (29%)
  Pallas kernels  32.8 us (16%)
  blocking collectives  27.6 us (13%)
  local copies, waits for them, and re-layouts  8.99 us (4%)
  other arithmetic  8.06 us (4%)
    all_to_all x1, blocking collectives, local(): lax.all_to_all(sent, GRAD_GROUP, split_axis=0, concat_axis=0, tiled=True)  27.6 us
    ppermute x1, waiting for transfers between devices, table_blocks(): both = jnp.stack([cut, lax.ppermute(cut, 'zh', [(0, 1), (1, 0)])], 1)  26 us
    ppermute x1, waiting for transfers between devices, local(): total = kept + lax.ppermute(given, 'zl1', [(0, 1), (1, 0)])  17.6 us
    all_to_all x1, starting transfers between devices, local(): lax.all_to_all(dense.reshape(owners, rows_dev, -1), TABLE, split_axis=0,...  14.1 us
    pallas_call x1, Pallas kernels, picked_rows(): pl.pallas_call(pick_kernel, grid=(members,), in_specs=[pl.BlockSpec((1, l...  12.1 us
    pallas_call x1, Pallas kernels, dense_rows(): pl.pallas_call(dense_kernel, grid=(rows // tile,), in_specs=[pl.BlockSpec...  11.9 us
    ppermute x3, starting transfers between devices, table_blocks(): backward = lax.ppermute(backward, RING, back)  11.8 us
    ppermute x4, waiting for transfers between devices, table_blocks(): forward = lax.ppermute(forward, RING, ahead)  11.2 us
  transfers between devices with their start and end apart: 14, of which 8 were waited for; matrix products, arithmetic and copies ran while one was open for 3% of the time, Pallas kernels for 6%

profile of v1, /device:TPU:1, one launch (start us, length us, event | category | flops | bytes accessed | tf_op | source)
XLA Modules:
  0.0 206.7 jit_solution(10383311078166543016)
XLA Ops:
  2.9 2.8 %select_reduce_fusion.1.mix_ref.mix_a_ref = bf16[64,128]{1,0:T(8,128)(2,1)S(1)} fusion(f32[64,128]{1,0:T(8,128)S(1)} %get-tuple-element.21, s32[64,128]{1,0:T(8,128)S(1)} %get-tuple-element.19.slots_ref), kind=kLoop, calls=%fused_computation.2 | loop fusion | flops 3137536 | bytes 81920 | tf_op jit(solution)/shard_map/reduce_sum | solution.py:22
  7.8 1.8 outgoing_rows.1
  9.6 27.6 %all_to_all.15.rows_ref = bf16[32,144,128]{2,1,0:T(8,128)(2,1)S(1)} all-to-all(bf16[32,144,128]{2,1,0:T(8,128)(2,1)S(1)} %outgoing_rows.1), channel_id=1, replica_groups=mesh['zl1'=2,'zl0'=2,'c'=2,'x1'=2,'x0'=2,'y1'=4,'y0'=2,'zh'=2] {'x1','zl..., dimensions={0} | all-to-all | bytes 2359296 | tf_op jit(solution)/shard_map/all_to_all | solution.py:237
  37.6 11.9 %dense_rows.1 = bf16[4096,128]{1,0:T(8,128)(2,1)} custom-call(f32[32,128]{1,0:T(8,128)S(1)} %bitcast.91, bf16[32,144,128]{2,1,0:T(8,128)(2,1)S(1)} %all_to_all.15.rows_ref), custom_call_target="tpu_custom_call" | custom-call | tf_op jit(solution)/shard_map/dense_rows/pallas_call | solution.py:85
  49.5 14.1 %all-to-all-start.2 = ((bf16[64,64,128]{2,1,0:T(8,128)(2,1)}), bf16[64,64,128]{2,1,0:T(8,128)(2,1)S(1)}, u32[]{:S(2)}, u32[]{:S(2)}) async-start(bf16[64,64,128]{2,1,0:T(8,128)(2,1)} %bitcast.36), calls=%async_computation.2 | async-start | bytes 2097152 | tf_op jit(solution)/shard_map/all_to_all | solution.py:244
  64.1 6.8 %collective-permute-start = (bf16[4,64,256]{2,1,0:T(8,128)(2,1)S(1)}, bf16[4,64,256]{2,1,0:T(8,128)(2,1)S(1)}, u32[]{:S(2)}, u32[]{:S(2)}) collective-permute-start(bf16[4,64,256]{2,1,0:T(8,128)(2,1)S(1)} %bitcast.93), channel_id=1, source_target_pairs={{0,1},{1,0},{2,3},{3,2},{4,5},{5,4},{6,7},{7,6},{8,9},{9,8},{10,11... | collective-permute-start | bytes 393224 | tf_op jit(solution)/shard_map/ppermute | solution.py:199
  71.0 26.0 %collective-permute-done = bf16[4,64,256]{2,1,0:T(8,128)(2,1)S(1)} collective-permute-done((bf16[4,64,256]{2,1,0:T(8,128)(2,1)S(1)}, bf16[4,64,256]{2,1,0:T(8,128)(2,1)S(1)}, u32[]{:S(2)}, u32[]{:S(2)}) %collective-permute-start) | collective-permute-done | bytes 131104 | tf_op jit(solution)/shard_map/ppermute | solution.py:199
  97.0 3.1 %collective-permute-start.1 = (bf16[2,64,256]{2,1,0:T(8,128)(2,1)S(1)}, bf16[2,64,256]{2,1,0:T(8,128)(2,1)S(1)}, u32[]{:S(2)}, u32[]{:S(2)}) collective-permute-start(bf16[2,64,256]{2,1,0:T(8,128)(2,1)S(1)} %get-tuple-element.15), channel_id=1, source_target_pairs={{0,16},{16,0},{32,48},{48,32},{1,17},{17,1},{33,49},{49,33},{2,18}... | collective-permute-start | bytes 196616 | tf_op jit(solution)/shard_map/ppermute | solution.py:204
  100.1 4.5 %collective-permute-start.2 = (bf16[2,64,256]{2,1,0:T(8,128)(2,1)S(1)}, bf16[2,64,256]{2,1,0:T(8,128)(2,1)S(1)}, u32[]{:S(2)}, u32[]{:S(2)}) collective-permute-start(bf16[2,64,256]{2,1,0:T(8,128)(2,1)S(1)} %get-tuple-element.16), channel_id=1, source_target_pairs={{0,32},{16,48},{32,0},{48,16},{1,33},{17,49},{33,1},{49,17},{2,34}... | collective-permute-start | bytes 196616 | tf_op jit(solution)/shard_map/ppermute | solution.py:204
  104.6 2.0 collective-permute-start.3
  106.7 4.2 %collective-permute-done.3 = bf16[2,64,256]{2,1,0:T(8,128)(2,1)S(1)} collective-permute-done((bf16[2,64,256]{2,1,0:T(8,128)(2,1)S(1)}, bf16[2,64,256]{2,1,0:T(8,128)(2,1)S(1)}, u32[]{:S(2)}, u32[]{:S(2)}) %collective-permute-start.3) | collective-permute-done | bytes 65568 | tf_op jit(solution)/shard_map/ppermute | solution.py:204
  110.9 3.5 %collective-permute-start.4 = (bf16[512,256]{1,0:T(8,128)(2,1)S(1)}, bf16[512,256]{1,0:T(8,128)(2,1)S(1)}, u32[]{:S(2)}, u32[]{:S(2)}) collective-permute-start(bf16[512,256]{1,0:T(8,128)(2,1)S(1)} %bitcast.87), channel_id=1, source_target_pairs={{0,2},{2,4},{4,6},{6,8},{8,10},{10,12},{12,14},{14,0},{1,3},{3,5},... | collective-permute-start | bytes 786440 | tf_op jit(solution)/shard_map/ppermute | solution.py:212
  114.4 3.0 %collective-permute-start.5 = (bf16[512,256]{1,0:T(8,128)(2,1)S(1)}, bf16[512,256]{1,0:T(8,128)(2,1)S(1)}, u32[]{:S(2)}, u32[]{:S(2)}) collective-permute-start(bf16[512,256]{1,0:T(8,128)(2,1)S(1)} %bitcast.88), channel_id=1, source_target_pairs={{0,14},{2,0},{4,2},{6,4},{8,6},{10,8},{12,10},{14,12},{1,15},{3,1}... | collective-permute-start | bytes 786440 | tf_op jit(solution)/shard_map/ppermute | solution.py:216
  117.4 1.8 collective-permute-done.4.refs_1_
  119.2 2.2 %collective-permute-start.6 = (bf16[512,256]{1,0:T(8,128)(2,1)S(1)}, bf16[512,256]{1,0:T(8,128)(2,1)S(1)}, u32[]{:S(2)}, u32[]{:S(2)}) collective-permute-start(bf16[512,256]{1,0:T(8,128)(2,1)S(1)} %collective-permute-done.4.refs_1_), channel_id=1, source_target_pairs={{0,2},{2,4},{4,6},{6,8},{8,10},{10,12},{12,14},{14,0},{1,3},{3,5},... | collective-permute-start | bytes 786440 | tf_op jit(solution)/shard_map/ppermute | solution.py:212
  121.8 4.2 %collective-permute-start.7 = (bf16[512,256]{1,0:T(8,128)(2,1)S(1)}, bf16[512,256]{1,0:T(8,128)(2,1)S(1)}, u32[]{:S(2)}, u32[]{:S(2)}) collective-permute-start(bf16[512,256]{1,0:T(8,128)(2,1)S(1)} %collective-permute-done.5.refs_2_), channel_id=1, source_target_pairs={{0,14},{2,0},{4,2},{6,4},{8,6},{10,8},{12,10},{14,12},{1,15},{3,1}... | collective-permute-start | bytes 786440 | tf_op jit(solution)/shard_map/ppermute | solution.py:216
  126.0 1.6 collective-permute-done.6.refs_3_
  127.5 1.9 collective-permute-start.8
  129.8 4.6 %collective-permute-start.9 = (bf16[512,256]{1,0:T(8,128)(2,1)S(1)}, bf16[512,256]{1,0:T(8,128)(2,1)S(1)}, u32[]{:S(2)}, u32[]{:S(2)}) collective-permute-start(bf16[512,256]{1,0:T(8,128)(2,1)S(1)} %collective-permute-done.7.refs_4_), channel_id=1, source_target_pairs={{0,14},{2,0},{4,2},{6,4},{8,6},{10,8},{12,10},{14,12},{1,15},{3,1}... | collective-permute-start | bytes 786440 | tf_op jit(solution)/shard_map/ppermute | solution.py:216
  134.4 1.4 collective-permute-done.8.refs_5_
  135.8 1.9 collective-permute-start.10
  137.8 6.4 %collective-permute-done.10.refs_7_ = bf16[512,256]{1,0:T(8,128)(2,1)S(1)} collective-permute-done((bf16[512,256]{1,0:T(8,128)(2,1)S(1)}, bf16[512,256]{1,0:T(8,128)(2,1)S(1)}, u32[]{:S(2)}, u32[]{:S(2)}) %collective-permute-start.10) | collective-permute-done | bytes 262176 | tf_op jit(solution)/shard_map/ppermute | solution.py:212
  144.2 12.1 %picked_rows.1 = bf16[16,256,256]{2,1,0:T(8,128)(2,1)S(1)} custom-call(f32[16,2,128]{2,1,0:T(2,128)S(1)} %dynamic-slice_bitcast_fusion.1.ids_ref, f32[8,512]{1,0:T(8,128)S(1)} %add_convert_fusion.place_ref, bf16[512,256]{1,0:T(8,128)(2,1)S(1)} %bitcast.89, bf16[512,256]{1,0:T(8,128)(2,1)S(1)} %collective-permute-done.4.refs_1_, ...), custom_call_target="tpu_custom_call" | custom-call | tf_op jit(solution)/shard_map/picked_rows/pallas_call | solution.py:120
  156.3 1.3 copy-done
  158.6 10.9 %all-to-all-start.1 = ((bf16[16,256,256]{2,1,0:T(8,128)(2,1)}), bf16[16,256,256]{2,1,0:T(8,128)(2,1)S(1)}, u32[]{:S(2)}, u32[]{:S(2)}) async-start(bf16[16,256,256]{2,1,0:T(8,128)(2,1)} %copy-done), calls=%async_computation.1 | async-start | bytes 4194304 | tf_op jit(solution)/shard_map/all_to_all | solution.py:251
  169.5 1.5 convert_reduce_fusion
  171.0 4.1 %collective-permute-start.11 = (f32[2,2,64,128]{3,2,1,0:T(8,128)S(1)}, f32[2,2,64,128]{3,2,1,0:T(8,128)S(1)}, u32[]{:S(2)}, u32[]{:S(2)}) collective-permute-start(f32[2,2,64,128]{3,2,1,0:T(8,128)S(1)} %dynamic-slice_bitcast_fusion), channel_id=1, source_target_pairs={{0,256},{256,0},{1,257},{257,1},{2,258},{258,2},{3,259},{259,3},{4... | collective-permute-start | bytes 393224 | tf_op jit(solution)/shard_map/ppermute | solution.py:258
  175.1 2.8 %select_reduce_fusion.mix_b_ref = bf16[64,128]{1,0:T(8,128)(2,1)S(1)} fusion(f32[64,128]{1,0:T(8,128)S(1)} %get-tuple-element.20, s32[64,128]{1,0:T(8,128)S(1)} %get-tuple-element.18), kind=kLoop, calls=%fused_computation | loop fusion | flops 3137536 | bytes 81920 | tf_op jit(solution)/shard_map/reduce_sum | solution.py:22
  177.9 17.6 %collective-permute-done.11 = f32[2,2,64,128]{3,2,1,0:T(8,128)S(1)} collective-permute-done((f32[2,2,64,128]{3,2,1,0:T(8,128)S(1)}, f32[2,2,64,128]{3,2,1,0:T(8,128)S(1)}, u32[]{:S(2)}, u32[]{:S(2)}) %collective-permute-start.11) | collective-permute-done | bytes 131104 | tf_op jit(solution)/shard_map/ppermute | solution.py:258
  196.4 2.2 %all-to-all-done.1.rows_ref = bf16[16,256,256]{2,1,0:T(8,128)(2,1)S(1)} async-done(((bf16[16,256,256]{2,1,0:T(8,128)(2,1)}), bf16[16,256,256]{2,1,0:T(8,128)(2,1)S(1)}, u32[]{:S(2)}, u32[]{:S(2)}) %all-to-all-start.1) | async-done | bytes 2097184 | tf_op jit(solution)/shard_map/all_to_all | solution.py:251
  198.6 1.0 copy-done.5
  199.7 7.0 %final_outputs.1 = (bf16[64,4096]{1,0:T(8,128)(2,1)}, bf16[64,4096]{1,0:T(8,128)(2,1)}, f32[64,128]{1,0:T(8,128)}) custom-call(bf16[16,256,256]{2,1,0:T(8,128)(2,1)S(1)} %all-to-all-done.1.rows_ref, bf16[64,128]{1,0:T(8,128)(2,1)S(1)} %select_reduce_fusion.1.mix_ref.mix_a_ref, bf16[64,128]{1,0:T(8,128)(2,1)S(1)} %select_reduce_fusion.mix_b_ref, ...), custom_call_target="tpu_custom_call" | custom-call | tf_op jit(solution)/shard_map/final_outputs/pallas_call | solution.py:172
  (50 shorter events, 7.7 us)
Async XLA Ops:
  5.7 1.0 copy-start.1
  6.7 1.0 copy-start.3
  37.6 26.0 %copy-start.7 = (bf16[64,4096]{1,0:T(8,128)(2,1)S(1)}, bf16[64,4096]{1,0:T(8,128)(2,1)}, u32[]{:S(2)}) copy-start(bf16[64,4096]{1,0:T(8,128)(2,1)} %param.10) | copy-start | bytes 1572868
  49.5 108.2 %all-to-all-start.2 = ((bf16[64,64,128]{2,1,0:T(8,128)(2,1)}), bf16[64,64,128]{2,1,0:T(8,128)(2,1)S(1)}, u32[]{:S(2)}, u32[]{:S(2)}) async-start(bf16[64,64,128]{2,1,0:T(8,128)(2,1)} %bitcast.36), calls=%async_computation.2 | async-start | bytes 2097152 | tf_op jit(solution)/shard_map/all_to_all | solution.py:244
  64.1 32.9 %collective-permute-start = (bf16[4,64,256]{2,1,0:T(8,128)(2,1)S(1)}, bf16[4,64,256]{2,1,0:T(8,128)(2,1)S(1)}, u32[]{:S(2)}, u32[]{:S(2)}) collective-permute-start(bf16[4,64,256]{2,1,0:T(8,128)(2,1)S(1)} %bitcast.93), channel_id=1, source_target_pairs={{0,1},{1,0},{2,3},{3,2},{4,5},{5,4},{6,7},{7,6},{8,9},{9,8},{10,11... | collective-permute-start | bytes 393224 | tf_op jit(solution)/shard_map/ppermute | solution.py:199
  97.0 9.6 %collective-permute-start.1 = (bf16[2,64,256]{2,1,0:T(8,128)(2,1)S(1)}, bf16[2,64,256]{2,1,0:T(8,128)(2,1)S(1)}, u32[]{:S(2)}, u32[]{:S(2)}) collective-permute-start(bf16[2,64,256]{2,1,0:T(8,128)(2,1)S(1)} %get-tuple-element.15), channel_id=1, source_target_pairs={{0,16},{16,0},{32,48},{48,32},{1,17},{17,1},{33,49},{49,33},{2,18}... | collective-permute-start | bytes 196616 | tf_op jit(solution)/shard_map/ppermute | solution.py:204
  100.1 6.6 %collective-permute-start.2 = (bf16[2,64,256]{2,1,0:T(8,128)(2,1)S(1)}, bf16[2,64,256]{2,1,0:T(8,128)(2,1)S(1)}, u32[]{:S(2)}, u32[]{:S(2)}) collective-permute-start(bf16[2,64,256]{2,1,0:T(8,128)(2,1)S(1)} %get-tuple-element.16), channel_id=1, source_target_pairs={{0,32},{16,48},{32,0},{48,16},{1,33},{17,49},{33,1},{49,17},{2,34}... | collective-permute-start | bytes 196616 | tf_op jit(solution)/shard_map/ppermute | solution.py:204
  104.6 6.2 %collective-permute-start.3 = (bf16[2,64,256]{2,1,0:T(8,128)(2,1)S(1)}, bf16[2,64,256]{2,1,0:T(8,128)(2,1)S(1)}, u32[]{:S(2)}, u32[]{:S(2)}) collective-permute-start(bf16[2,64,256]{2,1,0:T(8,128)(2,1)S(1)} %get-tuple-element.17), channel_id=1, source_target_pairs={{0,48},{16,32},{32,16},{48,0},{1,49},{17,33},{33,17},{49,1},{2,50}... | collective-permute-start | bytes 196616 | tf_op jit(solution)/shard_map/ppermute | solution.py:204
  110.9 8.3 %collective-permute-start.4 = (bf16[512,256]{1,0:T(8,128)(2,1)S(1)}, bf16[512,256]{1,0:T(8,128)(2,1)S(1)}, u32[]{:S(2)}, u32[]{:S(2)}) collective-permute-start(bf16[512,256]{1,0:T(8,128)(2,1)S(1)} %bitcast.87), channel_id=1, source_target_pairs={{0,2},{2,4},{4,6},{6,8},{8,10},{10,12},{12,14},{14,0},{1,3},{3,5},... | collective-permute-start | bytes 786440 | tf_op jit(solution)/shard_map/ppermute | solution.py:212
  114.4 7.4 %collective-permute-start.5 = (bf16[512,256]{1,0:T(8,128)(2,1)S(1)}, bf16[512,256]{1,0:T(8,128)(2,1)S(1)}, u32[]{:S(2)}, u32[]{:S(2)}) collective-permute-start(bf16[512,256]{1,0:T(8,128)(2,1)S(1)} %bitcast.88), channel_id=1, source_target_pairs={{0,14},{2,0},{4,2},{6,4},{8,6},{10,8},{12,10},{14,12},{1,15},{3,1}... | collective-permute-start | bytes 786440 | tf_op jit(solution)/shard_map/ppermute | solution.py:216
  119.2 8.3 %collective-permute-start.6 = (bf16[512,256]{1,0:T(8,128)(2,1)S(1)}, bf16[512,256]{1,0:T(8,128)(2,1)S(1)}, u32[]{:S(2)}, u32[]{:S(2)}) collective-permute-start(bf16[512,256]{1,0:T(8,128)(2,1)S(1)} %collective-permute-done.4.refs_1_), channel_id=1, source_target_pairs={{0,2},{2,4},{4,6},{6,8},{8,10},{10,12},{12,14},{14,0},{1,3},{3,5},... | collective-permute-start | bytes 786440 | tf_op jit(solution)/shard_map/ppermute | solution.py:212
  121.8 8.1 %collective-permute-start.7 = (bf16[512,256]{1,0:T(8,128)(2,1)S(1)}, bf16[512,256]{1,0:T(8,128)(2,1)S(1)}, u32[]{:S(2)}, u32[]{:S(2)}) collective-permute-start(bf16[512,256]{1,0:T(8,128)(2,1)S(1)} %collective-permute-done.5.refs_2_), channel_id=1, source_target_pairs={{0,14},{2,0},{4,2},{6,4},{8,6},{10,8},{12,10},{14,12},{1,15},{3,1}... | collective-permute-start | bytes 786440 | tf_op jit(solution)/shard_map/ppermute | solution.py:216
  127.5 8.3 %collective-permute-start.8 = (bf16[512,256]{1,0:T(8,128)(2,1)S(1)}, bf16[512,256]{1,0:T(8,128)(2,1)S(1)}, u32[]{:S(2)}, u32[]{:S(2)}) collective-permute-start(bf16[512,256]{1,0:T(8,128)(2,1)S(1)} %collective-permute-done.6.refs_3_), channel_id=1, source_target_pairs={{0,2},{2,4},{4,6},{6,8},{8,10},{10,12},{12,14},{14,0},{1,3},{3,5},... | collective-permute-start | bytes 786440 | tf_op jit(solution)/shard_map/ppermute | solution.py:212
  129.8 8.0 %collective-permute-start.9 = (bf16[512,256]{1,0:T(8,128)(2,1)S(1)}, bf16[512,256]{1,0:T(8,128)(2,1)S(1)}, u32[]{:S(2)}, u32[]{:S(2)}) collective-permute-start(bf16[512,256]{1,0:T(8,128)(2,1)S(1)} %collective-permute-done.7.refs_4_), channel_id=1, source_target_pairs={{0,14},{2,0},{4,2},{6,4},{8,6},{10,8},{12,10},{14,12},{1,15},{3,1}... | collective-permute-start | bytes 786440 | tf_op jit(solution)/shard_map/ppermute | solution.py:216
  135.8 8.4 %collective-permute-start.10 = (bf16[512,256]{1,0:T(8,128)(2,1)S(1)}, bf16[512,256]{1,0:T(8,128)(2,1)S(1)}, u32[]{:S(2)}, u32[]{:S(2)}) collective-permute-start(bf16[512,256]{1,0:T(8,128)(2,1)S(1)} %collective-permute-done.8.refs_5_), channel_id=1, source_target_pairs={{0,2},{2,4},{4,6},{6,8},{8,10},{10,12},{12,14},{14,0},{1,3},{3,5},... | collective-permute-start | bytes 786440 | tf_op jit(solution)/shard_map/ppermute | solution.py:212
  156.3 1.3 copy-start
  157.6 1.0 copy-start.6
  158.6 40.0 %all-to-all-start.1 = ((bf16[16,256,256]{2,1,0:T(8,128)(2,1)}), bf16[16,256,256]{2,1,0:T(8,128)(2,1)S(1)}, u32[]{:S(2)}, u32[]{:S(2)}) async-start(bf16[16,256,256]{2,1,0:T(8,128)(2,1)} %copy-done), calls=%async_computation.1 | async-start | bytes 4194304 | tf_op jit(solution)/shard_map/all_to_all | solution.py:251
  169.5 29.2 %copy-start.2 = (bf16[1,64,4096]{2,1,0:T(8,128)(2,1)S(1)}, bf16[1,64,4096]{2,1,0:T(8,128)(2,1)}, u32[]{:S(2)}) copy-start(bf16[1,64,4096]{2,1,0:T(8,128)(2,1)} %param.7) | copy-start | bytes 1572868
  169.5 29.2 %copy-start.4 = (bf16[1,64,4096]{2,1,0:T(8,128)(2,1)S(1)}, bf16[1,64,4096]{2,1,0:T(8,128)(2,1)}, u32[]{:S(2)}) copy-start(bf16[1,64,4096]{2,1,0:T(8,128)(2,1)} %param.8) | copy-start | bytes 1572868
  171.0 24.5 %collective-permute-start.11 = (f32[2,2,64,128]{3,2,1,0:T(8,128)S(1)}, f32[2,2,64,128]{3,2,1,0:T(8,128)S(1)}, u32[]{:S(2)}, u32[]{:S(2)}) collective-permute-start(f32[2,2,64,128]{3,2,1,0:T(8,128)S(1)} %dynamic-slice_bitcast_fusion), channel_id=1, source_target_pairs={{0,256},{256,0},{1,257},{257,1},{2,258},{258,2},{3,259},{259,3},{4... | collective-permute-start | bytes 393224 | tf_op jit(solution)/shard_map/ppermute | solution.py:258
  198.6 1.0 copy-start.5

commit v2 on v1

v2 whole, which is shorter than its diff:
```python
import jax
import jax.numpy as jnp
from jax import lax
from jax.experimental import pallas as pl
from jax.experimental.pallas import tpu as pltpu
from jax.sharding import Mesh
from jax.sharding import PartitionSpec as P

SECTION = ("zl1", "zl0", "c")
TABLE = ("x1", "x0", "y1", "y0", "zh")
GRAD_GROUP = ("x1", "zl0", "c", "x0", "y0")
ROW_GROUP = ("x1", "zl0", "c", "x0")
RING = ("y1", "y0")
ROWS_DEV = 64
F32 = jnp.float32
BF16 = jnp.bfloat16
VMEM = pltpu.CompilerParams(vmem_limit_bytes=40 * 1024 * 1024)


def gated(gate, incoming):
    g = gate.astype(F32)
    sig = 1.0 / (1.0 + jnp.exp(-g))
    return g, sig, incoming.astype(F32)


def mixing_of(slots, weights):
    position = lax.broadcasted_iota(jnp.int32, slots.shape, 1)
    total = jnp.zeros(slots.shape, F32)
    for p in range(slots.shape[1]):
        total += jnp.where(slots[:, p : p + 1] == position, weights[:, p : p + 1], 0.0)
    return total.astype(BF16)


def outgoing_kernel(gate_ref, cot_ref, slots_ref, weights_ref, ids_ref, out_ref, mix_ref):
    listed = mix_ref.shape[1]

    @pl.when(pl.program_id(0) == 0)
    def _():
        mix_ref[...] = mixing_of(slots_ref[0, 0], weights_ref[0, 0])

    g, sig, inc = gated(gate_ref[0], cot_ref[0])
    grad_memory = (inc * g * sig).astype(BF16)
    rows = lax.dot_general(
        mix_ref[...], grad_memory, (((0,), (0,)), ((), ())), preferred_element_type=F32
    ).astype(BF16)
    ids = [ids_ref[0, c] for c in range(2)]
    codes = jnp.concatenate(
        [part for i in ids for part in (i // ROWS_DEV, i % ROWS_DEV)] + [jnp.zeros((12, listed), jnp.int32)]
    )
    codes = codes.astype(F32).astype(BF16)
    for k in range(out_ref.shape[0]):
        out_ref[k, :listed, :] = rows[:, k * 128 : (k + 1) * 128]
        out_ref[k, listed:, :] = codes


def outgoing(gate, cot, slots, weights, row_ids, features):
    _, tokens, width = gate.shape
    listed = row_ids.shape[-1]
    chunks, step = width // features, 8
    part = pl.BlockSpec((1, tokens, step * features), lambda i: (0, 0, i))
    picks = pl.BlockSpec((1, 1, tokens, listed), lambda i: (0, 0, 0, 0))
    return pl.pallas_call(
        outgoing_kernel,
        grid=(chunks // step,),
        in_specs=[part, part, picks, picks, pl.BlockSpec(row_ids.shape, lambda i: (0, 0, 0, 0))],
        out_specs=[
            pl.BlockSpec((step, listed + 16, features), lambda i: (i, 0, 0)),
            pl.BlockSpec((tokens, listed), lambda i: (0, 0)),
        ],
        out_shape=[
            jax.ShapeDtypeStruct((chunks, listed + 16, features), BF16),
            jax.ShapeDtypeStruct((tokens, listed), BF16),
        ],
        compiler_params=VMEM,
        name="outgoing_rows",
    )(gate, cot, slots, weights, row_ids)


def mixing_kernel(slots_ref, weights_ref, out_ref):
    out_ref[...] = mixing_of(slots_ref[0, 0], weights_ref[0, 0])


def mixing_b(slots, weights):
    tokens, listed = slots.shape[2:]
    picks = pl.BlockSpec((1, 1, tokens, listed), lambda i: (0, 1, 0, 0))
    return pl.pallas_call(
        mixing_kernel,
        grid=(1,),
        in_specs=[picks, picks],
        out_specs=pl.BlockSpec((tokens, listed), lambda i: (0, 0)),
        out_shape=jax.ShapeDtypeStruct((tokens, listed), BF16),
        compiler_params=VMEM,
        name="mixing_b",
    )(slots, weights)


def dense_kernel(ids_ref, rows_ref, out_ref):
    tile, features = out_ref.shape
    lists, listed = ids_ref.shape
    row = (lax.broadcasted_iota(jnp.int32, (tile, listed), 0) + pl.program_id(0) * tile).astype(F32)
    total = jnp.zeros((tile, features), F32)
    together = 8
    for first in range(0, lists, together):
        hot = [
            jnp.where(row == ids_ref[pl.ds(k, 1), :], 1.0, 0.0).astype(BF16)
            for k in range(first, first + together)
        ]
        rows = [rows_ref[k, :listed, :] for k in range(first, first + together)]
        total += jnp.dot(
            jnp.concatenate(hot, axis=1), jnp.concatenate(rows, axis=0), preferred_element_type=F32
        )
    out_ref[...] = total.astype(BF16)


def dense_rows(ids, received, rows):
    lists, listed = ids.shape
    features = received.shape[-1]
    tile = 256
    return pl.pallas_call(
        dense_kernel,
        grid=(rows // tile,),
        in_specs=[
            pl.BlockSpec((lists, listed), lambda i: (0, 0)),
            pl.BlockSpec(received.shape, lambda i: (0, 0, 0)),
        ],
        out_specs=pl.BlockSpec((tile, features), lambda i: (i, 0)),
        out_shape=jax.ShapeDtypeStruct((rows, features), BF16),
        compiler_params=VMEM,
        name="dense_rows",
    )(ids, received)


def pick_kernel(ids_ref, place_ref, *refs):
    blocks, out_ref = refs[:-1], refs[-1]
    lists, listed = ids_ref.shape[1:]
    wanted = jnp.concatenate(
        [jnp.transpose(jnp.broadcast_to(ids_ref[0, k : k + 1, :], (128, listed))) for k in range(lists)],
        axis=0,
    )
    total = jnp.zeros(out_ref.shape[1:], F32)
    for b, block in enumerate(blocks):
        rows = block.shape[0]
        hot = [
            jnp.where(wanted == place_ref[b : b + 1, q : q + 128], 1.0, 0.0).astype(BF16)
            for q in range(0, rows, 128)
        ]
        total += jnp.dot(jnp.concatenate(hot, axis=1), block[...], preferred_element_type=F32)
    out_ref[0] = total.astype(BF16)


def picked_rows(ids, places, blocks):
    members, lists, listed = ids.shape
    rows, features = blocks[0].shape
    return pl.pallas_call(
        pick_kernel,
        grid=(members,),
        in_specs=[
            pl.BlockSpec((1, lists, listed), lambda i: (i, 0, 0)),
            pl.BlockSpec(places.shape, lambda i: (0, 0)),
        ]
        + [pl.BlockSpec((rows, features), lambda i: (0, 0))] * len(blocks),
        out_specs=pl.BlockSpec((1, lists * listed, features), lambda i: (i, 0, 0)),
        out_shape=jax.ShapeDtypeStruct((members, lists * listed, features), BF16),
        compiler_params=VMEM,
        name="picked_rows",
    )(ids, places, *blocks)


def final_kernel(
    rows_ref, mix_a_ref, mix_b_ref, gate_a_ref, cot_ref, gate_b_ref, slots_ref,
    mixed_ref, grad_gate_ref, grad_weights_ref, scores_ref,
):
    listed = mix_a_ref.shape[1]
    step, _, features = rows_ref.shape

    @pl.when(pl.program_id(0) == 0)
    def _():
        scores_ref[...] = jnp.zeros_like(scores_ref)

    part = jnp.zeros(scores_ref.shape, F32)
    for k in range(step):
        at = slice(k * features, (k + 1) * features)
        fetched_a = rows_ref[k, :listed, :]
        fetched_b = rows_ref[k, listed:, :]
        memory_b = jnp.dot(mix_b_ref[...], fetched_b, preferred_element_type=F32)
        gb = gate_b_ref[0, :, at].astype(F32)
        mixed_ref[0, :, at] = (gb / (1.0 + jnp.exp(-gb)) * memory_b).astype(BF16)
        memory_a = jnp.dot(mix_a_ref[...], fetched_a, preferred_element_type=F32)
        g, sig, inc = gated(gate_a_ref[0, :, at], cot_ref[0, :, at])
        grad_gate_ref[0, :, at] = (inc * memory_a * sig * (1.0 + g * (1.0 - sig))).astype(BF16)
        grad_memory = (inc * g * sig).astype(BF16)
        part += lax.dot_general(
            grad_memory, fetched_a, (((1,), (1,)), ((), ())), preferred_element_type=F32
        )
    scores_ref[...] += part

    @pl.when(pl.program_id(0) == pl.num_programs(0) - 1)
    def _():
        grad_weights_ref[0] = jnp.take_along_axis(scores_ref[...], slots_ref[0, 0], axis=1)


def final_outputs(fetched, mix_a, mix_b, gate_a, cot, gate_b, slots):
    chunks, rows, features = fetched.shape
    _, tokens, width = gate_a.shape
    listed = mix_a.shape[1]
    step = 4
    whole = pl.BlockSpec((tokens, listed), lambda i: (0, 0))
    part = pl.BlockSpec((1, tokens, step * features), lambda i: (0, 0, i))
    return pl.pallas_call(
        final_kernel,
        grid=(chunks // step,),
        in_specs=[
            pl.BlockSpec((step, rows, features), lambda i: (i, 0, 0)),
            whole, whole, part, part, part,
            pl.BlockSpec((1, 1, tokens, listed), lambda i: (0, 0, 0, 0)),
        ],
        out_specs=[part, part, pl.BlockSpec((1, tokens, listed), lambda i: (0, 0, 0))],
        out_shape=[
            jax.ShapeDtypeStruct((1, tokens, width), BF16),
            jax.ShapeDtypeStruct((1, tokens, width), BF16),
            jax.ShapeDtypeStruct((1, tokens, listed), F32),
        ],
        scratch_shapes=[pltpu.VMEM((tokens, listed), F32)],
        compiler_params=VMEM,
        name="final_outputs",
    )(fetched, mix_a, mix_b, gate_a, cot, gate_b, slots)


def both_halves(table):
    rows_dev, width = table.shape
    cut = table.reshape(rows_dev, 2, 4, 2, -1)
    cut = lax.dynamic_index_in_dim(cut, lax.axis_index(("zl0", "c")), 2, keepdims=False)
    cut = jnp.transpose(cut.reshape(rows_dev, 4, -1), (1, 0, 2))
    return cut, lax.ppermute(cut, "zh", [(0, 1), (1, 0)])


def across_x(own, other):
    at_x = lax.axis_index(("x1", "x0"))
    mine = []
    for k in range(4):
        part = jnp.concatenate(
            [lax.dynamic_index_in_dim(h, at_x ^ k, 0, keepdims=False) for h in (own, other)]
        )
        if k:
            part = lax.ppermute(part, ("x1", "x0"), [(i, i ^ k) for i in range(4)])
        mine.append(part)
    return jnp.concatenate(mine)


def ring_step(forward, backward):
    n_y = lax.axis_size(RING)
    ahead = [(i, (i + 1) % n_y) for i in range(n_y)]
    back = [(i, (i - 1) % n_y) for i in range(n_y)]
    return (
        lax.ppermute(forward, RING, ahead),
        None if backward is None else lax.ppermute(backward, RING, back),
    )


def block_places(rows_dev, offsets):
    n_y = lax.axis_size(RING)
    xs = lax.axis_index(("x1", "x0")) ^ jnp.arange(4, dtype=jnp.int32)
    zs = lax.axis_index("zh") ^ jnp.arange(2, dtype=jnp.int32)
    ys = (lax.axis_index(RING) + jnp.array(offsets, jnp.int32)) & (n_y - 1)
    holder = (xs[None, :, None] * n_y + ys[:, None, None]) * 2 + zs[None, None, :]
    places = holder[..., None] * rows_dev + jnp.arange(rows_dev, dtype=jnp.int32)
    return places.reshape(len(offsets), -1).astype(F32)


def local(gate_a, cotangent_a, gate_b, table, row_ids, slots, weights):
    rows_dev = table.shape[0]
    owners = lax.axis_size(TABLE)
    listed = row_ids.shape[-1]

    own, other = both_halves(table)
    sent, mix_a = outgoing(gate_a, cotangent_a, slots, weights, row_ids, 128)
    sent, own, other = lax.optimization_barrier((sent, own, other))
    received = lax.all_to_all(sent, GRAD_GROUP, split_axis=0, concat_axis=0, tiled=True)
    block = across_x(own, other)
    received, block = lax.optimization_barrier((received, block))

    codes = received[:, listed : listed + 4, :].astype(F32)
    ids = codes[:, 0::2] * ROWS_DEV + codes[:, 1::2]
    dense = dense_rows(ids[:, 0], received, owners * rows_dev)
    f1, b1 = ring_step(block, block)
    dense, f1, b1 = lax.optimization_barrier((dense, f1, b1))
    arrived = lax.all_to_all(
        dense.reshape(owners, rows_dev, -1), TABLE, split_axis=0, concat_axis=0, tiled=True
    )
    f2, b2 = ring_step(f1, b1)
    f3, b3 = ring_step(f2, b2)
    f4, _ = ring_step(f3, None)

    near = ids.reshape(-1, 2, 2, listed)
    near = lax.dynamic_index_in_dim(near, lax.axis_index("y0"), 1, keepdims=False)
    places = block_places(rows_dev, (0, -1, 1, -2, 2, -3, 3, -4))
    picked = picked_rows(near, places, (block, f1, b1, f2, b2, f3, b3, f4))
    fetched = lax.all_to_all(picked, ROW_GROUP, split_axis=0, concat_axis=0, tiled=True)

    features = arrived.shape[-1]
    summed = jnp.sum(arrived.reshape(2, 2, -1, 2, 2, rows_dev, features).astype(F32), axis=(2, 4))
    mine = lax.axis_index("zl1")
    kept = lax.dynamic_index_in_dim(summed, mine, 0, keepdims=False)
    given = lax.dynamic_index_in_dim(summed, 1 - mine, 0, keepdims=False)
    total = kept + lax.ppermute(given, "zl1", [(0, 1), (1, 0)])
    grad_table = jnp.transpose(total, (2, 0, 1, 3)).reshape(rows_dev, -1)

    mix_b = mixing_b(slots, weights)
    mixed, grad_gate, grad_weights = final_outputs(
        fetched, mix_a, mix_b, gate_a, cotangent_a, gate_b, slots
    )
    return mixed, grad_gate, grad_weights, grad_table


def solution(mesh):
    finer = Mesh(
        mesh.devices.reshape(2, 2, 2, 2, 2, 4, 2, 2),
        ("zl1", "zl0", "c", "x1", "x0", "y1", "y0", "zh"),
    )
    return jax.shard_map(
        local,
        mesh=finer,
        in_specs=(
            P(SECTION, TABLE, None),
            P(SECTION, TABLE, None),
            P(SECTION, TABLE, None),
            P(TABLE, None),
            P(SECTION, None, TABLE, None),
            P(SECTION, None, TABLE, None),
            P(SECTION, None, TABLE, None),
        ),
        out_specs=(
            P(SECTION, TABLE, None),
            P(SECTION, TABLE, None),
            P(SECTION, TABLE, None),
            P(TABLE, SECTION),
        ),
        check_vma=False,
    )
```

time: 208 us -> 184 us (0.88)
  blocking collectives: 27.6 us -> 0 us
  other arithmetic: 8.06 us -> 2.65 us
  starting transfers between devices: 66.8 us -> 72 us
  local copies, waits for them, and re-layouts: 8.99 us -> 12.2 us
    all_to_all x1 -> x0, blocking collectives: 27.6 us -> none  [local(): lax.all_to_all(sent, GRAD_GROUP, split_axis=0, concat_axis=0, tiled=True)]
    all_to_all x0 -> x1, starting transfers between devices: none -> 7.33 us  [local(): lax.all_to_all(sent, GRAD_GROUP, split_axis=0, concat_axis=0, tiled=True)]
    reduce_sum x2 -> x0, other arithmetic: 5.58 us -> none  [mixing_of(): jnp.sum(jnp.where(matches, weights[:, :, None], 0.0), axis=1).astype(BF16)]
    ppermute x11, starting transfers between devices: 37.7 us -> 42.1 us  [the longest x3 11.9 us: ring_step(): lax.ppermute(backward, RING, back)]
    all_to_all x1, starting transfers between devices: 14.1 us -> 10.1 us  [local(): lax.all_to_all(dense.reshape(owners, rows_dev, -1), TABLE, split_axis=0,...]
    unnamed x16 -> x32, local copies, waits for them, and re-layouts: 5.44 us -> 8.57 us
    pallas_call x2 -> x3, Pallas kernels: 8.82 us -> 9.74 us  [the longest x1 4.76 us: outgoing(): pl.pallas_call(outgoing_kernel, grid=(chunks // step,), in_specs=[part, p...]
  transfers between devices with their start and end apart: 14 -> 15, of which waited for: 8 -> 7; matrix products, arithmetic and copies ran while one was open for 3% -> 3% of each run, Pallas kernels for 6% -> 17%
where the time goes in v2:
time: 184 us; the launch traced here: 183 us
  starting transfers between devices  72 us (39%)
  waiting for transfers between devices  61.1 us (33%)
  Pallas kernels  33.7 us (18%)
  local copies, waits for them, and re-layouts  12.2 us (7%)
  other arithmetic  2.65 us (1%)
    ppermute x4, waiting for transfers between devices, ring_step(): lax.ppermute(forward, RING, ahead)  32.3 us
    ppermute x1, waiting for transfers between devices, local(): total = kept + lax.ppermute(given, 'zl1', [(0, 1), (1, 0)])  17.9 us
    pallas_call x1, Pallas kernels, picked_rows(): pl.pallas_call(pick_kernel, grid=(members,), in_specs=[pl.BlockSpec((1, l...  12.1 us
    ppermute x3, starting transfers between devices, ring_step(): lax.ppermute(backward, RING, back)  11.9 us
    pallas_call x1, Pallas kernels, dense_rows(): pl.pallas_call(dense_kernel, grid=(rows // tile,), in_specs=[pl.BlockSpec...  11.9 us
    ppermute x1, starting transfers between devices, both_halves(): return (cut, lax.ppermute(cut, 'zh', [(0, 1), (1, 0)]))  11.5 us
    all_to_all x1, starting transfers between devices, local(): lax.all_to_all(dense.reshape(owners, rows_dev, -1), TABLE, split_axis=0,...  10.1 us
    ppermute x3, waiting for transfers between devices, across_x(): part = lax.ppermute(part, ('x1', 'x0'), [(i, i ^ k) for i in range(4)])  9.85 us
  transfers between devices with their start and end apart: 15, of which 7 were waited for; matrix products, arithmetic and copies ran while one was open for 3% of the time, Pallas kernels for 17%

profile of v2, /device:TPU:1, one launch (start us, length us, event | category | flops | bytes accessed | tf_op | source)
XLA Modules:
  0.0 182.7 jit_solution(17584755495460145560)
XLA Ops:
  0.6 1.4 reshape.78
  2.2 11.5 %collective-permute-start = (bf16[4,64,256]{2,1,0:T(8,128)(2,1)S(1)}, bf16[4,64,256]{2,1,0:T(8,128)(2,1)S(1)}, u32[]{:S(2)}, u32[]{:S(2)}) collective-permute-start(bf16[4,64,256]{2,1,0:T(8,128)(2,1)S(1)} %bitcast.38), channel_id=1, source_target_pairs={{0,1},{1,0},{2,3},{3,2},{4,5},{5,4},{6,7},{7,6},{8,9},{9,8},{10,11... | collective-permute-start | bytes 393224 | tf_op jit(solution)/shard_map/ppermute | solution.py:234
  13.7 1.0 copy-done.1
  14.7 1.0 copy-done.3
  18.1 4.8 %outgoing_rows.1 = (bf16[32,144,128]{2,1,0:T(8,128)(2,1)}, bf16[64,128]{1,0:T(8,128)(2,1)S(1)}) custom-call(bf16[1,64,4096]{2,1,0:T(8,128)(2,1)S(1)} %copy-done.1, bf16[1,64,4096]{2,1,0:T(8,128)(2,1)S(1)} %copy-done.3, s32[1,2,64,128]{3,2,1,0:T(8,128)S(1)} %copy-done.5, f32[1,2,64,128]{3,2,1,0:T(8,128)S(1)} %copy-done.8, s32[1,2,1,128]{3,2,1,0:T(1,128)S(1)} %copy-done.10), custom_call_target="tpu_custom_call" | custom-call | tf_op jit(solution)/shard_map/outgoing_rows/pallas_call | solution.py:62
  22.9 7.3 %all-to-all-start = ((bf16[32,144,128]{2,1,0:T(8,128)(2,1)}), bf16[32,144,128]{2,1,0:T(8,128)(2,1)S(1)}, u32[]{:S(2)}, u32[]{:S(2)}) async-start(bf16[32,144,128]{2,1,0:T(8,128)(2,1)} %get-tuple-element.18), calls=%async_computation | async-start | bytes 2359296 | tf_op jit(solution)/shard_map/all_to_all | solution.py:278
  30.3 4.5 %collective-permute-start.3 = (bf16[128,256]{1,0:T(8,128)(2,1)S(1)}, bf16[128,256]{1,0:T(8,128)(2,1)S(1)}, u32[]{:S(2)}, u32[]{:S(2)}) collective-permute-start(bf16[128,256]{1,0:T(8,128)(2,1)S(1)} %pad_maximum_fusion.2), channel_id=1, source_target_pairs={{0,48},{16,32},{32,16},{48,0},{1,49},{17,33},{33,17},{49,1},{2,50}... | collective-permute-start | bytes 196616 | tf_op jit(solution)/shard_map/ppermute | solution.py:245
  34.8 2.5 %collective-permute-start.2 = (bf16[128,256]{1,0:T(8,128)(2,1)S(1)}, bf16[128,256]{1,0:T(8,128)(2,1)S(1)}, u32[]{:S(2)}, u32[]{:S(2)}) collective-permute-start(bf16[128,256]{1,0:T(8,128)(2,1)S(1)} %pad_maximum_fusion.1), channel_id=1, source_target_pairs={{0,32},{16,48},{32,0},{48,16},{1,33},{17,49},{33,1},{49,17},{2,34}... | collective-permute-start | bytes 196616 | tf_op jit(solution)/shard_map/ppermute | solution.py:245
  37.3 2.0 %collective-permute-start.1 = (bf16[128,256]{1,0:T(8,128)(2,1)S(1)}, bf16[128,256]{1,0:T(8,128)(2,1)S(1)}, u32[]{:S(2)}, u32[]{:S(2)}) collective-permute-start(bf16[128,256]{1,0:T(8,128)(2,1)S(1)} %pad_maximum_fusion), channel_id=1, source_target_pairs={{0,16},{16,0},{32,48},{48,32},{1,17},{17,1},{33,49},{49,33},{2,18}... | collective-permute-start | bytes 196616 | tf_op jit(solution)/shard_map/ppermute | solution.py:245
  39.4 9.0 %collective-permute-done.1 = bf16[128,256]{1,0:T(8,128)(2,1)S(1)} collective-permute-done((bf16[128,256]{1,0:T(8,128)(2,1)S(1)}, bf16[128,256]{1,0:T(8,128)(2,1)S(1)}, u32[]{:S(2)}, u32[]{:S(2)}) %collective-permute-start.1) | collective-permute-done | bytes 65568 | tf_op jit(solution)/shard_map/ppermute | solution.py:245
  49.3 3.0 %collective-permute-start.4 = (bf16[512,256]{1,0:T(8,128)(2,1)S(1)}, bf16[512,256]{1,0:T(8,128)(2,1)S(1)}, u32[]{:S(2)}, u32[]{:S(2)}) collective-permute-start(bf16[512,256]{1,0:T(8,128)(2,1)S(1)} %constant_dynamic-update-slice_fusion.refs_0_), channel_id=1, source_target_pairs={{0,2},{2,4},{4,6},{6,8},{8,10},{10,12},{12,14},{14,0},{1,3},{3,5},... | collective-permute-start | bytes 786440 | tf_op jit(solution)/shard_map/ppermute | solution.py:255
  52.2 3.8 %collective-permute-start.5 = (bf16[512,256]{1,0:T(8,128)(2,1)S(1)}, bf16[512,256]{1,0:T(8,128)(2,1)S(1)}, u32[]{:S(2)}, u32[]{:S(2)}) collective-permute-start(bf16[512,256]{1,0:T(8,128)(2,1)S(1)} %constant_dynamic-update-slice_fusion.refs_0_), channel_id=1, source_target_pairs={{0,14},{2,0},{4,2},{6,4},{8,6},{10,8},{12,10},{14,12},{1,15},{3,1}... | collective-permute-start | bytes 786440 | tf_op jit(solution)/shard_map/ppermute | solution.py:256
  56.4 11.9 %dense_rows.1 = bf16[4096,128]{1,0:T(8,128)(2,1)} custom-call(f32[32,128]{1,0:T(8,128)S(1)} %bitcast.36, bf16[32,144,128]{2,1,0:T(8,128)(2,1)S(1)} %all-to-all-done.rows_ref), custom_call_target="tpu_custom_call" | custom-call | tf_op jit(solution)/shard_map/dense_rows/pallas_call | solution.py:119
  68.3 10.1 %all-to-all-start.2 = ((bf16[64,64,128]{2,1,0:T(8,128)(2,1)}), bf16[64,64,128]{2,1,0:T(8,128)(2,1)S(1)}, u32[]{:S(2)}, u32[]{:S(2)}) async-start(bf16[64,64,128]{2,1,0:T(8,128)(2,1)} %bitcast.14), calls=%async_computation.2 | async-start | bytes 2097152 | tf_op jit(solution)/shard_map/all_to_all | solution.py:287
  78.4 2.9 %collective-permute-start.6 = (bf16[512,256]{1,0:T(8,128)(2,1)S(1)}, bf16[512,256]{1,0:T(8,128)(2,1)S(1)}, u32[]{:S(2)}, u32[]{:S(2)}) collective-permute-start(bf16[512,256]{1,0:T(8,128)(2,1)S(1)} %collective-permute-done.4.refs_1_), channel_id=1, source_target_pairs={{0,2},{2,4},{4,6},{6,8},{8,10},{10,12},{12,14},{14,0},{1,3},{3,5},... | collective-permute-start | bytes 786440 | tf_op jit(solution)/shard_map/ppermute | solution.py:255
  81.4 3.6 %collective-permute-start.7 = (bf16[512,256]{1,0:T(8,128)(2,1)S(1)}, bf16[512,256]{1,0:T(8,128)(2,1)S(1)}, u32[]{:S(2)}, u32[]{:S(2)}) collective-permute-start(bf16[512,256]{1,0:T(8,128)(2,1)S(1)} %collective-permute-done.5.refs_2_), channel_id=1, source_target_pairs={{0,14},{2,0},{4,2},{6,4},{8,6},{10,8},{12,10},{14,12},{1,15},{3,1}... | collective-permute-start | bytes 786440 | tf_op jit(solution)/shard_map/ppermute | solution.py:256
  85.0 23.6 %collective-permute-done.6.refs_3_ = bf16[512,256]{1,0:T(8,128)(2,1)S(1)} collective-permute-done((bf16[512,256]{1,0:T(8,128)(2,1)S(1)}, bf16[512,256]{1,0:T(8,128)(2,1)S(1)}, u32[]{:S(2)}, u32[]{:S(2)}) %collective-permute-start.6) | collective-permute-done | bytes 262176 | tf_op jit(solution)/shard_map/ppermute | solution.py:255
  108.5 1.9 %collective-permute-start.8 = (bf16[512,256]{1,0:T(8,128)(2,1)S(1)}, bf16[512,256]{1,0:T(8,128)(2,1)S(1)}, u32[]{:S(2)}, u32[]{:S(2)}) collective-permute-start(bf16[512,256]{1,0:T(8,128)(2,1)S(1)} %collective-permute-done.6.refs_3_), channel_id=1, source_target_pairs={{0,2},{2,4},{4,6},{6,8},{8,10},{10,12},{12,14},{14,0},{1,3},{3,5},... | collective-permute-start | bytes 786440 | tf_op jit(solution)/shard_map/ppermute | solution.py:255
  110.8 4.6 %collective-permute-start.9 = (bf16[512,256]{1,0:T(8,128)(2,1)S(1)}, bf16[512,256]{1,0:T(8,128)(2,1)S(1)}, u32[]{:S(2)}, u32[]{:S(2)}) collective-permute-start(bf16[512,256]{1,0:T(8,128)(2,1)S(1)} %collective-permute-done.7.refs_4_), channel_id=1, source_target_pairs={{0,14},{2,0},{4,2},{6,4},{8,6},{10,8},{12,10},{14,12},{1,15},{3,1}... | collective-permute-start | bytes 786440 | tf_op jit(solution)/shard_map/ppermute | solution.py:256
  115.4 2.4 %collective-permute-done.8.refs_5_ = bf16[512,256]{1,0:T(8,128)(2,1)S(1)} collective-permute-done((bf16[512,256]{1,0:T(8,128)(2,1)S(1)}, bf16[512,256]{1,0:T(8,128)(2,1)S(1)}, u32[]{:S(2)}, u32[]{:S(2)}) %collective-permute-start.8) | collective-permute-done | bytes 262176 | tf_op jit(solution)/shard_map/ppermute | solution.py:255
  117.8 1.9 %collective-permute-start.10 = (bf16[512,256]{1,0:T(8,128)(2,1)S(1)}, bf16[512,256]{1,0:T(8,128)(2,1)S(1)}, u32[]{:S(2)}, u32[]{:S(2)}) collective-permute-start(bf16[512,256]{1,0:T(8,128)(2,1)S(1)} %collective-permute-done.8.refs_5_), channel_id=1, source_target_pairs={{0,2},{2,4},{4,6},{6,8},{8,10},{10,12},{12,14},{14,0},{1,3},{3,5},... | collective-permute-start | bytes 786440 | tf_op jit(solution)/shard_map/ppermute | solution.py:255
  119.8 6.4 %collective-permute-done.10.refs_7_ = bf16[512,256]{1,0:T(8,128)(2,1)S(1)} collective-permute-done((bf16[512,256]{1,0:T(8,128)(2,1)S(1)}, bf16[512,256]{1,0:T(8,128)(2,1)S(1)}, u32[]{:S(2)}, u32[]{:S(2)}) %collective-permute-start.10) | collective-permute-done | bytes 262176 | tf_op jit(solution)/shard_map/ppermute | solution.py:255
  126.1 12.1 %picked_rows.1 = bf16[16,256,256]{2,1,0:T(8,128)(2,1)S(1)} custom-call(f32[16,2,128]{2,1,0:T(2,128)S(1)} %dynamic-slice_bitcast_fusion.7.ids_ref, f32[8,512]{1,0:T(8,128)S(1)} %add_convert_fusion.place_ref, bf16[512,256]{1,0:T(8,128)(2,1)S(1)} %constant_dynamic-update-slice_fusion.refs_0_, bf16[512,256]{1,0:T(8,128)(2,1)S(1)} %collective-permute-done.4.refs_1_, ...), custom_call_target="tpu_custom_call" | custom-call | tf_op jit(solution)/shard_map/picked_rows/pallas_call | solution.py:154
  138.2 1.4 copy-done
  140.6 9.4 %all-to-all-start.1 = ((bf16[16,256,256]{2,1,0:T(8,128)(2,1)}), bf16[16,256,256]{2,1,0:T(8,128)(2,1)S(1)}, u32[]{:S(2)}, u32[]{:S(2)}) async-start(bf16[16,256,256]{2,1,0:T(8,128)(2,1)} %copy-done), calls=%async_computation.1 | async-start | bytes 4194304 | tf_op jit(solution)/shard_map/all_to_all | solution.py:298
  150.0 1.5 convert_reduce_fusion
  152.9 3.0 %collective-permute-start.11 = (f32[2,2,64,128]{3,2,1,0:T(8,128)}, f32[2,2,64,128]{3,2,1,0:T(8,128)S(1)}, u32[]{:S(2)}, u32[]{:S(2)}) collective-permute-start(f32[2,2,64,128]{3,2,1,0:T(8,128)} %dynamic-slice_bitcast_fusion), channel_id=1, source_target_pairs={{0,256},{256,0},{1,257},{257,1},{2,258},{258,2},{3,259},{259,3},{4... | collective-permute-start | bytes 393224 | tf_op jit(solution)/shard_map/ppermute | solution.py:305
  155.9 2.4 %mixing_b.1.mix_b_ref = bf16[64,128]{1,0:T(8,128)(2,1)S(1)} custom-call(s32[1,2,64,128]{3,2,1,0:T(8,128)S(1)} %copy-done.6, f32[1,2,64,128]{3,2,1,0:T(8,128)S(1)} %copy-done.9), custom_call_target="tpu_custom_call" | custom-call | tf_op jit(solution)/shard_map/mixing_b/pallas_call | solution.py:86
  158.4 17.9 %collective-permute-done.11 = f32[2,2,64,128]{3,2,1,0:T(8,128)S(1)} collective-permute-done((f32[2,2,64,128]{3,2,1,0:T(8,128)}, f32[2,2,64,128]{3,2,1,0:T(8,128)S(1)}, u32[]{:S(2)}, u32[]{:S(2)}) %collective-permute-start.11) | collective-permute-done | bytes 131104 | tf_op jit(solution)/shard_map/ppermute | solution.py:305
  178.0 1.1 all-to-all-done.1.rows_ref
  179.1 1.0 copy-done.7
  180.2 2.5 %final_outputs.1 = (bf16[1,64,4096]{2,1,0:T(8,128)(2,1)}, bf16[1,64,4096]{2,1,0:T(8,128)(2,1)}, f32[1,64,128]{2,1,0:T(8,128)}) custom-call(bf16[16,256,256]{2,1,0:T(8,128)(2,1)S(1)} %all-to-all-done.1.rows_ref, bf16[64,128]{1,0:T(8,128)(2,1)S(1)} %get-tuple-element.25.mix_a_ref, bf16[64,128]{1,0:T(8,128)(2,1)S(1)} %mixing_b.1.mix_b_ref, ...), custom_call_target="tpu_custom_call" | custom-call | tf_op jit(solution)/shard_map/final_outputs/pallas_call | solution.py:209
  (64 shorter events, 8.3 us)
Async XLA Ops:
  2.2 20.7 %collective-permute-start = (bf16[4,64,256]{2,1,0:T(8,128)(2,1)S(1)}, bf16[4,64,256]{2,1,0:T(8,128)(2,1)S(1)}, u32[]{:S(2)}, u32[]{:S(2)}) collective-permute-start(bf16[4,64,256]{2,1,0:T(8,128)(2,1)S(1)} %bitcast.38), channel_id=1, source_target_pairs={{0,1},{1,0},{2,3},{3,2},{4,5},{5,4},{6,7},{7,6},{8,9},{9,8},{10,11... | collective-permute-start | bytes 393224 | tf_op jit(solution)/shard_map/ppermute | solution.py:234
  13.7 1.0 copy-start.1
  14.7 1.0 copy-start.3
  15.8 0.8 copy-start.5
  16.6 0.8 copy-start.8
  17.4 0.7 copy-start.10
  22.9 26.4 %all-to-all-start = ((bf16[32,144,128]{2,1,0:T(8,128)(2,1)}), bf16[32,144,128]{2,1,0:T(8,128)(2,1)S(1)}, u32[]{:S(2)}, u32[]{:S(2)}) async-start(bf16[32,144,128]{2,1,0:T(8,128)(2,1)} %get-tuple-element.18), calls=%async_computation | async-start | bytes 2359296 | tf_op jit(solution)/shard_map/all_to_all | solution.py:278
  30.3 19.0 %collective-permute-start.3 = (bf16[128,256]{1,0:T(8,128)(2,1)S(1)}, bf16[128,256]{1,0:T(8,128)(2,1)S(1)}, u32[]{:S(2)}, u32[]{:S(2)}) collective-permute-start(bf16[128,256]{1,0:T(8,128)(2,1)S(1)} %pad_maximum_fusion.2), channel_id=1, source_target_pairs={{0,48},{16,32},{32,16},{48,0},{1,49},{17,33},{33,17},{49,1},{2,50}... | collective-permute-start | bytes 196616 | tf_op jit(solution)/shard_map/ppermute | solution.py:245
  34.8 13.5 %collective-permute-start.2 = (bf16[128,256]{1,0:T(8,128)(2,1)S(1)}, bf16[128,256]{1,0:T(8,128)(2,1)S(1)}, u32[]{:S(2)}, u32[]{:S(2)}) collective-permute-start(bf16[128,256]{1,0:T(8,128)(2,1)S(1)} %pad_maximum_fusion.1), channel_id=1, source_target_pairs={{0,32},{16,48},{32,0},{48,16},{1,33},{17,49},{33,1},{49,17},{2,34}... | collective-permute-start | bytes 196616 | tf_op jit(solution)/shard_map/ppermute | solution.py:245
  37.3 11.0 %collective-permute-start.1 = (bf16[128,256]{1,0:T(8,128)(2,1)S(1)}, bf16[128,256]{1,0:T(8,128)(2,1)S(1)}, u32[]{:S(2)}, u32[]{:S(2)}) collective-permute-start(bf16[128,256]{1,0:T(8,128)(2,1)S(1)} %pad_maximum_fusion), channel_id=1, source_target_pairs={{0,16},{16,0},{32,48},{48,32},{1,17},{17,1},{33,49},{49,33},{2,18}... | collective-permute-start | bytes 196616 | tf_op jit(solution)/shard_map/ppermute | solution.py:245
  49.3 19.0 %collective-permute-start.4 = (bf16[512,256]{1,0:T(8,128)(2,1)S(1)}, bf16[512,256]{1,0:T(8,128)(2,1)S(1)}, u32[]{:S(2)}, u32[]{:S(2)}) collective-permute-start(bf16[512,256]{1,0:T(8,128)(2,1)S(1)} %constant_dynamic-update-slice_fusion.refs_0_), channel_id=1, source_target_pairs={{0,2},{2,4},{4,6},{6,8},{8,10},{10,12},{12,14},{14,0},{1,3},{3,5},... | collective-permute-start | bytes 786440 | tf_op jit(solution)/shard_map/ppermute | solution.py:255
  52.2 16.0 %collective-permute-start.5 = (bf16[512,256]{1,0:T(8,128)(2,1)S(1)}, bf16[512,256]{1,0:T(8,128)(2,1)S(1)}, u32[]{:S(2)}, u32[]{:S(2)}) collective-permute-start(bf16[512,256]{1,0:T(8,128)(2,1)S(1)} %constant_dynamic-update-slice_fusion.refs_0_), channel_id=1, source_target_pairs={{0,14},{2,0},{4,2},{6,4},{8,6},{10,8},{12,10},{14,12},{1,15},{3,1}... | collective-permute-start | bytes 786440 | tf_op jit(solution)/shard_map/ppermute | solution.py:256
  56.4 22.0 %copy-start.13 = (s32[8]{0:T(128)S(1)}, s32[8]{0:T(128)}, u32[]{:S(2)}) copy-start(s32[8]{0:T(128)} %constant.85.clone) | copy-start | bytes 100
  68.3 71.3 %all-to-all-start.2 = ((bf16[64,64,128]{2,1,0:T(8,128)(2,1)}), bf16[64,64,128]{2,1,0:T(8,128)(2,1)S(1)}, u32[]{:S(2)}, u32[]{:S(2)}) async-start(bf16[64,64,128]{2,1,0:T(8,128)(2,1)} %bitcast.14), calls=%async_computation.2 | async-start | bytes 2097152 | tf_op jit(solution)/shard_map/all_to_all | solution.py:287
  78.4 30.1 %collective-permute-start.6 = (bf16[512,256]{1,0:T(8,128)(2,1)S(1)}, bf16[512,256]{1,0:T(8,128)(2,1)S(1)}, u32[]{:S(2)}, u32[]{:S(2)}) collective-permute-start(bf16[512,256]{1,0:T(8,128)(2,1)S(1)} %collective-permute-done.4.refs_1_), channel_id=1, source_target_pairs={{0,2},{2,4},{4,6},{6,8},{8,10},{10,12},{12,14},{14,0},{1,3},{3,5},... | collective-permute-start | bytes 786440 | tf_op jit(solution)/shard_map/ppermute | solution.py:255
  81.4 29.4 %collective-permute-start.7 = (bf16[512,256]{1,0:T(8,128)(2,1)S(1)}, bf16[512,256]{1,0:T(8,128)(2,1)S(1)}, u32[]{:S(2)}, u32[]{:S(2)}) collective-permute-start(bf16[512,256]{1,0:T(8,128)(2,1)S(1)} %collective-permute-done.5.refs_2_), channel_id=1, source_target_pairs={{0,14},{2,0},{4,2},{6,4},{8,6},{10,8},{12,10},{14,12},{1,15},{3,1}... | collective-permute-start | bytes 786440 | tf_op jit(solution)/shard_map/ppermute | solution.py:256
  108.5 9.3 %collective-permute-start.8 = (bf16[512,256]{1,0:T(8,128)(2,1)S(1)}, bf16[512,256]{1,0:T(8,128)(2,1)S(1)}, u32[]{:S(2)}, u32[]{:S(2)}) collective-permute-start(bf16[512,256]{1,0:T(8,128)(2,1)S(1)} %collective-permute-done.6.refs_3_), channel_id=1, source_target_pairs={{0,2},{2,4},{4,6},{6,8},{8,10},{10,12},{12,14},{14,0},{1,3},{3,5},... | collective-permute-start | bytes 786440 | tf_op jit(solution)/shard_map/ppermute | solution.py:255
  110.8 8.9 %collective-permute-start.9 = (bf16[512,256]{1,0:T(8,128)(2,1)S(1)}, bf16[512,256]{1,0:T(8,128)(2,1)S(1)}, u32[]{:S(2)}, u32[]{:S(2)}) collective-permute-start(bf16[512,256]{1,0:T(8,128)(2,1)S(1)} %collective-permute-done.7.refs_4_), channel_id=1, source_target_pairs={{0,14},{2,0},{4,2},{6,4},{8,6},{10,8},{12,10},{14,12},{1,15},{3,1}... | collective-permute-start | bytes 786440 | tf_op jit(solution)/shard_map/ppermute | solution.py:256
  117.8 8.3 %collective-permute-start.10 = (bf16[512,256]{1,0:T(8,128)(2,1)S(1)}, bf16[512,256]{1,0:T(8,128)(2,1)S(1)}, u32[]{:S(2)}, u32[]{:S(2)}) collective-permute-start(bf16[512,256]{1,0:T(8,128)(2,1)S(1)} %collective-permute-done.8.refs_5_), channel_id=1, source_target_pairs={{0,2},{2,4},{4,6},{6,8},{8,10},{10,12},{12,14},{14,0},{1,3},{3,5},... | collective-permute-start | bytes 786440 | tf_op jit(solution)/shard_map/ppermute | solution.py:255
  138.2 1.4 copy-start
  139.6 16.3 %copy-start.6 = (s32[1,2,64,128]{3,2,1,0:T(8,128)S(1)}, s32[1,2,64,128]{3,2,1,0:T(8,128)}, u32[]{:S(2)}) copy-start(s32[1,2,64,128]{3,2,1,0:T(8,128)} %slots_ref.5) | copy-start | bytes 196612
  139.6 16.4 %copy-start.9 = (f32[1,2,64,128]{3,2,1,0:T(8,128)S(1)}, f32[1,2,64,128]{3,2,1,0:T(8,128)}, u32[]{:S(2)}) copy-start(f32[1,2,64,128]{3,2,1,0:T(8,128)} %weights_ref.3) | copy-start | bytes 196612
  139.6 1.0 copy-start.11
  140.6 38.6 %all-to-all-start.1 = ((bf16[16,256,256]{2,1,0:T(8,128)(2,1)}), bf16[16,256,256]{2,1,0:T(8,128)(2,1)S(1)}, u32[]{:S(2)}, u32[]{:S(2)}) async-start(bf16[16,256,256]{2,1,0:T(8,128)(2,1)} %copy-done), calls=%async_computation.1 | async-start | bytes 4194304 | tf_op jit(solution)/shard_map/all_to_all | solution.py:298
  150.0 29.1 %copy-start.2 = (bf16[1,64,4096]{2,1,0:T(8,128)(2,1)S(1)}, bf16[1,64,4096]{2,1,0:T(8,128)(2,1)}, u32[]{:S(2)}) copy-start(bf16[1,64,4096]{2,1,0:T(8,128)(2,1)} %gate_a_ref.1) | copy-start | bytes 1572868
  150.0 29.1 %copy-start.4 = (bf16[1,64,4096]{2,1,0:T(8,128)(2,1)S(1)}, bf16[1,64,4096]{2,1,0:T(8,128)(2,1)}, u32[]{:S(2)}) copy-start(bf16[1,64,4096]{2,1,0:T(8,128)(2,1)} %cot_ref.3) | copy-start | bytes 1572868
  151.5 0.7 copy-start.12
  152.9 23.4 %collective-permute-start.11 = (f32[2,2,64,128]{3,2,1,0:T(8,128)}, f32[2,2,64,128]{3,2,1,0:T(8,128)S(1)}, u32[]{:S(2)}, u32[]{:S(2)}) collective-permute-start(f32[2,2,64,128]{3,2,1,0:T(8,128)} %dynamic-slice_bitcast_fusion), channel_id=1, source_target_pairs={{0,256},{256,0},{1,257},{257,1},{2,258},{258,2},{3,259},{259,3},{4... | collective-permute-start | bytes 393224 | tf_op jit(solution)/shard_map/ppermute | solution.py:305
  179.1 1.0 copy-start.7

commit v3 on v2

--- a/solution.py
+++ b/solution.py
@@ -15,6 +15,7 @@
 F32 = jnp.float32
 BF16 = jnp.bfloat16
 VMEM = pltpu.CompilerParams(vmem_limit_bytes=40 * 1024 * 1024)
+MOST_VMEM = pltpu.CompilerParams(vmem_limit_bytes=60 * 1024 * 1024)
 
 
 def gated(gate, incoming):
@@ -71,27 +72,47 @@
             jax.ShapeDtypeStruct((chunks, listed + 16, features), BF16),
             jax.ShapeDtypeStruct((tokens, listed), BF16),
         ],
-        compiler_params=VMEM,
+        compiler_params=MOST_VMEM,
         name="outgoing_rows",
     )(gate, cot, slots, weights, row_ids)
 
 
-def mixing_kernel(slots_ref, weights_ref, out_ref):
-    out_ref[...] = mixing_of(slots_ref[0, 0], weights_ref[0, 0])
-
-
-def mixing_b(slots, weights):
-    tokens, listed = slots.shape[2:]
+def factors_kernel(
+    gate_a_ref, cot_ref, gate_b_ref, slots_ref, weights_ref,
+    to_gate_ref, to_memory_ref, swish_ref, mix_ref,
+):
+    @pl.when(pl.program_id(0) == 0)
+    def _():
+        mix_ref[...] = mixing_of(slots_ref[0, 0], weights_ref[0, 0])
+
+    g, sig, inc = gated(gate_a_ref[0], cot_ref[0])
+    to_gate_ref[...] = inc * sig * (1.0 + g * (1.0 - sig))
+    to_memory_ref[...] = (inc * g * sig).astype(BF16)
+    gb = gate_b_ref[0].astype(F32)
+    swish_ref[...] = gb / (1.0 + jnp.exp(-gb))
+
+
+def factors(gate_a, cot, gate_b, slots, weights):
+    _, tokens, width = gate_a.shape
+    listed = slots.shape[-1]
+    cols = width // 2
+    part = pl.BlockSpec((1, tokens, cols), lambda i: (0, 0, i))
+    out = pl.BlockSpec((tokens, cols), lambda i: (0, i))
     picks = pl.BlockSpec((1, 1, tokens, listed), lambda i: (0, 1, 0, 0))
     return pl.pallas_call(
-        mixing_kernel,
-        grid=(1,),
-        in_specs=[picks, picks],
-        out_specs=pl.BlockSpec((tokens, listed), lambda i: (0, 0)),
-        out_shape=jax.ShapeDtypeStruct((tokens, listed), BF16),
-        compiler_params=VMEM,
-        name="mixing_b",
-    )(slots, weights)
+        factors_kernel,
+        grid=(width // cols,),
+        in_specs=[part, part, part, picks, picks],
+        out_specs=[out, out, out, pl.BlockSpec((tokens, listed), lambda i: (0, 0))],
+        out_shape=[
+            jax.ShapeDtypeStruct((tokens, width), F32),
+            jax.ShapeDtypeStruct((tokens, width), BF16),
+            jax.ShapeDtypeStruct((tokens, width), F32),
+            jax.ShapeDtypeStruct((tokens, listed), BF16),
+        ],
+        compiler_params=MOST_VMEM,
+        name="factors",
+    )(gate_a, cot, gate_b, slots, weights)
 
 
 def dense_kernel(ids_ref, rows_ref, out_ref):
@@ -161,13 +182,13 @@
         + [pl.BlockSpec((rows, features), lambda i: (0, 0))] * len(blocks),
         out_specs=pl.BlockSpec((1, lists * listed, features), lambda i: (i, 0, 0)),
         out_shape=jax.ShapeDtypeStruct((members, lists * listed, features), BF16),
-        compiler_params=VMEM,
+        compiler_params=MOST_VMEM,
         name="picked_rows",
     )(ids, places, *blocks)
 
 
 def final_kernel(
-    rows_ref, mix_a_ref, mix_b_ref, gate_a_ref, cot_ref, gate_b_ref, slots_ref,
+    rows_ref, mix_a_ref, mix_b_ref, to_gate_ref, to_memory_ref, swish_ref, slots_ref,
     mixed_ref, grad_gate_ref, grad_weights_ref, scores_ref,
 ):
     listed = mix_a_ref.shape[1]
@@ -183,14 +204,11 @@
         fetched_a = rows_ref[k, :listed, :]
         fetched_b = rows_ref[k, listed:, :]
         memory_b = jnp.dot(mix_b_ref[...], fetched_b, preferred_element_type=F32)
-        gb = gate_b_ref[0, :, at].astype(F32)
-        mixed_ref[0, :, at] = (gb / (1.0 + jnp.exp(-gb)) * memory_b).astype(BF16)
+        mixed_ref[0, :, at] = (swish_ref[:, at] * memory_b).astype(BF16)
         memory_a = jnp.dot(mix_a_ref[...], fetched_a, preferred_element_type=F32)
-        g, sig, inc = gated(gate_a_ref[0, :, at], cot_ref[0, :, at])
-        grad_gate_ref[0, :, at] = (inc * memory_a * sig * (1.0 + g * (1.0 - sig))).astype(BF16)
-        grad_memory = (inc * g * sig).astype(BF16)
+        grad_gate_ref[0, :, at] = (to_gate_ref[:, at] * memory_a).astype(BF16)
         part += lax.dot_general(
-            grad_memory, fetched_a, (((1,), (1,)), ((), ())), preferred_element_type=F32
+            to_memory_ref[:, at], fetched_a, (((1,), (1,)), ((), ())), preferred_element_type=F32
         )
     scores_ref[...] += part
 
@@ -199,13 +217,14 @@
         grad_weights_ref[0] = jnp.take_along_axis(scores_ref[...], slots_ref[0, 0], axis=1)
 
 
-def final_outputs(fetched, mix_a, mix_b, gate_a, cot, gate_b, slots):
+def final_outputs(fetched, mix_a, mix_b, to_gate, to_memory, swish, slots):
     chunks, rows, features = fetched.shape
-    _, tokens, width = gate_a.shape
+    tokens, width = to_gate.shape
     listed = mix_a.shape[1]
     step = 4
     whole = pl.BlockSpec((tokens, listed), lambda i: (0, 0))
-    part = pl.BlockSpec((1, tokens, step * features), lambda i: (0, 0, i))
+    part = pl.BlockSpec((tokens, step * features), lambda i: (0, i))
+    out = pl.BlockSpec((1, tokens, step * features), lambda i: (0, 0, i))
     return pl.pallas_call(
         final_kernel,
         grid=(chunks // step,),
@@ -214,32 +233,43 @@
             whole, whole, part, part, part,
             pl.BlockSpec((1, 1, tokens, listed), lambda i: (0, 0, 0, 0)),
         ],
-        out_specs=[part, part, pl.BlockSpec((1, tokens, listed), lambda i: (0, 0, 0))],
+        out_specs=[out, out, pl.BlockSpec((1, tokens, listed), lambda i: (0, 0, 0))],
         out_shape=[
             jax.ShapeDtypeStruct((1, tokens, width), BF16),
             jax.ShapeDtypeStruct((1, tokens, width), BF16),
             jax.ShapeDtypeStruct((1, tokens, listed), F32),
         ],
         scratch_shapes=[pltpu.VMEM((tokens, listed), F32)],
-        compiler_params=VMEM,
+        compiler_params=MOST_VMEM,
         name="final_outputs",
-    )(fetched, mix_a, mix_b, gate_a, cot, gate_b, slots)
+    )(fetched, mix_a, mix_b, to_gate, to_memory, swish, slots)
+
+
+def features_for(table, zl0):
+    rows_dev, width = table.shape
+    at = (zl0 * 2 + lax.axis_index("c")) * (width // 8)
+    return jnp.stack(
+        [lax.dynamic_slice(table, (0, at + h * (width // 2)), (rows_dev, width // 8)) for h in range(2)]
+    )
 
 
 def both_halves(table):
-    rows_dev, width = table.shape
-    cut = table.reshape(rows_dev, 2, 4, 2, -1)
-    cut = lax.dynamic_index_in_dim(cut, lax.axis_index(("zl0", "c")), 2, keepdims=False)
-    cut = jnp.transpose(cut.reshape(rows_dev, 4, -1), (1, 0, 2))
-    return cut, lax.ppermute(cut, "zh", [(0, 1), (1, 0)])
+    zl0 = lax.axis_index("zl0")
+    mirrored = lax.ppermute(features_for(table, 1 - zl0), ("zl1", "zl0", "zh"), [(i, 7 - i) for i in range(8)])
+    return features_for(table, zl0), mirrored
 
 
 def across_x(own, other):
     at_x = lax.axis_index(("x1", "x0"))
+    rows, half = own.shape[1], own.shape[2] // 2
     mine = []
     for k in range(4):
+        to = at_x ^ k
         part = jnp.concatenate(
-            [lax.dynamic_index_in_dim(h, at_x ^ k, 0, keepdims=False) for h in (own, other)]
+            [
+                lax.dynamic_slice(h, (to // 2, 0, (to % 2) * half), (1, rows, half))[0]
+                for h in (own, other)
+            ]
         )
         if k:
             part = lax.ppermute(part, ("x1", "x0"), [(i, i ^ k) for i in range(4)])
@@ -274,21 +304,22 @@
 
     own, other = both_halves(table)
     sent, mix_a = outgoing(gate_a, cotangent_a, slots, weights, row_ids, 128)
-    sent, own, other = lax.optimization_barrier((sent, own, other))
+    sent, other = lax.optimization_barrier((sent, other))
+    block = across_x(own, other)
+    sent, block = lax.optimization_barrier((sent, block))
     received = lax.all_to_all(sent, GRAD_GROUP, split_axis=0, concat_axis=0, tiled=True)
-    block = across_x(own, other)
-    received, block = lax.optimization_barrier((received, block))
+    f1, b1 = ring_step(block, block)
+    f2, b2 = ring_step(f1, b1)
+    received, f2, b2 = lax.optimization_barrier((received, f2, b2))
 
     codes = received[:, listed : listed + 4, :].astype(F32)
     ids = codes[:, 0::2] * ROWS_DEV + codes[:, 1::2]
     dense = dense_rows(ids[:, 0], received, owners * rows_dev)
-    f1, b1 = ring_step(block, block)
-    dense, f1, b1 = lax.optimization_barrier((dense, f1, b1))
+    f3, b3 = ring_step(f2, b2)
+    dense, f3, b3 = lax.optimization_barrier((dense, f3, b3))
     arrived = lax.all_to_all(
         dense.reshape(owners, rows_dev, -1), TABLE, split_axis=0, concat_axis=0, tiled=True
     )
-    f2, b2 = ring_step(f1, b1)
-    f3, b3 = ring_step(f2, b2)
     f4, _ = ring_step(f3, None)
 
     near = ids.reshape(-1, 2, 2, listed)
@@ -305,9 +336,10 @@
     total = kept + lax.ppermute(given, "zl1", [(0, 1), (1, 0)])
     grad_table = jnp.transpose(total, (2, 0, 1, 3)).reshape(rows_dev, -1)
 
-    mix_b = mixing_b(slots, weights)
+    picked_first = lax.optimization_barrier((picked, gate_a, cotangent_a, gate_b))
+    to_gate, to_memory, swish, mix_b = factors(*picked_first[1:], slots, weights)
     mixed, grad_gate, grad_weights = final_outputs(
-        fetched, mix_a, mix_b, gate_a, cotangent_a, gate_b, slots
+        fetched, mix_a, mix_b, to_gate, to_memory, swish, slots
     )
     return mixed, grad_gate, grad_weights, grad_table
 

time: 184 us -> 192 us (1.043)
  Pallas kernels: 33.7 us -> 42.8 us
  waiting for transfers between devices: 61.1 us -> 69 us
  local copies, waits for them, and re-layouts: 12.2 us -> 5.12 us
    ppermute x3, waiting for transfers between devices: 0.01 us -> 16 us  [ring_step(): lax.ppermute(backward, RING, back)]
    unnamed x32 -> x23, local copies, waits for them, and re-layouts: 8.57 us -> 2.13 us
    ppermute x3, waiting for transfers between devices: 9.85 us -> 4.04 us  [across_x(): part = lax.ppermute(part, ('x1', 'x0'), [(i, i ^ k) for i in range(4)])]
    pallas_call x1, Pallas kernels: 2.43 us -> 5.3 us  [factors(): pl.pallas_call(factors_kernel, grid=(width // cols,), in_specs=[part, par...]
    ppermute x4, waiting for transfers between devices: 32.3 us -> 29.5 us  [ring_step(): lax.ppermute(forward, RING, ahead)]
    pallas_call x1, Pallas kernels: 12.1 us -> 14.7 us  [picked_rows(): pl.pallas_call(pick_kernel, grid=(members,), in_specs=[pl.BlockSpec((1, l...]
    ppermute x3, starting transfers between devices: 11.9 us -> 14 us  [ring_step(): lax.ppermute(backward, RING, back)]
    pallas_call x1, Pallas kernels: 2.54 us -> 4.61 us  [final_outputs(): pl.pallas_call(final_kernel, grid=(chunks // step,), in_specs=[pl.BlockSp...]
  transfers between devices with their start and end apart: 15 -> 15, of which waited for: 7 -> 8; matrix products, arithmetic and copies ran while one was open for 3% -> 2% of each run, Pallas kernels for 17% -> 20%
where the time goes in v3:
time: 192 us; the launch traced here: 191 us
  starting transfers between devices  71.9 us (37%)
  waiting for transfers between devices  69 us (36%)
  Pallas kernels  42.8 us (22%)
  local copies, waits for them, and re-layouts  5.12 us (3%)
    ppermute x4, waiting for transfers between devices, ring_step(): lax.ppermute(forward, RING, ahead)  29.5 us
    ppermute x1, waiting for transfers between devices, local(): total = kept + lax.ppermute(given, 'zl1', [(0, 1), (1, 0)])  17.3 us
    ppermute x3, waiting for transfers between devices, ring_step(): lax.ppermute(backward, RING, back)  16 us
    pallas_call x1, Pallas kernels, picked_rows(): pl.pallas_call(pick_kernel, grid=(members,), in_specs=[pl.BlockSpec((1, l...  14.7 us
    ppermute x3, starting transfers between devices, ring_step(): lax.ppermute(backward, RING, back)  14 us
    pallas_call x1, Pallas kernels, dense_rows(): pl.pallas_call(dense_kernel, grid=(rows // tile,), in_specs=[pl.BlockSpec...  11.9 us
    ppermute x1, starting transfers between devices, both_halves(): lax.ppermute(features_for(table, 1 - zl0), ('zl1', 'zl0', 'zh'), [(i, 7 -...  11.5 us
    all_to_all x1, starting transfers between devices, local(): lax.all_to_all(dense.reshape(owners, rows_dev, -1), TABLE, split_axis=0,...  10.6 us
  transfers between devices with their start and end apart: 15, of which 8 were waited for; matrix products, arithmetic and copies ran while one was open for 2% of the time, Pallas kernels for 20%

profile of v3, /device:TPU:1, one launch (start us, length us, event | category | flops | bytes accessed | tf_op | source)
XLA Modules:
  0.0 191.2 jit_solution(759821263188968318)
XLA Ops:
  0.6 1.0 dynamic-slice_bitcast_fusion.1
  1.6 11.5 %collective-permute-start = (bf16[2,64,512]{2,1,0:T(8,128)(2,1)S(1)}, bf16[2,64,512]{2,1,0:T(8,128)(2,1)S(1)}, u32[]{:S(2)}, u32[]{:S(2)}) collective-permute-start(bf16[2,64,512]{2,1,0:T(8,128)(2,1)S(1)} %pad_maximum_fusion), channel_id=1, source_target_pairs={{0,385},{1,384},{128,257},{129,256},{256,129},{257,128},{384,1},{3... | collective-permute-start | bytes 393224 | tf_op jit(solution)/shard_map/ppermute | solution.py:258
  13.3 6.4 %outgoing_rows.1 = (bf16[32,144,128]{2,1,0:T(8,128)(2,1)}, bf16[64,128]{1,0:T(8,128)(2,1)}) custom-call(bf16[1,64,4096]{2,1,0:T(8,128)(2,1)} %gate_a_ref, bf16[1,64,4096]{2,1,0:T(8,128)(2,1)} %cot_ref.2, s32[1,2,64,128]{3,2,1,0:T(8,128)} %slots_ref.5, f32[1,2,64,128]{3,2,1,0:T(8,128)} %weights_ref.3, s32[1,2,1,128]{3,2,1,0:T(1,128)} %ids_ref.1), custom_call_target="tpu_custom_call" | custom-call | tf_op jit(solution)/shard_map/outgoing_rows/pallas_call | solution.py:63
  19.9 3.1 %collective-permute-start.1 = (bf16[128,256]{1,0:T(8,128)(2,1)S(1)}, bf16[128,256]{1,0:T(8,128)(2,1)S(1)}, u32[]{:S(2)}, u32[]{:S(2)}) collective-permute-start(bf16[128,256]{1,0:T(8,128)(2,1)S(1)} %pad_maximum_fusion.1), channel_id=1, source_target_pairs={{0,16},{16,0},{32,48},{48,32},{1,17},{17,1},{33,49},{49,33},{2,18}... | collective-permute-start | bytes 196616 | tf_op jit(solution)/shard_map/ppermute | solution.py:275
  23.1 4.4 %collective-permute-start.2 = (bf16[128,256]{1,0:T(8,128)(2,1)S(1)}, bf16[128,256]{1,0:T(8,128)(2,1)S(1)}, u32[]{:S(2)}, u32[]{:S(2)}) collective-permute-start(bf16[128,256]{1,0:T(8,128)(2,1)S(1)} %pad_maximum_fusion.2), channel_id=1, source_target_pairs={{0,32},{16,48},{32,0},{48,16},{1,33},{17,49},{33,1},{49,17},{2,34}... | collective-permute-start | bytes 196616 | tf_op jit(solution)/shard_map/ppermute | solution.py:275
  27.4 2.1 %collective-permute-start.3 = (bf16[128,256]{1,0:T(8,128)(2,1)S(1)}, bf16[128,256]{1,0:T(8,128)(2,1)S(1)}, u32[]{:S(2)}, u32[]{:S(2)}) collective-permute-start(bf16[128,256]{1,0:T(8,128)(2,1)S(1)} %pad_maximum_fusion.3), channel_id=1, source_target_pairs={{0,48},{16,32},{32,16},{48,0},{1,49},{17,33},{33,17},{49,1},{2,50}... | collective-permute-start | bytes 196616 | tf_op jit(solution)/shard_map/ppermute | solution.py:275
  29.6 4.0 %collective-permute-done.3 = bf16[128,256]{1,0:T(8,128)(2,1)S(1)} collective-permute-done((bf16[128,256]{1,0:T(8,128)(2,1)S(1)}, bf16[128,256]{1,0:T(8,128)(2,1)S(1)}, u32[]{:S(2)}, u32[]{:S(2)}) %collective-permute-start.3) | collective-permute-done | bytes 65568 | tf_op jit(solution)/shard_map/ppermute | solution.py:275
  33.7 6.5 %all-to-all-start = ((bf16[32,144,128]{2,1,0:T(8,128)(2,1)}), bf16[32,144,128]{2,1,0:T(8,128)(2,1)S(1)}, u32[]{:S(2)}, u32[]{:S(2)}) async-start(bf16[32,144,128]{2,1,0:T(8,128)(2,1)} %get-tuple-element.29), calls=%async_computation | async-start | bytes 2359296 | tf_op jit(solution)/shard_map/all_to_all | solution.py:310
  40.2 5.8 %collective-permute-start.6 = (bf16[512,256]{1,0:T(8,128)(2,1)S(1)}, bf16[512,256]{1,0:T(8,128)(2,1)S(1)}, u32[]{:S(2)}, u32[]{:S(2)}) collective-permute-start(bf16[512,256]{1,0:T(8,128)(2,1)S(1)} %constant_dynamic-update-slice_fusion.refs_0_), channel_id=1, source_target_pairs={{0,14},{2,0},{4,2},{6,4},{8,6},{10,8},{12,10},{14,12},{1,15},{3,1}... | collective-permute-start | bytes 786440 | tf_op jit(solution)/shard_map/ppermute | solution.py:286
  46.0 1.9 %collective-permute-start.4 = (bf16[512,256]{1,0:T(8,128)(2,1)S(1)}, bf16[512,256]{1,0:T(8,128)(2,1)S(1)}, u32[]{:S(2)}, u32[]{:S(2)}) collective-permute-start(bf16[512,256]{1,0:T(8,128)(2,1)S(1)} %constant_dynamic-update-slice_fusion.refs_0_), channel_id=1, source_target_pairs={{0,2},{2,4},{4,6},{6,8},{8,10},{10,12},{12,14},{14,0},{1,3},{3,5},... | collective-permute-start | bytes 786440 | tf_op jit(solution)/shard_map/ppermute | solution.py:285
  47.9 12.8 %collective-permute-done.6.refs_2_ = bf16[512,256]{1,0:T(8,128)(2,1)S(1)} collective-permute-done((bf16[512,256]{1,0:T(8,128)(2,1)S(1)}, bf16[512,256]{1,0:T(8,128)(2,1)S(1)}, u32[]{:S(2)}, u32[]{:S(2)}) %collective-permute-start.6) | collective-permute-done | bytes 262176 | tf_op jit(solution)/shard_map/ppermute | solution.py:286
  60.7 3.7 %collective-permute-start.7 = (bf16[512,256]{1,0:T(8,128)(2,1)S(1)}, bf16[512,256]{1,0:T(8,128)(2,1)S(1)}, u32[]{:S(2)}, u32[]{:S(2)}) collective-permute-start(bf16[512,256]{1,0:T(8,128)(2,1)S(1)} %collective-permute-done.6.refs_2_), channel_id=1, source_target_pairs={{0,14},{2,0},{4,2},{6,4},{8,6},{10,8},{12,10},{14,12},{1,15},{3,1}... | collective-permute-start | bytes 786440 | tf_op jit(solution)/shard_map/ppermute | solution.py:286
  64.4 1.9 %collective-permute-start.5 = (bf16[512,256]{1,0:T(8,128)(2,1)S(1)}, bf16[512,256]{1,0:T(8,128)(2,1)S(1)}, u32[]{:S(2)}, u32[]{:S(2)}) collective-permute-start(bf16[512,256]{1,0:T(8,128)(2,1)S(1)} %collective-permute-done.4.refs_1_), channel_id=1, source_target_pairs={{0,2},{2,4},{4,6},{6,8},{8,10},{10,12},{12,14},{14,0},{1,3},{3,5},... | collective-permute-start | bytes 786440 | tf_op jit(solution)/shard_map/ppermute | solution.py:285
  66.3 3.2 %collective-permute-done.7.refs_4_ = bf16[512,256]{1,0:T(8,128)(2,1)S(1)} collective-permute-done((bf16[512,256]{1,0:T(8,128)(2,1)S(1)}, bf16[512,256]{1,0:T(8,128)(2,1)S(1)}, u32[]{:S(2)}, u32[]{:S(2)}) %collective-permute-start.7) | collective-permute-done | bytes 262176 | tf_op jit(solution)/shard_map/ppermute | solution.py:286
  69.5 4.6 %collective-permute-done.5.refs_3_ = bf16[512,256]{1,0:T(8,128)(2,1)S(1)} collective-permute-done((bf16[512,256]{1,0:T(8,128)(2,1)S(1)}, bf16[512,256]{1,0:T(8,128)(2,1)S(1)}, u32[]{:S(2)}, u32[]{:S(2)}) %collective-permute-start.5) | collective-permute-done | bytes 262176 | tf_op jit(solution)/shard_map/ppermute | solution.py:285
  74.1 1.9 collective-permute-start.8
  76.0 4.6 %collective-permute-start.9 = (bf16[512,256]{1,0:T(8,128)(2,1)S(1)}, bf16[512,256]{1,0:T(8,128)(2,1)S(1)}, u32[]{:S(2)}, u32[]{:S(2)}) collective-permute-start(bf16[512,256]{1,0:T(8,128)(2,1)S(1)} %collective-permute-done.7.refs_4_), channel_id=1, source_target_pairs={{0,14},{2,0},{4,2},{6,4},{8,6},{10,8},{12,10},{14,12},{1,15},{3,1}... | collective-permute-start | bytes 786440 | tf_op jit(solution)/shard_map/ppermute | solution.py:286
  80.9 11.9 %dense_rows.1 = bf16[4096,128]{1,0:T(8,128)(2,1)} custom-call(f32[32,128]{1,0:T(8,128)S(1)} %bitcast.43, bf16[32,144,128]{2,1,0:T(8,128)(2,1)S(1)} %all-to-all-done.rows_ref), custom_call_target="tpu_custom_call" | custom-call | tf_op jit(solution)/shard_map/dense_rows/pallas_call | solution.py:140
  92.9 10.6 %all-to-all-start.2 = ((bf16[64,64,128]{2,1,0:T(8,128)(2,1)}), bf16[64,64,128]{2,1,0:T(8,128)(2,1)S(1)}, u32[]{:S(2)}, u32[]{:S(2)}) async-start(bf16[64,64,128]{2,1,0:T(8,128)(2,1)} %bitcast.15), calls=%async_computation.2 | async-start | bytes 2097152 | tf_op jit(solution)/shard_map/all_to_all | solution.py:320
  103.9 2.9 %collective-permute-start.10 = (bf16[512,256]{1,0:T(8,128)(2,1)S(1)}, bf16[512,256]{1,0:T(8,128)(2,1)S(1)}, u32[]{:S(2)}, u32[]{:S(2)}) collective-permute-start(bf16[512,256]{1,0:T(8,128)(2,1)S(1)} %collective-permute-done.8.refs_5_), channel_id=1, source_target_pairs={{0,2},{2,4},{4,6},{6,8},{8,10},{10,12},{12,14},{14,0},{1,3},{3,5},... | collective-permute-start | bytes 786440 | tf_op jit(solution)/shard_map/ppermute | solution.py:285
  106.9 0.6 add_convert_fusion.place_ref
  108.1 24.9 %collective-permute-done.10.refs_7_ = bf16[512,256]{1,0:T(8,128)(2,1)S(1)} collective-permute-done((bf16[512,256]{1,0:T(8,128)(2,1)S(1)}, bf16[512,256]{1,0:T(8,128)(2,1)S(1)}, u32[]{:S(2)}, u32[]{:S(2)}) %collective-permute-start.10) | collective-permute-done | bytes 262176 | tf_op jit(solution)/shard_map/ppermute | solution.py:285
  133.0 0.7 copy-done.8
  133.7 14.7 %picked_rows.1 = bf16[16,256,256]{2,1,0:T(8,128)(2,1)} custom-call(f32[16,2,128]{2,1,0:T(2,128)} %dynamic-slice_bitcast_fusion.8.ids_ref, f32[8,512]{1,0:T(8,128)} %add_convert_fusion.place_ref, bf16[512,256]{1,0:T(8,128)(2,1)} %copy-done.1, bf16[512,256]{1,0:T(8,128)(2,1)} %copy-done.3, bf16[512,256]{1,0:T(8,128)(2,1)} %copy-done.2, ...), custom_call_target="tpu_custom_call" | custom-call | tf_op jit(solution)/shard_map/picked_rows/pallas_call | solution.py:175
  148.4 7.7 %all-to-all-start.1 = ((bf16[16,256,256]{2,1,0:T(8,128)(2,1)}), bf16[16,256,256]{2,1,0:T(8,128)(2,1)S(1)}, u32[]{:S(2)}, u32[]{:S(2)}) async-start(bf16[16,256,256]{2,1,0:T(8,128)(2,1)} %picked_rows.1), calls=%async_computation.1 | async-start | bytes 4194304 | tf_op jit(solution)/shard_map/all_to_all | solution.py:329
  156.3 3.4 %collective-permute-start.11 = (f32[2,2,64,128]{3,2,1,0:T(8,128)S(1)}, f32[2,2,64,128]{3,2,1,0:T(8,128)S(1)}, u32[]{:S(2)}, u32[]{:S(2)}) collective-permute-start(f32[2,2,64,128]{3,2,1,0:T(8,128)S(1)} %dynamic-slice_bitcast_fusion), channel_id=1, source_target_pairs={{0,256},{256,0},{1,257},{257,1},{2,258},{258,2},{3,259},{259,3},{4... | collective-permute-start | bytes 393224 | tf_op jit(solution)/shard_map/ppermute | solution.py:336
  159.6 5.3 %factors.1 = (f32[64,4096]{1,0:T(8,128)}, bf16[64,4096]{1,0:T(8,128)(2,1)}, f32[64,4096]{1,0:T(8,128)}, bf16[64,128]{1,0:T(8,128)(2,1)}) custom-call(bf16[1,64,4096]{2,1,0:T(8,128)(2,1)} %gate_a_ref, bf16[1,64,4096]{2,1,0:T(8,128)(2,1)} %cot_ref.2, bf16[1,64,4096]{2,1,0:T(8,128)(2,1)} %gate_b_ref, s32[1,2,64,128]{3,2,1,0:T(8,128)} %slots_ref.5, ...), custom_call_target="tpu_custom_call" | custom-call | tf_op jit(solution)/shard_map/factors/pallas_call | solution.py:102
  164.9 17.3 %collective-permute-done.11 = f32[2,2,64,128]{3,2,1,0:T(8,128)S(1)} collective-permute-done((f32[2,2,64,128]{3,2,1,0:T(8,128)S(1)}, f32[2,2,64,128]{3,2,1,0:T(8,128)S(1)}, u32[]{:S(2)}, u32[]{:S(2)}) %collective-permute-start.11) | collective-permute-done | bytes 131104 | tf_op jit(solution)/shard_map/ppermute | solution.py:336
  182.4 0.8 reshape.73
  183.1 2.1 %all-to-all-done.1.rows_ref = bf16[16,256,256]{2,1,0:T(8,128)(2,1)S(1)} async-done(((bf16[16,256,256]{2,1,0:T(8,128)(2,1)}), bf16[16,256,256]{2,1,0:T(8,128)(2,1)S(1)}, u32[]{:S(2)}, u32[]{:S(2)}) %all-to-all-start.1) | async-done | bytes 2097184 | tf_op jit(solution)/shard_map/all_to_all | solution.py:329
  185.2 1.3 copy-done
  186.6 4.6 %final_outputs.1 = (bf16[1,64,4096]{2,1,0:T(8,128)(2,1)}, bf16[1,64,4096]{2,1,0:T(8,128)(2,1)}, f32[1,64,128]{2,1,0:T(8,128)}) custom-call(bf16[16,256,256]{2,1,0:T(8,128)(2,1)} %copy-done, bf16[64,128]{1,0:T(8,128)(2,1)} %get-tuple-element.36.mix_a_ref, bf16[64,128]{1,0:T(8,128)(2,1)} %get-tuple-element.40.mix_b_ref, ...), custom_call_target="tpu_custom_call" | custom-call | tf_op jit(solution)/shard_map/final_outputs/pallas_call | solution.py:228
  (56 shorter events, 2.0 us)
Async XLA Ops:
  1.6 18.3 %collective-permute-start = (bf16[2,64,512]{2,1,0:T(8,128)(2,1)S(1)}, bf16[2,64,512]{2,1,0:T(8,128)(2,1)S(1)}, u32[]{:S(2)}, u32[]{:S(2)}) collective-permute-start(bf16[2,64,512]{2,1,0:T(8,128)(2,1)S(1)} %pad_maximum_fusion), channel_id=1, source_target_pairs={{0,385},{1,384},{128,257},{129,256},{256,129},{257,128},{384,1},{3... | collective-permute-start | bytes 393224 | tf_op jit(solution)/shard_map/ppermute | solution.py:258
  19.9 9.7 %collective-permute-start.1 = (bf16[128,256]{1,0:T(8,128)(2,1)S(1)}, bf16[128,256]{1,0:T(8,128)(2,1)S(1)}, u32[]{:S(2)}, u32[]{:S(2)}) collective-permute-start(bf16[128,256]{1,0:T(8,128)(2,1)S(1)} %pad_maximum_fusion.1), channel_id=1, source_target_pairs={{0,16},{16,0},{32,48},{48,32},{1,17},{17,1},{33,49},{49,33},{2,18}... | collective-permute-start | bytes 196616 | tf_op jit(solution)/shard_map/ppermute | solution.py:275
  23.1 6.5 %collective-permute-start.2 = (bf16[128,256]{1,0:T(8,128)(2,1)S(1)}, bf16[128,256]{1,0:T(8,128)(2,1)S(1)}, u32[]{:S(2)}, u32[]{:S(2)}) collective-permute-start(bf16[128,256]{1,0:T(8,128)(2,1)S(1)} %pad_maximum_fusion.2), channel_id=1, source_target_pairs={{0,32},{16,48},{32,0},{48,16},{1,33},{17,49},{33,1},{49,17},{2,34}... | collective-permute-start | bytes 196616 | tf_op jit(solution)/shard_map/ppermute | solution.py:275
  27.4 6.2 %collective-permute-start.3 = (bf16[128,256]{1,0:T(8,128)(2,1)S(1)}, bf16[128,256]{1,0:T(8,128)(2,1)S(1)}, u32[]{:S(2)}, u32[]{:S(2)}) collective-permute-start(bf16[128,256]{1,0:T(8,128)(2,1)S(1)} %pad_maximum_fusion.3), channel_id=1, source_target_pairs={{0,48},{16,32},{32,16},{48,0},{1,49},{17,33},{33,17},{49,1},{2,50}... | collective-permute-start | bytes 196616 | tf_op jit(solution)/shard_map/ppermute | solution.py:275
  33.7 59.1 %copy-start.1 = (bf16[512,256]{1,0:T(8,128)(2,1)}, bf16[512,256]{1,0:T(8,128)(2,1)S(1)}, u32[]{:S(2)}) copy-start(bf16[512,256]{1,0:T(8,128)(2,1)S(1)} %constant_dynamic-update-slice_fusion.refs_0_) | copy-start | bytes 786436
  33.7 40.4 %all-to-all-start = ((bf16[32,144,128]{2,1,0:T(8,128)(2,1)}), bf16[32,144,128]{2,1,0:T(8,128)(2,1)S(1)}, u32[]{:S(2)}, u32[]{:S(2)}) async-start(bf16[32,144,128]{2,1,0:T(8,128)(2,1)} %get-tuple-element.29), calls=%async_computation | async-start | bytes 2359296 | tf_op jit(solution)/shard_map/all_to_all | solution.py:310
  40.2 20.5 %collective-permute-start.6 = (bf16[512,256]{1,0:T(8,128)(2,1)S(1)}, bf16[512,256]{1,0:T(8,128)(2,1)S(1)}, u32[]{:S(2)}, u32[]{:S(2)}) collective-permute-start(bf16[512,256]{1,0:T(8,128)(2,1)S(1)} %constant_dynamic-update-slice_fusion.refs_0_), channel_id=1, source_target_pairs={{0,14},{2,0},{4,2},{6,4},{8,6},{10,8},{12,10},{14,12},{1,15},{3,1}... | collective-permute-start | bytes 786440 | tf_op jit(solution)/shard_map/ppermute | solution.py:286
  46.0 18.4 %collective-permute-start.4 = (bf16[512,256]{1,0:T(8,128)(2,1)S(1)}, bf16[512,256]{1,0:T(8,128)(2,1)S(1)}, u32[]{:S(2)}, u32[]{:S(2)}) collective-permute-start(bf16[512,256]{1,0:T(8,128)(2,1)S(1)} %constant_dynamic-update-slice_fusion.refs_0_), channel_id=1, source_target_pairs={{0,2},{2,4},{4,6},{6,8},{8,10},{10,12},{12,14},{14,0},{1,3},{3,5},... | collective-permute-start | bytes 786440 | tf_op jit(solution)/shard_map/ppermute | solution.py:285
  60.7 32.2 %copy-start.2 = (bf16[512,256]{1,0:T(8,128)(2,1)}, bf16[512,256]{1,0:T(8,128)(2,1)S(1)}, u32[]{:S(2)}) copy-start(bf16[512,256]{1,0:T(8,128)(2,1)S(1)} %collective-permute-done.6.refs_2_) | copy-start | bytes 786436
  60.7 8.8 %collective-permute-start.7 = (bf16[512,256]{1,0:T(8,128)(2,1)S(1)}, bf16[512,256]{1,0:T(8,128)(2,1)S(1)}, u32[]{:S(2)}, u32[]{:S(2)}) collective-permute-start(bf16[512,256]{1,0:T(8,128)(2,1)S(1)} %collective-permute-done.6.refs_2_), channel_id=1, source_target_pairs={{0,14},{2,0},{4,2},{6,4},{8,6},{10,8},{12,10},{14,12},{1,15},{3,1}... | collective-permute-start | bytes 786440 | tf_op jit(solution)/shard_map/ppermute | solution.py:286
  64.3 28.5 %copy-start.3 = (bf16[512,256]{1,0:T(8,128)(2,1)}, bf16[512,256]{1,0:T(8,128)(2,1)S(1)}, u32[]{:S(2)}) copy-start(bf16[512,256]{1,0:T(8,128)(2,1)S(1)} %collective-permute-done.4.refs_1_) | copy-start | bytes 786436
  64.4 9.8 %collective-permute-start.5 = (bf16[512,256]{1,0:T(8,128)(2,1)S(1)}, bf16[512,256]{1,0:T(8,128)(2,1)S(1)}, u32[]{:S(2)}, u32[]{:S(2)}) collective-permute-start(bf16[512,256]{1,0:T(8,128)(2,1)S(1)} %collective-permute-done.4.refs_1_), channel_id=1, source_target_pairs={{0,2},{2,4},{4,6},{6,8},{8,10},{10,12},{12,14},{14,0},{1,3},{3,5},... | collective-permute-start | bytes 786440 | tf_op jit(solution)/shard_map/ppermute | solution.py:285
  69.5 23.4 %copy-start.4 = (bf16[512,256]{1,0:T(8,128)(2,1)}, bf16[512,256]{1,0:T(8,128)(2,1)S(1)}, u32[]{:S(2)}) copy-start(bf16[512,256]{1,0:T(8,128)(2,1)S(1)} %collective-permute-done.7.refs_4_) | copy-start | bytes 786436
  74.1 18.8 %copy-start.5 = (bf16[512,256]{1,0:T(8,128)(2,1)}, bf16[512,256]{1,0:T(8,128)(2,1)S(1)}, u32[]{:S(2)}) copy-start(bf16[512,256]{1,0:T(8,128)(2,1)S(1)} %collective-permute-done.5.refs_3_) | copy-start | bytes 786436
  74.1 18.7 %collective-permute-start.8 = (bf16[512,256]{1,0:T(8,128)(2,1)S(1)}, bf16[512,256]{1,0:T(8,128)(2,1)S(1)}, u32[]{:S(2)}, u32[]{:S(2)}) collective-permute-start(bf16[512,256]{1,0:T(8,128)(2,1)S(1)} %collective-permute-done.5.refs_3_), channel_id=1, source_target_pairs={{0,2},{2,4},{4,6},{6,8},{8,10},{10,12},{12,14},{14,0},{1,3},{3,5},... | collective-permute-start | bytes 786440 | tf_op jit(solution)/shard_map/ppermute | solution.py:285
  76.0 16.8 %collective-permute-start.9 = (bf16[512,256]{1,0:T(8,128)(2,1)S(1)}, bf16[512,256]{1,0:T(8,128)(2,1)S(1)}, u32[]{:S(2)}, u32[]{:S(2)}) collective-permute-start(bf16[512,256]{1,0:T(8,128)(2,1)S(1)} %collective-permute-done.7.refs_4_), channel_id=1, source_target_pairs={{0,14},{2,0},{4,2},{6,4},{8,6},{10,8},{12,10},{14,12},{1,15},{3,1}... | collective-permute-start | bytes 786440 | tf_op jit(solution)/shard_map/ppermute | solution.py:286
  80.9 22.6 %copy-start.9 = (s32[8]{0:T(128)S(1)}, s32[8]{0:T(128)}, u32[]{:S(2)}) copy-start(s32[8]{0:T(128)} %constant.143.clone) | copy-start | bytes 100
  92.8 40.1 %copy-start.6 = (bf16[512,256]{1,0:T(8,128)(2,1)}, bf16[512,256]{1,0:T(8,128)(2,1)S(1)}, u32[]{:S(2)}) copy-start(bf16[512,256]{1,0:T(8,128)(2,1)S(1)} %collective-permute-done.8.refs_5_) | copy-start | bytes 786436
  92.8 40.1 %copy-start.7 = (bf16[512,256]{1,0:T(8,128)(2,1)}, bf16[512,256]{1,0:T(8,128)(2,1)S(1)}, u32[]{:S(2)}) copy-start(bf16[512,256]{1,0:T(8,128)(2,1)S(1)} %collective-permute-done.9.refs_6_) | copy-start | bytes 786436
  92.9 55.5 %all-to-all-start.2 = ((bf16[64,64,128]{2,1,0:T(8,128)(2,1)}), bf16[64,64,128]{2,1,0:T(8,128)(2,1)S(1)}, u32[]{:S(2)}, u32[]{:S(2)}) async-start(bf16[64,64,128]{2,1,0:T(8,128)(2,1)} %bitcast.15), calls=%async_computation.2 | async-start | bytes 2097152 | tf_op jit(solution)/shard_map/all_to_all | solution.py:320
  103.9 29.0 %collective-permute-start.10 = (bf16[512,256]{1,0:T(8,128)(2,1)S(1)}, bf16[512,256]{1,0:T(8,128)(2,1)S(1)}, u32[]{:S(2)}, u32[]{:S(2)}) collective-permute-start(bf16[512,256]{1,0:T(8,128)(2,1)S(1)} %collective-permute-done.8.refs_5_), channel_id=1, source_target_pairs={{0,2},{2,4},{4,6},{6,8},{8,10},{10,12},{12,14},{14,0},{1,3},{3,5},... | collective-permute-start | bytes 786440 | tf_op jit(solution)/shard_map/ppermute | solution.py:285
  133.0 0.7 copy-start.8
  148.4 36.9 %all-to-all-start.1 = ((bf16[16,256,256]{2,1,0:T(8,128)(2,1)}), bf16[16,256,256]{2,1,0:T(8,128)(2,1)S(1)}, u32[]{:S(2)}, u32[]{:S(2)}) async-start(bf16[16,256,256]{2,1,0:T(8,128)(2,1)} %picked_rows.1), calls=%async_computation.1 | async-start | bytes 4194304 | tf_op jit(solution)/shard_map/all_to_all | solution.py:329
  156.3 26.0 %collective-permute-start.11 = (f32[2,2,64,128]{3,2,1,0:T(8,128)S(1)}, f32[2,2,64,128]{3,2,1,0:T(8,128)S(1)}, u32[]{:S(2)}, u32[]{:S(2)}) collective-permute-start(f32[2,2,64,128]{3,2,1,0:T(8,128)S(1)} %dynamic-slice_bitcast_fusion), channel_id=1, source_target_pairs={{0,256},{256,0},{1,257},{257,1},{2,258},{258,2},{3,259},{259,3},{4... | collective-permute-start | bytes 393224 | tf_op jit(solution)/shard_map/ppermute | solution.py:336
  185.2 1.3 copy-start

commit v4 on v2

--- a/solution.py
+++ b/solution.py
@@ -15,6 +15,7 @@
 F32 = jnp.float32
 BF16 = jnp.bfloat16
 VMEM = pltpu.CompilerParams(vmem_limit_bytes=40 * 1024 * 1024)
+MOST_VMEM = pltpu.CompilerParams(vmem_limit_bytes=60 * 1024 * 1024)
 
 
 def gated(gate, incoming):
@@ -31,67 +32,67 @@
     return total.astype(BF16)
 
 
-def outgoing_kernel(gate_ref, cot_ref, slots_ref, weights_ref, ids_ref, out_ref, mix_ref):
-    listed = mix_ref.shape[1]
-
-    @pl.when(pl.program_id(0) == 0)
-    def _():
-        mix_ref[...] = mixing_of(slots_ref[0, 0], weights_ref[0, 0])
-
+def mixing_kernel(slots_ref, weights_ref, out_ref):
+    out_ref[0] = mixing_of(slots_ref[0, 0], weights_ref[0, 0])
+
+
+def mixing(slots, weights):
+    tokens, listed = slots.shape[2:]
+    picks = pl.BlockSpec((1, 1, tokens, listed), lambda c: (0, c, 0, 0))
+    return pl.pallas_call(
+        mixing_kernel,
+        grid=(2,),
+        in_specs=[picks, picks],
+        out_specs=pl.BlockSpec((1, tokens, listed), lambda c: (c, 0, 0)),
+        out_shape=jax.ShapeDtypeStruct((2, tokens, listed), BF16),
+        compiler_params=MOST_VMEM,
+        name="mixing",
+    )(slots, weights)
+
+
+def outgoing_kernel(gate_ref, cot_ref, mix_ref, ids_ref, own_ref, other_ref, out_ref):
+    listed = mix_ref.shape[2]
     g, sig, inc = gated(gate_ref[0], cot_ref[0])
     grad_memory = (inc * g * sig).astype(BF16)
     rows = lax.dot_general(
-        mix_ref[...], grad_memory, (((0,), (0,)), ((), ())), preferred_element_type=F32
+        mix_ref[0], grad_memory, (((0,), (0,)), ((), ())), preferred_element_type=F32
     ).astype(BF16)
     ids = [ids_ref[0, c] for c in range(2)]
     codes = jnp.concatenate(
         [part for i in ids for part in (i // ROWS_DEV, i % ROWS_DEV)] + [jnp.zeros((12, listed), jnp.int32)]
     )
     codes = codes.astype(F32).astype(BF16)
+    table = jnp.concatenate([own_ref[...], other_ref[...]])
+    held = table.shape[0]
     for k in range(out_ref.shape[0]):
+        at = (k // 2) * 256
         out_ref[k, :listed, :] = rows[:, k * 128 : (k + 1) * 128]
-        out_ref[k, listed:, :] = codes
-
-
-def outgoing(gate, cot, slots, weights, row_ids, features):
+        out_ref[k, listed : listed + 16, :] = codes
+        out_ref[k, listed + 16 : listed + 16 + held, :] = table[:, at : at + 128]
+        out_ref[k, listed + 16 + held :, :] = table[:, at + 128 : at + 256]
+
+
+def outgoing(gate, cot, mix, row_ids, own, other, features):
     _, tokens, width = gate.shape
-    listed = row_ids.shape[-1]
+    listed, held = row_ids.shape[-1], own.shape[0]
     chunks, step = width // features, 8
     part = pl.BlockSpec((1, tokens, step * features), lambda i: (0, 0, i))
-    picks = pl.BlockSpec((1, 1, tokens, listed), lambda i: (0, 0, 0, 0))
+    rows = pl.BlockSpec((held, step * features), lambda i: (0, i))
+    height = listed + 16 + 4 * held
     return pl.pallas_call(
         outgoing_kernel,
         grid=(chunks // step,),
-        in_specs=[part, part, picks, picks, pl.BlockSpec(row_ids.shape, lambda i: (0, 0, 0, 0))],
-        out_specs=[
-            pl.BlockSpec((step, listed + 16, features), lambda i: (i, 0, 0)),
-            pl.BlockSpec((tokens, listed), lambda i: (0, 0)),
+        in_specs=[
+            part, part,
+            pl.BlockSpec((1, tokens, listed), lambda i: (0, 0, 0)),
+            pl.BlockSpec(row_ids.shape, lambda i: (0, 0, 0, 0)),
+            rows, rows,
         ],
-        out_shape=[
-            jax.ShapeDtypeStruct((chunks, listed + 16, features), BF16),
-            jax.ShapeDtypeStruct((tokens, listed), BF16),
-        ],
-        compiler_params=VMEM,
+        out_specs=pl.BlockSpec((step, height, features), lambda i: (i, 0, 0)),
+        out_shape=jax.ShapeDtypeStruct((chunks, height, features), BF16),
+        compiler_params=MOST_VMEM,
         name="outgoing_rows",
-    )(gate, cot, slots, weights, row_ids)
-
-
-def mixing_kernel(slots_ref, weights_ref, out_ref):
-    out_ref[...] = mixing_of(slots_ref[0, 0], weights_ref[0, 0])
-
-
-def mixing_b(slots, weights):
-    tokens, listed = slots.shape[2:]
-    picks = pl.BlockSpec((1, 1, tokens, listed), lambda i: (0, 1, 0, 0))
-    return pl.pallas_call(
-        mixing_kernel,
-        grid=(1,),
-        in_specs=[picks, picks],
-        out_specs=pl.BlockSpec((tokens, listed), lambda i: (0, 0)),
-        out_shape=jax.ShapeDtypeStruct((tokens, listed), BF16),
-        compiler_params=VMEM,
-        name="mixing_b",
-    )(slots, weights)
+    )(gate, cot, mix, row_ids, own, other)
 
 
 def dense_kernel(ids_ref, rows_ref, out_ref):
@@ -170,7 +171,7 @@
     rows_ref, mix_a_ref, mix_b_ref, gate_a_ref, cot_ref, gate_b_ref, slots_ref,
     mixed_ref, grad_gate_ref, grad_weights_ref, scores_ref,
 ):
-    listed = mix_a_ref.shape[1]
+    listed = mix_a_ref.shape[2]
     step, _, features = rows_ref.shape
 
     @pl.when(pl.program_id(0) == 0)
@@ -182,10 +183,10 @@
         at = slice(k * features, (k + 1) * features)
         fetched_a = rows_ref[k, :listed, :]
         fetched_b = rows_ref[k, listed:, :]
-        memory_b = jnp.dot(mix_b_ref[...], fetched_b, preferred_element_type=F32)
+        memory_b = jnp.dot(mix_b_ref[0], fetched_b, preferred_element_type=F32)
         gb = gate_b_ref[0, :, at].astype(F32)
         mixed_ref[0, :, at] = (gb / (1.0 + jnp.exp(-gb)) * memory_b).astype(BF16)
-        memory_a = jnp.dot(mix_a_ref[...], fetched_a, preferred_element_type=F32)
+        memory_a = jnp.dot(mix_a_ref[0], fetched_a, preferred_element_type=F32)
         g, sig, inc = gated(gate_a_ref[0, :, at], cot_ref[0, :, at])
         grad_gate_ref[0, :, at] = (inc * memory_a * sig * (1.0 + g * (1.0 - sig))).astype(BF16)
         grad_memory = (inc * g * sig).astype(BF16)
@@ -199,19 +200,20 @@
         grad_weights_ref[0] = jnp.take_along_axis(scores_ref[...], slots_ref[0, 0], axis=1)
 
 
-def final_outputs(fetched, mix_a, mix_b, gate_a, cot, gate_b, slots):
+def final_outputs(fetched, mix, gate_a, cot, gate_b, slots):
     chunks, rows, features = fetched.shape
     _, tokens, width = gate_a.shape
-    listed = mix_a.shape[1]
+    listed = mix.shape[-1]
     step = 4
-    whole = pl.BlockSpec((tokens, listed), lambda i: (0, 0))
     part = pl.BlockSpec((1, tokens, step * features), lambda i: (0, 0, i))
     return pl.pallas_call(
         final_kernel,
         grid=(chunks // step,),
         in_specs=[
             pl.BlockSpec((step, rows, features), lambda i: (i, 0, 0)),
-            whole, whole, part, part, part,
+            pl.BlockSpec((1, tokens, listed), lambda i: (0, 0, 0)),
+            pl.BlockSpec((1, tokens, listed), lambda i: (1, 0, 0)),
+            part, part, part,
             pl.BlockSpec((1, 1, tokens, listed), lambda i: (0, 0, 0, 0)),
         ],
         out_specs=[part, part, pl.BlockSpec((1, tokens, listed), lambda i: (0, 0, 0))],
@@ -223,48 +225,43 @@
         scratch_shapes=[pltpu.VMEM((tokens, listed), F32)],
         compiler_params=VMEM,
         name="final_outputs",
-    )(fetched, mix_a, mix_b, gate_a, cot, gate_b, slots)
-
-
-def both_halves(table):
-    rows_dev, width = table.shape
-    cut = table.reshape(rows_dev, 2, 4, 2, -1)
-    cut = lax.dynamic_index_in_dim(cut, lax.axis_index(("zl0", "c")), 2, keepdims=False)
-    cut = jnp.transpose(cut.reshape(rows_dev, 4, -1), (1, 0, 2))
-    return cut, lax.ppermute(cut, "zh", [(0, 1), (1, 0)])
-
-
-def across_x(own, other):
-    at_x = lax.axis_index(("x1", "x0"))
-    mine = []
-    for k in range(4):
-        part = jnp.concatenate(
-            [lax.dynamic_index_in_dim(h, at_x ^ k, 0, keepdims=False) for h in (own, other)]
-        )
-        if k:
-            part = lax.ppermute(part, ("x1", "x0"), [(i, i ^ k) for i in range(4)])
-        mine.append(part)
-    return jnp.concatenate(mine)
-
-
-def ring_step(forward, backward):
+    )(fetched, mix, mix, gate_a, cot, gate_b, slots)
+
+
+def quarters(table):
+    rows = table.shape[0] // 4
+    zl0, core = lax.axis_index("zl0"), lax.axis_index("c")
+
+    def quarter(z):
+        return lax.dynamic_slice_in_dim(table, (z * 2 + core) * rows, rows, 0)
+
+    mirrored = [(i, 7 - i) for i in range(8)]
+    return quarter(zl0), lax.ppermute(quarter(1 - zl0), ("zl1", "zl0", "zh"), mirrored)
+
+
+def along_y(block, inner):
     n_y = lax.axis_size(RING)
-    ahead = [(i, (i + 1) % n_y) for i in range(n_y)]
-    back = [(i, (i - 1) % n_y) for i in range(n_y)]
-    return (
-        lax.ppermute(forward, RING, ahead),
-        None if backward is None else lax.ppermute(backward, RING, back),
-    )
-
-
-def block_places(rows_dev, offsets):
-    n_y = lax.axis_size(RING)
-    xs = lax.axis_index(("x1", "x0")) ^ jnp.arange(4, dtype=jnp.int32)
-    zs = lax.axis_index("zh") ^ jnp.arange(2, dtype=jnp.int32)
-    ys = (lax.axis_index(RING) + jnp.array(offsets, jnp.int32)) & (n_y - 1)
-    holder = (xs[None, :, None] * n_y + ys[:, None, None]) * 2 + zs[None, None, :]
-    places = holder[..., None] * rows_dev + jnp.arange(rows_dev, dtype=jnp.int32)
-    return places.reshape(len(offsets), -1).astype(F32)
+    if inner:
+        pairs = [(i, i ^ 1) for i in range(n_y)]
+    else:
+        pairs = [(i, (i + 1) % n_y if i % 2 else (i - 1) % n_y) for i in range(n_y)]
+    return lax.ppermute(block, RING, pairs)
+
+
+def block_places(members, held):
+    n_x, n_pairs = 4, lax.axis_size("y1")
+    y0, pair = lax.axis_index("y0"), lax.axis_index("y1")
+    turn = 2 * y0 - 1
+    pairs = (pair + jnp.stack([jnp.zeros_like(turn), turn, -turn, 2 * jnp.ones_like(turn)])) & (n_pairs - 1)
+    member = jnp.arange(members, dtype=jnp.int32)
+    x = (member >> 4) * 2 + ((member >> 1) & 1)
+    quarter, y_low = (member >> 2) & 3, member & 1
+    zh = lax.axis_index("zh") ^ jnp.arange(2, dtype=jnp.int32)
+    y = pairs[:, None] * 2 + y_low[None, :]
+    holder = (x[None, :, None] * (2 * n_pairs) + y[:, :, None]) * 2 + zh[None, None, :]
+    row = holder * ROWS_DEV + (quarter * held)[None, :, None]
+    places = row[..., None] + jnp.arange(held, dtype=jnp.int32)
+    return places.reshape(n_pairs, -1).astype(F32)
 
 
 def local(gate_a, cotangent_a, gate_b, table, row_ids, slots, weights):
@@ -272,29 +269,32 @@
     owners = lax.axis_size(TABLE)
     listed = row_ids.shape[-1]
 
-    own, other = both_halves(table)
-    sent, mix_a = outgoing(gate_a, cotangent_a, slots, weights, row_ids, 128)
-    sent, own, other = lax.optimization_barrier((sent, own, other))
+    own, other = quarters(table)
+    mix = mixing(slots, weights)
+    mix, other = lax.optimization_barrier((mix, other))
+    sent = outgoing(gate_a, cotangent_a, mix, row_ids, own, other, 128)
     received = lax.all_to_all(sent, GRAD_GROUP, split_axis=0, concat_axis=0, tiled=True)
-    block = across_x(own, other)
-    received, block = lax.optimization_barrier((received, block))
-
+
+    members, held = received.shape[0], own.shape[0]
+    first = listed + 16
+    halves = [
+        received[:, at : at + 2 * held].reshape(members * 2 * held, -1) for at in (first, first + 2 * held)
+    ]
+    block = jnp.concatenate(halves, axis=1)
     codes = received[:, listed : listed + 4, :].astype(F32)
     ids = codes[:, 0::2] * ROWS_DEV + codes[:, 1::2]
     dense = dense_rows(ids[:, 0], received, owners * rows_dev)
-    f1, b1 = ring_step(block, block)
-    dense, f1, b1 = lax.optimization_barrier((dense, f1, b1))
+    next_1 = along_y(block, False)
+    dense, next_1 = lax.optimization_barrier((dense, next_1))
     arrived = lax.all_to_all(
         dense.reshape(owners, rows_dev, -1), TABLE, split_axis=0, concat_axis=0, tiled=True
     )
-    f2, b2 = ring_step(f1, b1)
-    f3, b3 = ring_step(f2, b2)
-    f4, _ = ring_step(f3, None)
+    next_2 = along_y(next_1, True)
+    next_3 = along_y(next_2, False)
 
     near = ids.reshape(-1, 2, 2, listed)
     near = lax.dynamic_index_in_dim(near, lax.axis_index("y0"), 1, keepdims=False)
-    places = block_places(rows_dev, (0, -1, 1, -2, 2, -3, 3, -4))
-    picked = picked_rows(near, places, (block, f1, b1, f2, b2, f3, b3, f4))
+    picked = picked_rows(near, block_places(members, held), (block, next_1, next_2, next_3))
     fetched = lax.all_to_all(picked, ROW_GROUP, split_axis=0, concat_axis=0, tiled=True)
 
     features = arrived.shape[-1]
@@ -305,10 +305,7 @@
     total = kept + lax.ppermute(given, "zl1", [(0, 1), (1, 0)])
     grad_table = jnp.transpose(total, (2, 0, 1, 3)).reshape(rows_dev, -1)
 
-    mix_b = mixing_b(slots, weights)
-    mixed, grad_gate, grad_weights = final_outputs(
-        fetched, mix_a, mix_b, gate_a, cotangent_a, gate_b, slots
-    )
+    mixed, grad_gate, grad_weights = final_outputs(fetched, mix, gate_a, cotangent_a, gate_b, slots)
     return mixed, grad_gate, grad_weights, grad_table
 
 

time: 184 us -> 185 us (level)
  blocking collectives: 0 us -> 28.6 us
  starting transfers between devices: 72 us -> 45.3 us
  local copies, waits for them, and re-layouts: 12.2 us -> 6.76 us
  Pallas kernels: 33.7 us -> 37.5 us
    all_to_all x0 -> x1, blocking collectives: none -> 28.6 us  [local(): lax.all_to_all(sent, GRAD_GROUP, split_axis=0, concat_axis=0, tiled=True)]
    ppermute x11 -> x4, starting transfers between devices: 42.1 us -> 24.5 us  [the longest x3 13 us: along_y(): return lax.ppermute(block, RING, pairs)]
    all_to_all x1 -> x0, starting transfers between devices: 7.33 us -> none  [local(): lax.all_to_all(sent, GRAD_GROUP, split_axis=0, concat_axis=0, tiled=True)]
    unnamed x32 -> x14, local copies, waits for them, and re-layouts: 8.57 us -> 2.68 us
    pallas_call x1, Pallas kernels: 2.43 us -> 6.28 us  [mixing(): pl.pallas_call(mixing_kernel, grid=(2,), in_specs=[picks, picks], out_spe...]
    all_to_all x1, starting transfers between devices: 10.1 us -> 7.29 us  [local(): lax.all_to_all(dense.reshape(owners, rows_dev, -1), TABLE, split_axis=0,...]
    ppermute x1, starting transfers between devices: 3.03 us -> 4.93 us  [local(): total = kept + lax.ppermute(given, 'zl1', [(0, 1), (1, 0)])]
    ppermute x11 -> x4, waiting for transfers between devices: 42.2 us -> 41.6 us  [the longest x3 41.1 us: along_y(): return lax.ppermute(block, RING, pairs)]
  transfers between devices with their start and end apart: 15 -> 7, of which waited for: 7 -> 5; matrix products, arithmetic and copies ran while one was open for 3% -> 3% of each run, Pallas kernels for 17% -> 17%
where the time goes in v4:
time: 185 us; the launch traced here: 184 us
  waiting for transfers between devices  61.8 us (33%)
  starting transfers between devices  45.3 us (24%)
  Pallas kernels  37.5 us (20%)
  blocking collectives  28.6 us (15%)
  local copies, waits for them, and re-layouts  6.76 us (4%)
  other arithmetic  2.77 us (1%)
    ppermute x3, waiting for transfers between devices, along_y(): return lax.ppermute(block, RING, pairs)  41.1 us
    all_to_all x1, blocking collectives, local(): lax.all_to_all(sent, GRAD_GROUP, split_axis=0, concat_axis=0, tiled=True)  28.6 us
    ppermute x1, waiting for transfers between devices, local(): total = kept + lax.ppermute(given, 'zl1', [(0, 1), (1, 0)])  19.1 us
    ppermute x3, starting transfers between devices, along_y(): return lax.ppermute(block, RING, pairs)  13 us
    pallas_call x1, Pallas kernels, picked_rows(): pl.pallas_call(pick_kernel, grid=(members,), in_specs=[pl.BlockSpec((1, l...  12.8 us
    pallas_call x1, Pallas kernels, dense_rows(): pl.pallas_call(dense_kernel, grid=(rows // tile,), in_specs=[pl.BlockSpec...  11.9 us
    ppermute x1, starting transfers between devices, quarters(): lax.ppermute(quarter(1 - zl0), ('zl1', 'zl0', 'zh'), mirrored)  11.5 us
    all_to_all x1, starting transfers between devices, local(): lax.all_to_all(picked, ROW_GROUP, split_axis=0, concat_axis=0, tiled=True)  8.56 us
  transfers between devices with their start and end apart: 7, of which 5 were waited for; matrix products, arithmetic and copies ran while one was open for 3% of the time, Pallas kernels for 17%

profile of v4, /device:TPU:1, one launch (start us, length us, event | category | flops | bytes accessed | tf_op | source)
XLA Modules:
  0.0 183.6 jit_solution(7451988413430444870)
XLA Ops:
  0.6 1.6 constant_dynamic-slice_fusion
  2.3 11.5 %collective-permute-start = (bf16[16,4096]{1,0:T(8,128)(2,1)S(1)}, bf16[16,4096]{1,0:T(8,128)(2,1)S(1)}, u32[]{:S(2)}, u32[]{:S(2)}) collective-permute-start(bf16[16,4096]{1,0:T(8,128)(2,1)S(1)} %get-tuple-element.21), channel_id=1, source_target_pairs={{0,385},{1,384},{128,257},{129,256},{256,129},{257,128},{384,1},{3... | collective-permute-start | bytes 393224 | tf_op jit(solution)/shard_map/ppermute | solution.py:239
  13.8 6.3 %mixing.1.mix_ref.mix_a_ref.mix_b_ref = bf16[2,64,128]{2,1,0:T(8,128)(2,1)} custom-call(s32[1,2,64,128]{3,2,1,0:T(8,128)} %slots_ref.3, f32[1,2,64,128]{3,2,1,0:T(8,128)} %weights_ref.1), custom_call_target="tpu_custom_call" | custom-call | tf_op jit(solution)/shard_map/mixing/pallas_call | solution.py:42
  20.1 0.5 collective-permute-done.other_ref
  20.5 0.7 copy-done.6
  21.2 4.0 %outgoing_rows.1 = bf16[32,208,128]{2,1,0:T(8,128)(2,1)} custom-call(bf16[1,64,4096]{2,1,0:T(8,128)(2,1)} %gate_a_ref.1, bf16[1,64,4096]{2,1,0:T(8,128)(2,1)} %cot_ref.3, bf16[2,64,128]{2,1,0:T(8,128)(2,1)} %mixing.1.mix_ref.mix_a_ref.mix_b_ref, s32[1,2,1,128]{3,2,1,0:T(1,128)} %ids_ref.1, bf16[16,4096]{1,0:T(8,128)(2,1)} %get-tuple-element.20.own_ref, ...), custom_call_target="tpu_custom_call" | custom-call | tf_op jit(solution)/shard_map/outgoing_rows/pallas_call | solution.py:82
  25.2 28.6 %all_to_all.15.rows_ref = bf16[32,208,128]{2,1,0:T(8,128)(2,1)S(1)} all-to-all(bf16[32,208,128]{2,1,0:T(8,128)(2,1)} %outgoing_rows.1), channel_id=1, replica_groups=mesh['zl1'=2,'zl0'=2,'c'=2,'x1'=2,'x0'=2,'y1'=4,'y0'=2,'zh'=2] {'x1','zl..., dimensions={0} | all-to-all | bytes 3407872 | tf_op jit(solution)/shard_map/all_to_all | solution.py:276
  54.0 6.1 %collective-permute-start.1 = (bf16[1024,256]{1,0:T(8,128)(2,1)S(1)}, bf16[1024,256]{1,0:T(8,128)(2,1)S(1)}, u32[]{:S(2)}, u32[]{:S(2)}) collective-permute-start(bf16[1024,256]{1,0:T(8,128)(2,1)S(1)} %pad_maximum_fusion.refs_0_), channel_id=1, source_target_pairs={{0,14},{2,4},{4,2},{6,8},{8,6},{10,12},{12,10},{14,0},{1,15},{3,5}... | collective-permute-start | bytes 1572872 | tf_op jit(solution)/shard_map/ppermute | solution.py:248
  60.1 0.1 slice.20
  60.2 0.1 slice.19
  60.4 11.9 %dense_rows.1 = bf16[4096,128]{1,0:T(8,128)(2,1)} custom-call(f32[32,128]{1,0:T(8,128)S(1)} %bitcast.21, bf16[32,208,128]{2,1,0:T(8,128)(2,1)S(1)} %all_to_all.15.rows_ref), custom_call_target="tpu_custom_call" | custom-call | tf_op jit(solution)/shard_map/dense_rows/pallas_call | solution.py:120
  72.3 7.3 %all-to-all-start.2 = ((bf16[64,64,128]{2,1,0:T(8,128)(2,1)}), bf16[64,64,128]{2,1,0:T(8,128)(2,1)S(1)}, u32[]{:S(2)}, u32[]{:S(2)}) async-start(bf16[64,64,128]{2,1,0:T(8,128)(2,1)} %bitcast.7), calls=%async_computation.2 | async-start | bytes 2097152 | tf_op jit(solution)/shard_map/all_to_all | solution.py:289
  79.7 2.9 %collective-permute-start.2 = (bf16[1024,256]{1,0:T(8,128)(2,1)S(1)}, bf16[1024,256]{1,0:T(8,128)(2,1)S(1)}, u32[]{:S(2)}, u32[]{:S(2)}) collective-permute-start(bf16[1024,256]{1,0:T(8,128)(2,1)S(1)} %collective-permute-done.1.refs_1_), channel_id=1, source_target_pairs={{0,2},{2,0},{4,6},{6,4},{8,10},{10,8},{12,14},{14,12},{1,3},{3,1},... | collective-permute-start | bytes 1572872 | tf_op jit(solution)/shard_map/ppermute | solution.py:248
  82.8 31.1 %collective-permute-done.2.refs_2_ = bf16[1024,256]{1,0:T(8,128)(2,1)S(1)} collective-permute-done((bf16[1024,256]{1,0:T(8,128)(2,1)S(1)}, bf16[1024,256]{1,0:T(8,128)(2,1)S(1)}, u32[]{:S(2)}, u32[]{:S(2)}) %collective-permute-start.2) | collective-permute-done | bytes 524320 | tf_op jit(solution)/shard_map/ppermute | solution.py:248
  113.9 3.9 %collective-permute-start.3 = (bf16[1024,256]{1,0:T(8,128)(2,1)S(1)}, bf16[1024,256]{1,0:T(8,128)(2,1)S(1)}, u32[]{:S(2)}, u32[]{:S(2)}) collective-permute-start(bf16[1024,256]{1,0:T(8,128)(2,1)S(1)} %collective-permute-done.2.refs_2_), channel_id=1, source_target_pairs={{0,14},{2,4},{4,2},{6,8},{8,6},{10,12},{12,10},{14,0},{1,15},{3,5}... | collective-permute-start | bytes 1572872 | tf_op jit(solution)/shard_map/ppermute | solution.py:248
  117.9 0.1 copy.18
  118.0 0.2 add.146
  118.2 0.2 add.147
  118.5 10.0 %collective-permute-done.3.refs_3_ = bf16[1024,256]{1,0:T(8,128)(2,1)S(1)} collective-permute-done((bf16[1024,256]{1,0:T(8,128)(2,1)S(1)}, bf16[1024,256]{1,0:T(8,128)(2,1)S(1)}, u32[]{:S(2)}, u32[]{:S(2)}) %collective-permute-start.3) | collective-permute-done | bytes 524320 | tf_op jit(solution)/shard_map/ppermute | solution.py:248
  128.5 12.8 %picked_rows.1 = bf16[16,256,256]{2,1,0:T(8,128)(2,1)} custom-call(f32[16,2,128]{2,1,0:T(2,128)S(1)} %dynamic-slice_bitcast_fusion.1.ids_ref, f32[4,1024]{1,0:T(4,128)S(1)} %add_convert_fusion.place_ref, bf16[1024,256]{1,0:T(8,128)(2,1)S(1)} %pad_maximum_fusion.refs_0_, bf16[1024,256]{1,0:T(8,128)(2,1)S(1)} %collective-permute-done.1.refs_1_, ...), custom_call_target="tpu_custom_call" | custom-call | tf_op jit(solution)/shard_map/picked_rows/pallas_call | solution.py:155
  141.3 1.0 copy-done.5
  142.3 8.6 %all-to-all-start.1 = ((bf16[16,256,256]{2,1,0:T(8,128)(2,1)}), bf16[16,256,256]{2,1,0:T(8,128)(2,1)S(1)}, u32[]{:S(2)}, u32[]{:S(2)}) async-start(bf16[16,256,256]{2,1,0:T(8,128)(2,1)} %picked_rows.1), calls=%async_computation.1 | async-start | bytes 4194304 | tf_op jit(solution)/shard_map/all_to_all | solution.py:298
  150.9 1.5 convert_reduce_fusion
  152.4 0.7 dynamic-slice_bitcast_fusion
  153.1 4.9 %collective-permute-start.4 = (f32[2,2,64,128]{3,2,1,0:T(8,128)}, f32[2,2,64,128]{3,2,1,0:T(8,128)}, u32[]{:S(2)}, u32[]{:S(2)}) collective-permute-start(f32[2,2,64,128]{3,2,1,0:T(8,128)} %dynamic-slice_bitcast_fusion), channel_id=1, source_target_pairs={{0,256},{256,0},{1,257},{257,1},{2,258},{258,2},{3,259},{259,3},{4... | collective-permute-start | bytes 393224 | tf_op jit(solution)/shard_map/ppermute | solution.py:305
  158.0 19.1 %collective-permute-done.4 = f32[2,2,64,128]{3,2,1,0:T(8,128)} collective-permute-done((f32[2,2,64,128]{3,2,1,0:T(8,128)}, f32[2,2,64,128]{3,2,1,0:T(8,128)}, u32[]{:S(2)}, u32[]{:S(2)}) %collective-permute-start.4) | collective-permute-done | bytes 131104 | tf_op jit(solution)/shard_map/ppermute | solution.py:305
  177.1 0.9 fusion
  178.0 0.1 copy.19
  178.2 0.8 reshape.138
  178.9 1.1 all-to-all-done.1.rows_ref
  180.0 1.0 copy-done.2
  181.1 2.5 %final_outputs.1 = (bf16[1,64,4096]{2,1,0:T(8,128)(2,1)}, bf16[1,64,4096]{2,1,0:T(8,128)(2,1)}, f32[1,64,128]{2,1,0:T(8,128)}) custom-call(bf16[16,256,256]{2,1,0:T(8,128)(2,1)S(1)} %all-to-all-done.1.rows_ref, bf16[2,64,128]{2,1,0:T(8,128)(2,1)S(1)} %copy-done.3, bf16[2,64,128]{2,1,0:T(8,128)(2,1)S(1)} %copy-done.3, bf16[1,64,4096]{2,1,0:T(8,128)(2,1)S(1)} %copy-done, ...), custom_call_target="tpu_custom_call" | custom-call | tf_op jit(solution)/shard_map/final_outputs/pallas_call | solution.py:209
  (28 shorter events, 0.6 us)
Async XLA Ops:
  2.3 18.3 %collective-permute-start = (bf16[16,4096]{1,0:T(8,128)(2,1)S(1)}, bf16[16,4096]{1,0:T(8,128)(2,1)S(1)}, u32[]{:S(2)}, u32[]{:S(2)}) collective-permute-start(bf16[16,4096]{1,0:T(8,128)(2,1)S(1)} %get-tuple-element.21), channel_id=1, source_target_pairs={{0,385},{1,384},{128,257},{129,256},{256,129},{257,128},{384,1},{3... | collective-permute-start | bytes 393224 | tf_op jit(solution)/shard_map/ppermute | solution.py:239
  20.5 0.7 copy-start.6
  54.0 18.3 %collective-permute-start.1 = (bf16[1024,256]{1,0:T(8,128)(2,1)S(1)}, bf16[1024,256]{1,0:T(8,128)(2,1)S(1)}, u32[]{:S(2)}, u32[]{:S(2)}) collective-permute-start(bf16[1024,256]{1,0:T(8,128)(2,1)S(1)} %pad_maximum_fusion.refs_0_), channel_id=1, source_target_pairs={{0,14},{2,4},{4,2},{6,8},{8,6},{10,12},{12,10},{14,0},{1,15},{3,5}... | collective-permute-start | bytes 1572872 | tf_op jit(solution)/shard_map/ppermute | solution.py:248
  72.3 69.0 %all-to-all-start.2 = ((bf16[64,64,128]{2,1,0:T(8,128)(2,1)}), bf16[64,64,128]{2,1,0:T(8,128)(2,1)S(1)}, u32[]{:S(2)}, u32[]{:S(2)}) async-start(bf16[64,64,128]{2,1,0:T(8,128)(2,1)} %bitcast.7), calls=%async_computation.2 | async-start | bytes 2097152 | tf_op jit(solution)/shard_map/all_to_all | solution.py:289
  79.7 34.2 %collective-permute-start.2 = (bf16[1024,256]{1,0:T(8,128)(2,1)S(1)}, bf16[1024,256]{1,0:T(8,128)(2,1)S(1)}, u32[]{:S(2)}, u32[]{:S(2)}) collective-permute-start(bf16[1024,256]{1,0:T(8,128)(2,1)S(1)} %collective-permute-done.1.refs_1_), channel_id=1, source_target_pairs={{0,2},{2,0},{4,6},{6,4},{8,10},{10,8},{12,14},{14,12},{1,3},{3,1},... | collective-permute-start | bytes 1572872 | tf_op jit(solution)/shard_map/ppermute | solution.py:248
  113.9 14.6 %collective-permute-start.3 = (bf16[1024,256]{1,0:T(8,128)(2,1)S(1)}, bf16[1024,256]{1,0:T(8,128)(2,1)S(1)}, u32[]{:S(2)}, u32[]{:S(2)}) collective-permute-start(bf16[1024,256]{1,0:T(8,128)(2,1)S(1)} %collective-permute-done.2.refs_2_), channel_id=1, source_target_pairs={{0,14},{2,4},{4,2},{6,8},{8,6},{10,12},{12,10},{14,0},{1,15},{3,5}... | collective-permute-start | bytes 1572872 | tf_op jit(solution)/shard_map/ppermute | solution.py:248
  141.3 1.0 copy-start.5
  142.3 37.7 %all-to-all-start.1 = ((bf16[16,256,256]{2,1,0:T(8,128)(2,1)}), bf16[16,256,256]{2,1,0:T(8,128)(2,1)S(1)}, u32[]{:S(2)}, u32[]{:S(2)}) async-start(bf16[16,256,256]{2,1,0:T(8,128)(2,1)} %picked_rows.1), calls=%async_computation.1 | async-start | bytes 4194304 | tf_op jit(solution)/shard_map/all_to_all | solution.py:298
  150.9 29.1 %copy-start = (bf16[1,64,4096]{2,1,0:T(8,128)(2,1)S(1)}, bf16[1,64,4096]{2,1,0:T(8,128)(2,1)}, u32[]{:S(2)}) copy-start(bf16[1,64,4096]{2,1,0:T(8,128)(2,1)} %gate_a_ref.1) | copy-start | bytes 1572868
  150.9 29.1 %copy-start.1 = (bf16[1,64,4096]{2,1,0:T(8,128)(2,1)S(1)}, bf16[1,64,4096]{2,1,0:T(8,128)(2,1)}, u32[]{:S(2)}) copy-start(bf16[1,64,4096]{2,1,0:T(8,128)(2,1)} %cot_ref.3) | copy-start | bytes 1572868
  150.9 29.1 %copy-start.3 = (bf16[2,64,128]{2,1,0:T(8,128)(2,1)S(1)}, bf16[2,64,128]{2,1,0:T(8,128)(2,1)}, u32[]{:S(2)}) copy-start(bf16[2,64,128]{2,1,0:T(8,128)(2,1)} %mixing.1.mix_ref.mix_a_ref.mix_b_ref) | copy-start | bytes 98308
  150.9 29.1 %copy-start.4 = (s32[1,2,64,128]{3,2,1,0:T(8,128)S(1)}, s32[1,2,64,128]{3,2,1,0:T(8,128)}, u32[]{:S(2)}) copy-start(s32[1,2,64,128]{3,2,1,0:T(8,128)} %slots_ref.3) | copy-start | bytes 196612
  153.1 24.0 %collective-permute-start.4 = (f32[2,2,64,128]{3,2,1,0:T(8,128)}, f32[2,2,64,128]{3,2,1,0:T(8,128)}, u32[]{:S(2)}, u32[]{:S(2)}) collective-permute-start(f32[2,2,64,128]{3,2,1,0:T(8,128)} %dynamic-slice_bitcast_fusion), channel_id=1, source_target_pairs={{0,256},{256,0},{1,257},{257,1},{2,258},{258,2},{3,259},{259,3},{4... | collective-permute-start | bytes 393224 | tf_op jit(solution)/shard_map/ppermute | solution.py:305
  180.0 1.0 copy-start.2

commit v5 on v4

--- a/solution.py
+++ b/solution.py
@@ -8,10 +8,10 @@
 
 SECTION = ("zl1", "zl0", "c")
 TABLE = ("x1", "x0", "y1", "y0", "zh")
-GRAD_GROUP = ("x1", "zl0", "c", "x0", "y0")
-ROW_GROUP = ("x1", "zl0", "c", "x0")
+GROUP = ("x1", "zl0", "c", "x0", "y0")
 RING = ("y1", "y0")
 ROWS_DEV = 64
+AWAY = (-1, 1, 2)
 F32 = jnp.float32
 BF16 = jnp.bfloat16
 VMEM = pltpu.CompilerParams(vmem_limit_bytes=40 * 1024 * 1024)
@@ -33,29 +33,29 @@
 
 
 def mixing_kernel(slots_ref, weights_ref, out_ref):
-    out_ref[0] = mixing_of(slots_ref[0, 0], weights_ref[0, 0])
-
-
-def mixing(slots, weights):
+    out_ref[...] = mixing_of(slots_ref[0, 0], weights_ref[0, 0])
+
+
+def mixing(slots, weights, batch):
     tokens, listed = slots.shape[2:]
-    picks = pl.BlockSpec((1, 1, tokens, listed), lambda c: (0, c, 0, 0))
+    picks = pl.BlockSpec((1, 1, tokens, listed), lambda i: (0, batch, 0, 0))
     return pl.pallas_call(
         mixing_kernel,
-        grid=(2,),
+        grid=(1,),
         in_specs=[picks, picks],
-        out_specs=pl.BlockSpec((1, tokens, listed), lambda c: (c, 0, 0)),
-        out_shape=jax.ShapeDtypeStruct((2, tokens, listed), BF16),
+        out_specs=pl.BlockSpec((tokens, listed), lambda i: (0, 0)),
+        out_shape=jax.ShapeDtypeStruct((tokens, listed), BF16),
         compiler_params=MOST_VMEM,
         name="mixing",
     )(slots, weights)
 
 
 def outgoing_kernel(gate_ref, cot_ref, mix_ref, ids_ref, own_ref, other_ref, out_ref):
-    listed = mix_ref.shape[2]
+    listed = mix_ref.shape[1]
     g, sig, inc = gated(gate_ref[0], cot_ref[0])
     grad_memory = (inc * g * sig).astype(BF16)
     rows = lax.dot_general(
-        mix_ref[0], grad_memory, (((0,), (0,)), ((), ())), preferred_element_type=F32
+        mix_ref[...], grad_memory, (((0,), (0,)), ((), ())), preferred_element_type=F32
     ).astype(BF16)
     ids = [ids_ref[0, c] for c in range(2)]
     codes = jnp.concatenate(
@@ -63,13 +63,11 @@
     )
     codes = codes.astype(F32).astype(BF16)
     table = jnp.concatenate([own_ref[...], other_ref[...]])
-    held = table.shape[0]
     for k in range(out_ref.shape[0]):
-        at = (k // 2) * 256
-        out_ref[k, :listed, :] = rows[:, k * 128 : (k + 1) * 128]
+        at = slice(k * 128, (k + 1) * 128)
+        out_ref[k, :listed, :] = rows[:, at]
         out_ref[k, listed : listed + 16, :] = codes
-        out_ref[k, listed + 16 : listed + 16 + held, :] = table[:, at : at + 128]
-        out_ref[k, listed + 16 + held :, :] = table[:, at + 128 : at + 256]
+        out_ref[k, listed + 16 :, :] = table[:, at]
 
 
 def outgoing(gate, cot, mix, row_ids, own, other, features):
@@ -78,13 +76,13 @@
     chunks, step = width // features, 8
     part = pl.BlockSpec((1, tokens, step * features), lambda i: (0, 0, i))
     rows = pl.BlockSpec((held, step * features), lambda i: (0, i))
-    height = listed + 16 + 4 * held
+    height = listed + 16 + 2 * held
     return pl.pallas_call(
         outgoing_kernel,
         grid=(chunks // step,),
         in_specs=[
             part, part,
-            pl.BlockSpec((1, tokens, listed), lambda i: (0, 0, 0)),
+            pl.BlockSpec((tokens, listed), lambda i: (0, 0)),
             pl.BlockSpec(row_ids.shape, lambda i: (0, 0, 0, 0)),
             rows, rows,
         ],
@@ -127,6 +125,9 @@
         out_specs=pl.BlockSpec((tile, features), lambda i: (i, 0)),
         out_shape=jax.ShapeDtypeStruct((rows, features), BF16),
         compiler_params=VMEM,
+        cost_estimate=pl.CostEstimate(
+            flops=2 * rows * lists * listed * features, bytes_accessed=received.size * 2, transcendentals=0
+        ),
         name="dense_rows",
     )(ids, received)
 
@@ -163,6 +164,11 @@
         out_specs=pl.BlockSpec((1, lists * listed, features), lambda i: (i, 0, 0)),
         out_shape=jax.ShapeDtypeStruct((members, lists * listed, features), BF16),
         compiler_params=VMEM,
+        cost_estimate=pl.CostEstimate(
+            flops=2 * members * lists * listed * rows * len(blocks) * features,
+            bytes_accessed=members * lists * listed * features * 2,
+            transcendentals=0,
+        ),
         name="picked_rows",
     )(ids, places, *blocks)
 
@@ -171,8 +177,8 @@
     rows_ref, mix_a_ref, mix_b_ref, gate_a_ref, cot_ref, gate_b_ref, slots_ref,
     mixed_ref, grad_gate_ref, grad_weights_ref, scores_ref,
 ):
-    listed = mix_a_ref.shape[2]
-    step, _, features = rows_ref.shape
+    listed = mix_a_ref.shape[1]
+    step, features = rows_ref.shape[0] // 2, rows_ref.shape[2] * 2
 
     @pl.when(pl.program_id(0) == 0)
     def _():
@@ -181,12 +187,12 @@
     part = jnp.zeros(scores_ref.shape, F32)
     for k in range(step):
         at = slice(k * features, (k + 1) * features)
-        fetched_a = rows_ref[k, :listed, :]
-        fetched_b = rows_ref[k, listed:, :]
-        memory_b = jnp.dot(mix_b_ref[0], fetched_b, preferred_element_type=F32)
+        fetched = jnp.concatenate([rows_ref[2 * k], rows_ref[2 * k + 1]], axis=1)
+        fetched_a, fetched_b = fetched[:listed], fetched[listed:]
+        memory_b = jnp.dot(mix_b_ref[...], fetched_b, preferred_element_type=F32)
         gb = gate_b_ref[0, :, at].astype(F32)
         mixed_ref[0, :, at] = (gb / (1.0 + jnp.exp(-gb)) * memory_b).astype(BF16)
-        memory_a = jnp.dot(mix_a_ref[0], fetched_a, preferred_element_type=F32)
+        memory_a = jnp.dot(mix_a_ref[...], fetched_a, preferred_element_type=F32)
         g, sig, inc = gated(gate_a_ref[0, :, at], cot_ref[0, :, at])
         grad_gate_ref[0, :, at] = (inc * memory_a * sig * (1.0 + g * (1.0 - sig))).astype(BF16)
         grad_memory = (inc * g * sig).astype(BF16)
@@ -200,20 +206,19 @@
         grad_weights_ref[0] = jnp.take_along_axis(scores_ref[...], slots_ref[0, 0], axis=1)
 
 
-def final_outputs(fetched, mix, gate_a, cot, gate_b, slots):
+def final_outputs(fetched, mix_a, mix_b, gate_a, cot, gate_b, slots):
     chunks, rows, features = fetched.shape
     _, tokens, width = gate_a.shape
-    listed = mix.shape[-1]
-    step = 4
+    listed = mix_a.shape[1]
+    step = 8
+    whole = pl.BlockSpec((tokens, listed), lambda i: (0, 0))
     part = pl.BlockSpec((1, tokens, step * features), lambda i: (0, 0, i))
     return pl.pallas_call(
         final_kernel,
         grid=(chunks // step,),
         in_specs=[
             pl.BlockSpec((step, rows, features), lambda i: (i, 0, 0)),
-            pl.BlockSpec((1, tokens, listed), lambda i: (0, 0, 0)),
-            pl.BlockSpec((1, tokens, listed), lambda i: (1, 0, 0)),
-            part, part, part,
+            whole, whole, part, part, part,
             pl.BlockSpec((1, 1, tokens, listed), lambda i: (0, 0, 0, 0)),
         ],
         out_specs=[part, part, pl.BlockSpec((1, tokens, listed), lambda i: (0, 0, 0))],
@@ -225,7 +230,7 @@
         scratch_shapes=[pltpu.VMEM((tokens, listed), F32)],
         compiler_params=VMEM,
         name="final_outputs",
-    )(fetched, mix, mix, gate_a, cot, gate_b, slots)
+    )(fetched, mix_a, mix_b, gate_a, cot, gate_b, slots)
 
 
 def quarters(table):
@@ -239,20 +244,14 @@
     return quarter(zl0), lax.ppermute(quarter(1 - zl0), ("zl1", "zl0", "zh"), mirrored)
 
 
-def along_y(block, inner):
+def from_pair(block, away):
     n_y = lax.axis_size(RING)
-    if inner:
-        pairs = [(i, i ^ 1) for i in range(n_y)]
-    else:
-        pairs = [(i, (i + 1) % n_y if i % 2 else (i - 1) % n_y) for i in range(n_y)]
-    return lax.ppermute(block, RING, pairs)
+    return lax.ppermute(block, RING, [((i + 2 * away) % n_y, i) for i in range(n_y)])
 
 
 def block_places(members, held):
-    n_x, n_pairs = 4, lax.axis_size("y1")
-    y0, pair = lax.axis_index("y0"), lax.axis_index("y1")
-    turn = 2 * y0 - 1
-    pairs = (pair + jnp.stack([jnp.zeros_like(turn), turn, -turn, 2 * jnp.ones_like(turn)])) & (n_pairs - 1)
+    n_pairs = lax.axis_size("y1")
+    pairs = (lax.axis_index("y1") + jnp.array((0,) + AWAY, jnp.int32)) & (n_pairs - 1)
     member = jnp.arange(members, dtype=jnp.int32)
     x = (member >> 4) * 2 + ((member >> 1) & 1)
     quarter, y_low = (member >> 2) & 3, member & 1
@@ -270,32 +269,25 @@
     listed = row_ids.shape[-1]
 
     own, other = quarters(table)
-    mix = mixing(slots, weights)
-    mix, other = lax.optimization_barrier((mix, other))
-    sent = outgoing(gate_a, cotangent_a, mix, row_ids, own, other, 128)
-    received = lax.all_to_all(sent, GRAD_GROUP, split_axis=0, concat_axis=0, tiled=True)
+    mix_a = mixing(slots, weights, 0)
+    mix_a, other = lax.optimization_barrier((mix_a, other))
+    sent = outgoing(gate_a, cotangent_a, mix_a, row_ids, own, other, 128)
+    received = lax.all_to_all(sent, GROUP, split_axis=0, concat_axis=0, tiled=True)
 
     members, held = received.shape[0], own.shape[0]
-    first = listed + 16
-    halves = [
-        received[:, at : at + 2 * held].reshape(members * 2 * held, -1) for at in (first, first + 2 * held)
-    ]
-    block = jnp.concatenate(halves, axis=1)
+    block = received[:, listed + 16 :].reshape(members * 2 * held, -1)
     codes = received[:, listed : listed + 4, :].astype(F32)
     ids = codes[:, 0::2] * ROWS_DEV + codes[:, 1::2]
-    dense = dense_rows(ids[:, 0], received, owners * rows_dev)
-    next_1 = along_y(block, False)
-    dense, next_1 = lax.optimization_barrier((dense, next_1))
+    ids_a, rows = ids[:, 0], owners * rows_dev
+    others = [from_pair(block, away) for away in AWAY]
+    dense = dense_rows(ids_a, received, rows)
+    dense, *others = lax.optimization_barrier((dense, *others))
     arrived = lax.all_to_all(
         dense.reshape(owners, rows_dev, -1), TABLE, split_axis=0, concat_axis=0, tiled=True
     )
-    next_2 = along_y(next_1, True)
-    next_3 = along_y(next_2, False)
-
-    near = ids.reshape(-1, 2, 2, listed)
-    near = lax.dynamic_index_in_dim(near, lax.axis_index("y0"), 1, keepdims=False)
-    picked = picked_rows(near, block_places(members, held), (block, next_1, next_2, next_3))
-    fetched = lax.all_to_all(picked, ROW_GROUP, split_axis=0, concat_axis=0, tiled=True)
+
+    picked = picked_rows(ids, block_places(members, held), (block, *others))
+    fetched = lax.all_to_all(picked, GROUP, split_axis=0, concat_axis=0, tiled=True)
 
     features = arrived.shape[-1]
     summed = jnp.sum(arrived.reshape(2, 2, -1, 2, 2, rows_dev, features).astype(F32), axis=(2, 4))
@@ -305,7 +297,9 @@
     total = kept + lax.ppermute(given, "zl1", [(0, 1), (1, 0)])
     grad_table = jnp.transpose(total, (2, 0, 1, 3)).reshape(rows_dev, -1)
 
-    mixed, grad_gate, grad_weights = final_outputs(fetched, mix, gate_a, cotangent_a, gate_b, slots)
+    mixed, grad_gate, grad_weights = final_outputs(
+        fetched, mix_a, mixing(slots, weights, 1), gate_a, cotangent_a, gate_b, slots
+    )
     return mixed, grad_gate, grad_weights, grad_table
 
 

time: 185 us -> 169 us (0.914)
  waiting for transfers between devices: 61.8 us -> 28.6 us
  Pallas kernels: 37.5 us -> 50.4 us
  starting transfers between devices: 45.3 us -> 50.4 us
  blocking collectives: 28.6 us -> 25.7 us
  local copies, waits for them, and re-layouts: 6.76 us -> 8.79 us
    ppermute x3, waiting for transfers between devices: 41.1 us -> 3.39 us  [from_pair(): lax.ppermute(block, RING, [((i + 2 * away) % n_y, i) for i in range(n_y)])]
    pallas_call x1, Pallas kernels: 12.8 us -> 24.4 us  [picked_rows(): pl.pallas_call(pick_kernel, grid=(members,), in_specs=[pl.BlockSpec((1, l...]
    all_to_all x1, starting transfers between devices: 7.29 us -> 12.7 us  [local(): lax.all_to_all(dense.reshape(owners, rows_dev, -1), TABLE, split_axis=0,...]
    ppermute x1, waiting for transfers between devices: 19.1 us -> 14.7 us  [local(): total = kept + lax.ppermute(given, 'zl1', [(0, 1), (1, 0)])]
    all_to_all x1, waiting for transfers between devices: 0.01 us -> 4.15 us  [local(): lax.all_to_all(dense.reshape(owners, rows_dev, -1), TABLE, split_axis=0,...]
    all_to_all x1, blocking collectives: 28.6 us -> 25.7 us  [local(): lax.all_to_all(sent, GROUP, split_axis=0, concat_axis=0, tiled=True)]
    ppermute x1, waiting for transfers between devices: 0.47 us -> 2.94 us  [quarters(): lax.ppermute(quarter(1 - zl0), ('zl1', 'zl0', 'zh'), mirrored)]
    all_to_all x1, waiting for transfers between devices: 1.09 us -> 3.38 us  [local(): lax.all_to_all(picked, GROUP, split_axis=0, concat_axis=0, tiled=True)]
  transfers between devices with their start and end apart: 7 -> 7, of which waited for: 5 -> 5; matrix products, arithmetic and copies ran while one was open for 3% -> 3% of each run, Pallas kernels for 17% -> 26%
where the time goes in v5:
time: 169 us; the launch traced here: 167 us
  starting transfers between devices  50.4 us (30%)
  Pallas kernels  50.4 us (30%)
  waiting for transfers between devices  28.6 us (17%)
  blocking collectives  25.7 us (15%)
  local copies, waits for them, and re-layouts  8.79 us (5%)
  other arithmetic  2.64 us (2%)
    all_to_all x1, blocking collectives, local(): lax.all_to_all(sent, GROUP, split_axis=0, concat_axis=0, tiled=True)  25.7 us
    pallas_call x1, Pallas kernels, picked_rows(): pl.pallas_call(pick_kernel, grid=(members,), in_specs=[pl.BlockSpec((1, l...  24.4 us
    ppermute x1, waiting for transfers between devices, local(): total = kept + lax.ppermute(given, 'zl1', [(0, 1), (1, 0)])  14.7 us
    ppermute x3, starting transfers between devices, from_pair(): lax.ppermute(block, RING, [((i + 2 * away) % n_y, i) for i in range(n_y)])  13.9 us
    all_to_all x1, starting transfers between devices, local(): lax.all_to_all(dense.reshape(owners, rows_dev, -1), TABLE, split_axis=0,...  12.7 us
    pallas_call x1, Pallas kernels, dense_rows(): pl.pallas_call(dense_kernel, grid=(rows // tile,), in_specs=[pl.BlockSpec...  11.9 us
    ppermute x1, starting transfers between devices, quarters(): lax.ppermute(quarter(1 - zl0), ('zl1', 'zl0', 'zh'), mirrored)  11.5 us
    pallas_call x2, Pallas kernels, mixing(): pl.pallas_call(mixing_kernel, grid=(1,), in_specs=[picks, picks], out_spe...  7.64 us
  transfers between devices with their start and end apart: 7, of which 5 were waited for; matrix products, arithmetic and copies ran while one was open for 3% of the time, Pallas kernels for 26%

profile of v5, /device:TPU:1, one launch (start us, length us, event | category | flops | bytes accessed | tf_op | source)
XLA Modules:
  0.0 167.4 jit_solution(934334118742055361)
XLA Ops:
  0.6 1.6 constant_dynamic-slice_fusion
  2.3 11.5 %collective-permute-start = (bf16[16,4096]{1,0:T(8,128)(2,1)S(1)}, bf16[16,4096]{1,0:T(8,128)(2,1)S(1)}, u32[]{:S(2)}, u32[]{:S(2)}) collective-permute-start(bf16[16,4096]{1,0:T(8,128)(2,1)S(1)} %get-tuple-element.23), channel_id=1, source_target_pairs={{0,385},{1,384},{128,257},{129,256},{256,129},{257,128},{384,1},{3... | collective-permute-start | bytes 393224 | tf_op jit(solution)/shard_map/ppermute | solution.py:244
  13.8 3.8 %mixing.2.mix_ref.mix_a_ref = bf16[64,128]{1,0:T(8,128)(2,1)} custom-call(s32[1,2,64,128]{3,2,1,0:T(8,128)} %slots_ref.5, f32[1,2,64,128]{3,2,1,0:T(8,128)} %weights_ref.3), custom_call_target="tpu_custom_call" | custom-call | tf_op jit(solution)/shard_map/mixing/pallas_call | solution.py:42
  17.6 2.9 %collective-permute-done.other_ref = bf16[16,4096]{1,0:T(8,128)(2,1)S(1)} collective-permute-done((bf16[16,4096]{1,0:T(8,128)(2,1)S(1)}, bf16[16,4096]{1,0:T(8,128)(2,1)S(1)}, u32[]{:S(2)}, u32[]{:S(2)}) %collective-permute-start) | collective-permute-done | bytes 131104 | tf_op jit(solution)/shard_map/ppermute | solution.py:244
  20.5 0.7 copy-done.8
  21.2 4.0 %outgoing_rows.1 = bf16[32,176,128]{2,1,0:T(8,128)(2,1)} custom-call(bf16[1,64,4096]{2,1,0:T(8,128)(2,1)} %gate_a_ref.1, bf16[1,64,4096]{2,1,0:T(8,128)(2,1)} %cot_ref.3, bf16[64,128]{1,0:T(8,128)(2,1)} %mixing.2.mix_ref.mix_a_ref, s32[1,2,1,128]{3,2,1,0:T(1,128)} %ids_ref.1, bf16[16,4096]{1,0:T(8,128)(2,1)} %get-tuple-element.22.own_ref, ...), custom_call_target="tpu_custom_call" | custom-call | tf_op jit(solution)/shard_map/outgoing_rows/pallas_call | solution.py:80
  25.2 25.7 %all_to_all.15.rows_ref = bf16[32,176,128]{2,1,0:T(8,128)(2,1)S(1)} all-to-all(bf16[32,176,128]{2,1,0:T(8,128)(2,1)} %outgoing_rows.1), channel_id=1, replica_groups=mesh['zl1'=2,'zl0'=2,'c'=2,'x1'=2,'x0'=2,'y1'=4,'y0'=2,'zh'=2] {'x1','zl..., dimensions={0} | all-to-all | bytes 2883584 | tf_op jit(solution)/shard_map/all_to_all | solution.py:275
  50.9 0.1 slice.16
  51.2 4.2 %collective-permute-start.1 = (bf16[1024,128]{1,0:T(8,128)(2,1)S(1)}, bf16[1024,128]{1,0:T(8,128)(2,1)S(1)}, u32[]{:S(2)}, u32[]{:S(2)}) collective-permute-start(bf16[1024,128]{1,0:T(8,128)(2,1)S(1)} %bitcast.13), channel_id=1, source_target_pairs={{12,0},{14,2},{0,4},{2,6},{4,8},{6,10},{8,12},{10,14},{13,1},{15,3... | collective-permute-start | bytes 786440 | tf_op jit(solution)/shard_map/ppermute | solution.py:249
  55.4 3.2 %collective-permute-start.2 = (bf16[1024,128]{1,0:T(8,128)(2,1)S(1)}, bf16[1024,128]{1,0:T(8,128)(2,1)S(1)}, u32[]{:S(2)}, u32[]{:S(2)}) collective-permute-start(bf16[1024,128]{1,0:T(8,128)(2,1)S(1)} %bitcast.14), channel_id=1, source_target_pairs={{4,0},{6,2},{8,4},{10,6},{12,8},{14,10},{0,12},{2,14},{5,1},{7,3},... | collective-permute-start | bytes 786440 | tf_op jit(solution)/shard_map/ppermute | solution.py:249
  58.6 6.6 %collective-permute-start.3 = (bf16[1024,128]{1,0:T(8,128)(2,1)S(1)}, bf16[1024,128]{1,0:T(8,128)(2,1)S(1)}, u32[]{:S(2)}, u32[]{:S(2)}) collective-permute-start(bf16[1024,128]{1,0:T(8,128)(2,1)S(1)} %bitcast.15), channel_id=1, source_target_pairs={{8,0},{10,2},{12,4},{14,6},{0,8},{2,10},{4,12},{6,14},{9,1},{11,3}... | collective-permute-start | bytes 786440 | tf_op jit(solution)/shard_map/ppermute | solution.py:249
  65.2 11.9 %dense_rows.1 = bf16[4096,128]{1,0:T(8,128)(2,1)} custom-call(f32[32,128]{1,0:T(8,128)S(1)} %bitcast.17, bf16[32,176,128]{2,1,0:T(8,128)(2,1)S(1)} %all_to_all.15.rows_ref), custom_call_target="tpu_custom_call" | custom-call | flops 4294967296 | bytes 1441792 | tf_op jit(solution)/shard_map/dense_rows/pallas_call | solution.py:118
  77.1 3.4 %collective-permute-done.3.refs_3_ = bf16[1024,128]{1,0:T(8,128)(2,1)S(1)} collective-permute-done((bf16[1024,128]{1,0:T(8,128)(2,1)S(1)}, bf16[1024,128]{1,0:T(8,128)(2,1)S(1)}, u32[]{:S(2)}, u32[]{:S(2)}) %collective-permute-start.3) | collective-permute-done | bytes 262176 | tf_op jit(solution)/shard_map/ppermute | solution.py:249
  80.4 12.7 %all-to-all-start.2 = ((bf16[64,64,128]{2,1,0:T(8,128)(2,1)}), bf16[64,64,128]{2,1,0:T(8,128)(2,1)S(1)}, u32[]{:S(2)}, u32[]{:S(2)}) async-start(bf16[64,64,128]{2,1,0:T(8,128)(2,1)} %bitcast.2), calls=%async_computation.2 | async-start | bytes 2097152 | tf_op jit(solution)/shard_map/all_to_all | solution.py:285
  93.4 0.2 add.136
  93.7 0.2 add.137
  94.0 24.4 %picked_rows.1 = bf16[32,256,128]{2,1,0:T(8,128)(2,1)S(1)} custom-call(f32[32,2,128]{2,1,0:T(2,128)S(1)} %multiply_add_fusion.ids_ref, f32[4,1024]{1,0:T(4,128)S(1)} %add_convert_fusion.place_ref, bf16[1024,128]{1,0:T(8,128)(2,1)S(1)} %bitcast.16, bf16[1024,128]{1,0:T(8,128)(2,1)S(1)} %collective-permute-done.1.refs_1_, ...), custom_call_target="tpu_custom_call" | custom-call | flops 8589934592 | bytes 2097152 | tf_op jit(solution)/shard_map/picked_rows/pallas_call | solution.py:156
  118.4 1.3 copy-done.2
  119.7 4.2 %all-to-all-done.2 = bf16[64,64,128]{2,1,0:T(8,128)(2,1)S(1)} async-done(((bf16[64,64,128]{2,1,0:T(8,128)(2,1)}), bf16[64,64,128]{2,1,0:T(8,128)(2,1)S(1)}, u32[]{:S(2)}, u32[]{:S(2)}) %all-to-all-start.2) | async-done | bytes 1048608 | tf_op jit(solution)/shard_map/all_to_all | solution.py:285
  123.9 1.0 copy-done.7
  124.8 7.3 %all-to-all-start.1 = ((bf16[32,256,128]{2,1,0:T(8,128)(2,1)}), bf16[32,256,128]{2,1,0:T(8,128)(2,1)S(1)}, u32[]{:S(2)}, u32[]{:S(2)}) async-start(bf16[32,256,128]{2,1,0:T(8,128)(2,1)} %copy-done.2), calls=%async_computation.1 | async-start | bytes 4194304 | tf_op jit(solution)/shard_map/all_to_all | solution.py:290
  132.2 1.5 convert_reduce_fusion
  133.7 0.7 dynamic-slice_bitcast_fusion
  134.4 4.9 %collective-permute-start.4 = (f32[2,2,64,128]{3,2,1,0:T(8,128)}, f32[2,2,64,128]{3,2,1,0:T(8,128)}, u32[]{:S(2)}, u32[]{:S(2)}) collective-permute-start(f32[2,2,64,128]{3,2,1,0:T(8,128)} %dynamic-slice_bitcast_fusion), channel_id=1, source_target_pairs={{0,256},{256,0},{1,257},{257,1},{2,258},{258,2},{3,259},{259,3},{4... | collective-permute-start | bytes 393224 | tf_op jit(solution)/shard_map/ppermute | solution.py:297
  139.3 3.8 %mixing.3.mix_b_ref = bf16[64,128]{1,0:T(8,128)(2,1)} custom-call(s32[1,2,64,128]{3,2,1,0:T(8,128)} %slots_ref.5, f32[1,2,64,128]{3,2,1,0:T(8,128)} %weights_ref.3), custom_call_target="tpu_custom_call" | custom-call | tf_op jit(solution)/shard_map/mixing/pallas_call | solution.py:42
  143.1 14.7 %collective-permute-done.4 = f32[2,2,64,128]{3,2,1,0:T(8,128)} collective-permute-done((f32[2,2,64,128]{3,2,1,0:T(8,128)}, f32[2,2,64,128]{3,2,1,0:T(8,128)}, u32[]{:S(2)}, u32[]{:S(2)}) %collective-permute-start.4) | collective-permute-done | bytes 131104 | tf_op jit(solution)/shard_map/ppermute | solution.py:297
  157.9 0.9 fusion
  158.9 0.8 reshape.100
  159.7 3.4 %all-to-all-done.1.rows_ref = bf16[32,256,128]{2,1,0:T(8,128)(2,1)S(1)} async-done(((bf16[32,256,128]{2,1,0:T(8,128)(2,1)}), bf16[32,256,128]{2,1,0:T(8,128)(2,1)S(1)}, u32[]{:S(2)}, u32[]{:S(2)}) %all-to-all-start.1) | async-done | bytes 2097184 | tf_op jit(solution)/shard_map/all_to_all | solution.py:290
  163.1 1.0 copy-done.4
  164.1 0.7 copy-done.6
  164.8 2.5 %final_outputs.1 = (bf16[1,64,4096]{2,1,0:T(8,128)(2,1)}, bf16[1,64,4096]{2,1,0:T(8,128)(2,1)}, f32[1,64,128]{2,1,0:T(8,128)}) custom-call(bf16[32,256,128]{2,1,0:T(8,128)(2,1)S(1)} %all-to-all-done.1.rows_ref, bf16[64,128]{1,0:T(8,128)(2,1)S(1)} %copy-done.5, bf16[64,128]{1,0:T(8,128)(2,1)S(1)} %copy-done.6, bf16[1,64,4096]{2,1,0:T(8,128)(2,1)S(1)} %copy-done, ...), custom_call_target="tpu_custom_call" | custom-call | tf_op jit(solution)/shard_map/final_outputs/pallas_call | solution.py:216
  (33 shorter events, 0.7 us)
Async XLA Ops:
  2.3 18.3 %collective-permute-start = (bf16[16,4096]{1,0:T(8,128)(2,1)S(1)}, bf16[16,4096]{1,0:T(8,128)(2,1)S(1)}, u32[]{:S(2)}, u32[]{:S(2)}) collective-permute-start(bf16[16,4096]{1,0:T(8,128)(2,1)S(1)} %get-tuple-element.23), channel_id=1, source_target_pairs={{0,385},{1,384},{128,257},{129,256},{256,129},{257,128},{384,1},{3... | collective-permute-start | bytes 393224 | tf_op jit(solution)/shard_map/ppermute | solution.py:244
  20.5 0.7 copy-start.8
  51.2 25.9 %collective-permute-start.1 = (bf16[1024,128]{1,0:T(8,128)(2,1)S(1)}, bf16[1024,128]{1,0:T(8,128)(2,1)S(1)}, u32[]{:S(2)}, u32[]{:S(2)}) collective-permute-start(bf16[1024,128]{1,0:T(8,128)(2,1)S(1)} %bitcast.13), channel_id=1, source_target_pairs={{12,0},{14,2},{0,4},{2,6},{4,8},{6,10},{8,12},{10,14},{13,1},{15,3... | collective-permute-start | bytes 786440 | tf_op jit(solution)/shard_map/ppermute | solution.py:249
  55.4 21.7 %collective-permute-start.2 = (bf16[1024,128]{1,0:T(8,128)(2,1)S(1)}, bf16[1024,128]{1,0:T(8,128)(2,1)S(1)}, u32[]{:S(2)}, u32[]{:S(2)}) collective-permute-start(bf16[1024,128]{1,0:T(8,128)(2,1)S(1)} %bitcast.14), channel_id=1, source_target_pairs={{4,0},{6,2},{8,4},{10,6},{12,8},{14,10},{0,12},{2,14},{5,1},{7,3},... | collective-permute-start | bytes 786440 | tf_op jit(solution)/shard_map/ppermute | solution.py:249
  58.6 21.9 %collective-permute-start.3 = (bf16[1024,128]{1,0:T(8,128)(2,1)S(1)}, bf16[1024,128]{1,0:T(8,128)(2,1)S(1)}, u32[]{:S(2)}, u32[]{:S(2)}) collective-permute-start(bf16[1024,128]{1,0:T(8,128)(2,1)S(1)} %bitcast.15), channel_id=1, source_target_pairs={{8,0},{10,2},{12,4},{14,6},{0,8},{2,10},{4,12},{6,14},{9,1},{11,3}... | collective-permute-start | bytes 786440 | tf_op jit(solution)/shard_map/ppermute | solution.py:249
  77.0 16.1 %copy-start.9 = (s32[4]{0:T(128)S(1)}, s32[4]{0:T(128)}, u32[]{:S(2)}) copy-start(s32[4]{0:T(128)} %constant.57.clone) | copy-start | bytes 52
  80.4 43.4 %all-to-all-start.2 = ((bf16[64,64,128]{2,1,0:T(8,128)(2,1)}), bf16[64,64,128]{2,1,0:T(8,128)(2,1)S(1)}, u32[]{:S(2)}, u32[]{:S(2)}) async-start(bf16[64,64,128]{2,1,0:T(8,128)(2,1)} %bitcast.2), calls=%async_computation.2 | async-start | bytes 2097152 | tf_op jit(solution)/shard_map/all_to_all | solution.py:285
  118.4 1.3 copy-start.2
  123.8 1.0 copy-start.7
  124.8 38.2 %all-to-all-start.1 = ((bf16[32,256,128]{2,1,0:T(8,128)(2,1)}), bf16[32,256,128]{2,1,0:T(8,128)(2,1)S(1)}, u32[]{:S(2)}, u32[]{:S(2)}) async-start(bf16[32,256,128]{2,1,0:T(8,128)(2,1)} %copy-done.2), calls=%async_computation.1 | async-start | bytes 4194304 | tf_op jit(solution)/shard_map/all_to_all | solution.py:290
  132.2 30.9 %copy-start = (bf16[1,64,4096]{2,1,0:T(8,128)(2,1)S(1)}, bf16[1,64,4096]{2,1,0:T(8,128)(2,1)}, u32[]{:S(2)}) copy-start(bf16[1,64,4096]{2,1,0:T(8,128)(2,1)} %gate_a_ref.1) | copy-start | bytes 1572868
  132.2 30.9 %copy-start.1 = (bf16[1,64,4096]{2,1,0:T(8,128)(2,1)S(1)}, bf16[1,64,4096]{2,1,0:T(8,128)(2,1)}, u32[]{:S(2)}) copy-start(bf16[1,64,4096]{2,1,0:T(8,128)(2,1)} %cot_ref.3) | copy-start | bytes 1572868
  132.2 30.8 %copy-start.3 = (s32[1,2,64,128]{3,2,1,0:T(8,128)S(1)}, s32[1,2,64,128]{3,2,1,0:T(8,128)}, u32[]{:S(2)}) copy-start(s32[1,2,64,128]{3,2,1,0:T(8,128)} %slots_ref.5) | copy-start | bytes 196612
  132.2 30.8 %copy-start.5 = (bf16[64,128]{1,0:T(8,128)(2,1)S(1)}, bf16[64,128]{1,0:T(8,128)(2,1)}, u32[]{:S(2)}) copy-start(bf16[64,128]{1,0:T(8,128)(2,1)} %mixing.2.mix_ref.mix_a_ref) | copy-start | bytes 49156
  134.4 23.5 %collective-permute-start.4 = (f32[2,2,64,128]{3,2,1,0:T(8,128)}, f32[2,2,64,128]{3,2,1,0:T(8,128)}, u32[]{:S(2)}, u32[]{:S(2)}) collective-permute-start(f32[2,2,64,128]{3,2,1,0:T(8,128)} %dynamic-slice_bitcast_fusion), channel_id=1, source_target_pairs={{0,256},{256,0},{1,257},{257,1},{2,258},{258,2},{3,259},{259,3},{4... | collective-permute-start | bytes 393224 | tf_op jit(solution)/shard_map/ppermute | solution.py:297
  163.1 1.0 copy-start.4
  164.1 0.7 copy-start.6

commit v6 on v5

--- a/solution.py
+++ b/solution.py
@@ -11,7 +11,7 @@
 GROUP = ("x1", "zl0", "c", "x0", "y0")
 RING = ("y1", "y0")
 ROWS_DEV = 64
-AWAY = (-1, 1, 2)
+AWAY = (2, -1, 1)
 F32 = jnp.float32
 BF16 = jnp.bfloat16
 VMEM = pltpu.CompilerParams(vmem_limit_bytes=40 * 1024 * 1024)
@@ -36,7 +36,7 @@
     out_ref[...] = mixing_of(slots_ref[0, 0], weights_ref[0, 0])
 
 
-def mixing(slots, weights, batch):
+def mixing(slots, weights, batch, limit):
     tokens, listed = slots.shape[2:]
     picks = pl.BlockSpec((1, 1, tokens, listed), lambda i: (0, batch, 0, 0))
     return pl.pallas_call(
@@ -45,12 +45,12 @@
         in_specs=[picks, picks],
         out_specs=pl.BlockSpec((tokens, listed), lambda i: (0, 0)),
         out_shape=jax.ShapeDtypeStruct((tokens, listed), BF16),
-        compiler_params=MOST_VMEM,
+        compiler_params=limit,
         name="mixing",
     )(slots, weights)
 
 
-def outgoing_kernel(gate_ref, cot_ref, mix_ref, ids_ref, own_ref, other_ref, out_ref):
+def outgoing_kernel(gate_ref, cot_ref, mix_ref, ids_ref, out_ref):
     listed = mix_ref.shape[1]
     g, sig, inc = gated(gate_ref[0], cot_ref[0])
     grad_memory = (inc * g * sig).astype(BF16)
@@ -62,21 +62,16 @@
         [part for i in ids for part in (i // ROWS_DEV, i % ROWS_DEV)] + [jnp.zeros((12, listed), jnp.int32)]
     )
     codes = codes.astype(F32).astype(BF16)
-    table = jnp.concatenate([own_ref[...], other_ref[...]])
     for k in range(out_ref.shape[0]):
-        at = slice(k * 128, (k + 1) * 128)
-        out_ref[k, :listed, :] = rows[:, at]
-        out_ref[k, listed : listed + 16, :] = codes
-        out_ref[k, listed + 16 :, :] = table[:, at]
-
-
-def outgoing(gate, cot, mix, row_ids, own, other, features):
+        out_ref[k, :listed, :] = rows[:, k * 128 : (k + 1) * 128]
+        out_ref[k, listed:, :] = codes
+
+
+def outgoing(gate, cot, mix, row_ids, height, features):
     _, tokens, width = gate.shape
-    listed, held = row_ids.shape[-1], own.shape[0]
+    listed = row_ids.shape[-1]
     chunks, step = width // features, 8
     part = pl.BlockSpec((1, tokens, step * features), lambda i: (0, 0, i))
-    rows = pl.BlockSpec((held, step * features), lambda i: (0, i))
-    height = listed + 16 + 2 * held
     return pl.pallas_call(
         outgoing_kernel,
         grid=(chunks // step,),
@@ -84,13 +79,45 @@
             part, part,
             pl.BlockSpec((tokens, listed), lambda i: (0, 0)),
             pl.BlockSpec(row_ids.shape, lambda i: (0, 0, 0, 0)),
-            rows, rows,
         ],
-        out_specs=pl.BlockSpec((step, height, features), lambda i: (i, 0, 0)),
+        out_specs=pl.BlockSpec((step, listed + 16, features), lambda i: (i, 0, 0)),
         out_shape=jax.ShapeDtypeStruct((chunks, height, features), BF16),
         compiler_params=MOST_VMEM,
         name="outgoing_rows",
-    )(gate, cot, mix, row_ids, own, other)
+    )(gate, cot, mix, row_ids)
+
+
+def table_rows_kernel(own_ref, other_ref, payload_ref, out_ref):
+    features = out_ref.shape[2]
+
+    def put(rows_ref):
+        for k in range(out_ref.shape[0]):
+            out_ref[k] = rows_ref[:, k * features : (k + 1) * features]
+
+    @pl.when(pl.program_id(0) == 0)
+    def _():
+        put(own_ref)
+
+    @pl.when(pl.program_id(0) == 1)
+    def _():
+        put(other_ref)
+
+
+def with_table_rows(payload, own, other):
+    chunks, height, features = payload.shape
+    held, width = own.shape
+    at = height // held - 2
+    rows = pl.BlockSpec((held, width), lambda i: (0, 0))
+    return pl.pallas_call(
+        table_rows_kernel,
+        grid=(2,),
+        in_specs=[rows, rows, pl.BlockSpec(memory_space=pl.ANY)],
+        out_specs=pl.BlockSpec((chunks, held, features), lambda i: (0, at + i, 0)),
+        out_shape=jax.ShapeDtypeStruct(payload.shape, BF16),
+        input_output_aliases={2: 0},
+        compiler_params=MOST_VMEM,
+        name="table_rows",
+    )(own, other, payload)
 
 
 def dense_kernel(ids_ref, rows_ref, out_ref):
@@ -269,12 +296,14 @@
     listed = row_ids.shape[-1]
 
     own, other = quarters(table)
-    mix_a = mixing(slots, weights, 0)
-    mix_a, other = lax.optimization_barrier((mix_a, other))
-    sent = outgoing(gate_a, cotangent_a, mix_a, row_ids, own, other, 128)
+    held = own.shape[0]
+    mix_a = mixing(slots, weights, 0, MOST_VMEM)
+    sent = outgoing(gate_a, cotangent_a, mix_a, row_ids, listed + 16 + 2 * held, 128)
+    sent, other = lax.optimization_barrier((sent, other))
+    sent = with_table_rows(sent, own, other)
     received = lax.all_to_all(sent, GROUP, split_axis=0, concat_axis=0, tiled=True)
 
-    members, held = received.shape[0], own.shape[0]
+    members = received.shape[0]
     block = received[:, listed + 16 :].reshape(members * 2 * held, -1)
     codes = received[:, listed : listed + 4, :].astype(F32)
     ids = codes[:, 0::2] * ROWS_DEV + codes[:, 1::2]
@@ -298,7 +327,7 @@
     grad_table = jnp.transpose(total, (2, 0, 1, 3)).reshape(rows_dev, -1)
 
     mixed, grad_gate, grad_weights = final_outputs(
-        fetched, mix_a, mixing(slots, weights, 1), gate_a, cotangent_a, gate_b, slots
+        fetched, mix_a, mixing(slots, weights, 1, VMEM), gate_a, cotangent_a, gate_b, slots
     )
     return mixed, grad_gate, grad_weights, grad_table
 

time: 169 us -> 164 us (0.970)
  starting transfers between devices: 50.4 us -> 43.4 us
    all_to_all x1, starting transfers between devices: 12.7 us -> 6.22 us  [local(): lax.all_to_all(dense.reshape(owners, rows_dev, -1), TABLE, split_axis=0,...]
    ppermute x1, waiting for transfers between devices: 2.94 us -> 0.01 us  [quarters(): lax.ppermute(quarter(1 - zl0), ('zl1', 'zl0', 'zh'), mirrored)]
    ppermute x3, waiting for transfers between devices: 3.39 us -> 6.13 us  [from_pair(): lax.ppermute(block, RING, [((i + 2 * away) % n_y, i) for i in range(n_y)])]
    pallas_call x0 -> x1, Pallas kernels: none -> 1.71 us  [with_table_rows(): pl.pallas_call(table_rows_kernel, grid=(2,), in_specs=[rows, rows, pl.Blo...]
    unnamed x20 -> x22, local copies, waits for them, and re-layouts: 4.74 us -> 4.73 us
  transfers between devices with their start and end apart: 7 -> 7, of which waited for: 5 -> 4; matrix products, arithmetic and copies ran while one was open for 3% -> 3% of each run, Pallas kernels for 26% -> 28%
where the time goes in v6:
time: 164 us; the launch traced here: 163 us
  Pallas kernels  50.7 us (31%)
  starting transfers between devices  43.4 us (26%)
  waiting for transfers between devices  30 us (18%)
  blocking collectives  27 us (16%)
  local copies, waits for them, and re-layouts  8.78 us (5%)
  other arithmetic  2.64 us (2%)
    all_to_all x1, blocking collectives, local(): lax.all_to_all(sent, GROUP, split_axis=0, concat_axis=0, tiled=True)  27 us
    pallas_call x1, Pallas kernels, picked_rows(): pl.pallas_call(pick_kernel, grid=(members,), in_specs=[pl.BlockSpec((1, l...  24.4 us
    ppermute x1, waiting for transfers between devices, local(): total = kept + lax.ppermute(given, 'zl1', [(0, 1), (1, 0)])  15.4 us
    ppermute x3, starting transfers between devices, from_pair(): lax.ppermute(block, RING, [((i + 2 * away) % n_y, i) for i in range(n_y)])  13.9 us
    pallas_call x1, Pallas kernels, dense_rows(): pl.pallas_call(dense_kernel, grid=(rows // tile,), in_specs=[pl.BlockSpec...  11.9 us
    ppermute x1, starting transfers between devices, quarters(): lax.ppermute(quarter(1 - zl0), ('zl1', 'zl0', 'zh'), mirrored)  11.5 us
    all_to_all x1, starting transfers between devices, local(): lax.all_to_all(picked, GROUP, split_axis=0, concat_axis=0, tiled=True)  6.82 us
    pallas_call x2, Pallas kernels, mixing(): pl.pallas_call(mixing_kernel, grid=(1,), in_specs=[picks, picks], out_spe...  6.25 us
  transfers between devices with their start and end apart: 7, of which 4 were waited for; matrix products, arithmetic and copies ran while one was open for 3% of the time, Pallas kernels for 28%

profile of v6, /device:TPU:1, one launch (start us, length us, event | category | flops | bytes accessed | tf_op | source)
XLA Modules:
  0.0 163.4 jit_solution(6406864641981771157)
XLA Ops:
  0.6 1.6 %constant_dynamic-slice_fusion = (bf16[16,4096]{1,0:T(8,128)(2,1)S(1)}, bf16[16,4096]{1,0:T(8,128)(2,1)}) fusion(bf16[64,4096]{1,0:T(8,128)(2,1)} %param.11, s32[]{:T(128)S(6)} %select_n.14, s32[]{:T(128)S(6)} %select_n.13), kind=kLoop, calls=%fused_computation.9 | loop fusion | bytes 524296 | tf_op jit(solution)/shard_map/dynamic_slice | solution.py:268
  2.3 11.5 %collective-permute-start = (bf16[16,4096]{1,0:T(8,128)(2,1)S(1)}, bf16[16,4096]{1,0:T(8,128)(2,1)S(1)}, u32[]{:S(2)}, u32[]{:S(2)}) collective-permute-start(bf16[16,4096]{1,0:T(8,128)(2,1)S(1)} %get-tuple-element.22), channel_id=1, source_target_pairs={{0,385},{1,384},{128,257},{129,256},{256,129},{257,128},{384,1},{3... | collective-permute-start | bytes 393224 | tf_op jit(solution)/shard_map/ppermute | solution.py:271
  13.8 3.8 %mixing.2.mix_ref.mix_a_ref = bf16[64,128]{1,0:T(8,128)(2,1)} custom-call(s32[1,2,64,128]{3,2,1,0:T(8,128)} %slots_ref.5, f32[1,2,64,128]{3,2,1,0:T(8,128)} %weights_ref.3), custom_call_target="tpu_custom_call" | custom-call | tf_op jit(solution)/shard_map/mixing/pallas_call | solution.py:42
  17.6 3.9 %outgoing_rows.1.payload_ref = bf16[32,176,128]{2,1,0:T(8,128)(2,1)} custom-call(bf16[1,64,4096]{2,1,0:T(8,128)(2,1)} %gate_a_ref.1, bf16[1,64,4096]{2,1,0:T(8,128)(2,1)} %cot_ref.3, bf16[64,128]{1,0:T(8,128)(2,1)} %mixing.2.mix_ref.mix_a_ref, s32[1,2,1,128]{3,2,1,0:T(1,128)} %ids_ref.1), custom_call_target="tpu_custom_call" | custom-call | tf_op jit(solution)/shard_map/outgoing_rows/pallas_call | solution.py:75
  21.5 0.7 copy-done.9
  22.2 1.7 %table_rows.1 = bf16[32,176,128]{2,1,0:T(8,128)(2,1)} custom-call(bf16[16,4096]{1,0:T(8,128)(2,1)} %get-tuple-element.23.own_ref, bf16[16,4096]{1,0:T(8,128)(2,1)} %copy-done.9, bf16[32,176,128]{2,1,0:T(8,128)(2,1)} %outgoing_rows.1.payload_ref), custom_call_target="tpu_custom_call", output_to_operand_aliasing={{}: (2, {})} | custom-call | tf_op jit(solution)/shard_map/table_rows/pallas_call | solution.py:111
  23.9 27.0 %all_to_all.15.rows_ref = bf16[32,176,128]{2,1,0:T(8,128)(2,1)S(1)} all-to-all(bf16[32,176,128]{2,1,0:T(8,128)(2,1)} %table_rows.1), channel_id=1, replica_groups=mesh['zl1'=2,'zl0'=2,'c'=2,'x1'=2,'x0'=2,'y1'=4,'y0'=2,'zh'=2] {'x1','zl..., dimensions={0} | all-to-all | bytes 2883584 | tf_op jit(solution)/shard_map/all_to_all | solution.py:304
  51.0 0.1 slice.16
  51.2 6.6 %collective-permute-start.1 = (bf16[1024,128]{1,0:T(8,128)(2,1)S(1)}, bf16[1024,128]{1,0:T(8,128)(2,1)S(1)}, u32[]{:S(2)}, u32[]{:S(2)}) collective-permute-start(bf16[1024,128]{1,0:T(8,128)(2,1)S(1)} %bitcast.13), channel_id=1, source_target_pairs={{8,0},{10,2},{12,4},{14,6},{0,8},{2,10},{4,12},{6,14},{9,1},{11,3}... | collective-permute-start | bytes 786440 | tf_op jit(solution)/shard_map/ppermute | solution.py:276
  57.8 2.4 %collective-permute-start.2 = (bf16[1024,128]{1,0:T(8,128)(2,1)S(1)}, bf16[1024,128]{1,0:T(8,128)(2,1)S(1)}, u32[]{:S(2)}, u32[]{:S(2)}) collective-permute-start(bf16[1024,128]{1,0:T(8,128)(2,1)S(1)} %bitcast.14), channel_id=1, source_target_pairs={{12,0},{14,2},{0,4},{2,6},{4,8},{6,10},{8,12},{10,14},{13,1},{15,3... | collective-permute-start | bytes 786440 | tf_op jit(solution)/shard_map/ppermute | solution.py:276
  60.2 5.0 %collective-permute-start.3 = (bf16[1024,128]{1,0:T(8,128)(2,1)S(1)}, bf16[1024,128]{1,0:T(8,128)(2,1)S(1)}, u32[]{:S(2)}, u32[]{:S(2)}) collective-permute-start(bf16[1024,128]{1,0:T(8,128)(2,1)S(1)} %bitcast.15), channel_id=1, source_target_pairs={{4,0},{6,2},{8,4},{10,6},{12,8},{14,10},{0,12},{2,14},{5,1},{7,3},... | collective-permute-start | bytes 786440 | tf_op jit(solution)/shard_map/ppermute | solution.py:276
  65.3 11.9 %dense_rows.1 = bf16[4096,128]{1,0:T(8,128)(2,1)} custom-call(f32[32,128]{1,0:T(8,128)S(1)} %bitcast.17, bf16[32,176,128]{2,1,0:T(8,128)(2,1)S(1)} %all_to_all.15.rows_ref), custom_call_target="tpu_custom_call" | custom-call | flops 4294967296 | bytes 1441792 | tf_op jit(solution)/shard_map/dense_rows/pallas_call | solution.py:145
  77.1 6.1 %collective-permute-done.3.refs_3_ = bf16[1024,128]{1,0:T(8,128)(2,1)S(1)} collective-permute-done((bf16[1024,128]{1,0:T(8,128)(2,1)S(1)}, bf16[1024,128]{1,0:T(8,128)(2,1)S(1)}, u32[]{:S(2)}, u32[]{:S(2)}) %collective-permute-start.3) | collective-permute-done | bytes 262176 | tf_op jit(solution)/shard_map/ppermute | solution.py:276
  83.3 6.2 %all-to-all-start.2 = ((bf16[64,64,128]{2,1,0:T(8,128)(2,1)}), bf16[64,64,128]{2,1,0:T(8,128)(2,1)S(1)}, u32[]{:S(2)}, u32[]{:S(2)}) async-start(bf16[64,64,128]{2,1,0:T(8,128)(2,1)} %bitcast.2), calls=%async_computation.2 | async-start | bytes 2097152 | tf_op jit(solution)/shard_map/all_to_all | solution.py:314
  89.8 0.2 add.136
  90.0 0.2 add.137
  90.3 24.4 %picked_rows.1 = bf16[32,256,128]{2,1,0:T(8,128)(2,1)S(1)} custom-call(f32[32,2,128]{2,1,0:T(2,128)S(1)} %multiply_add_fusion.ids_ref, f32[4,1024]{1,0:T(4,128)S(1)} %add_convert_fusion.place_ref, bf16[1024,128]{1,0:T(8,128)(2,1)S(1)} %bitcast.16, bf16[1024,128]{1,0:T(8,128)(2,1)S(1)} %collective-permute-done.1.refs_1_, ...), custom_call_target="tpu_custom_call" | custom-call | flops 8589934592 | bytes 2097152 | tf_op jit(solution)/shard_map/picked_rows/pallas_call | solution.py:183
  114.7 1.3 copy-done
  116.1 4.7 %all-to-all-done.2 = bf16[64,64,128]{2,1,0:T(8,128)(2,1)S(1)} async-done(((bf16[64,64,128]{2,1,0:T(8,128)(2,1)}), bf16[64,64,128]{2,1,0:T(8,128)(2,1)S(1)}, u32[]{:S(2)}, u32[]{:S(2)}) %all-to-all-start.2) | async-done | bytes 1048608 | tf_op jit(solution)/shard_map/all_to_all | solution.py:314
  120.7 1.0 copy-done.7
  121.7 6.8 %all-to-all-start.1 = ((bf16[32,256,128]{2,1,0:T(8,128)(2,1)}), bf16[32,256,128]{2,1,0:T(8,128)(2,1)S(1)}, u32[]{:S(2)}, u32[]{:S(2)}) async-start(bf16[32,256,128]{2,1,0:T(8,128)(2,1)} %copy-done), calls=%async_computation.1 | async-start | bytes 4194304 | tf_op jit(solution)/shard_map/all_to_all | solution.py:319
  128.6 1.5 convert_reduce_fusion
  130.1 0.7 copy-done.8
  130.8 0.7 dynamic-slice_bitcast_fusion
  131.5 4.9 %collective-permute-start.4 = (f32[2,2,64,128]{3,2,1,0:T(8,128)}, f32[2,2,64,128]{3,2,1,0:T(8,128)S(1)}, u32[]{:S(2)}, u32[]{:S(2)}) collective-permute-start(f32[2,2,64,128]{3,2,1,0:T(8,128)} %dynamic-slice_bitcast_fusion), channel_id=1, source_target_pairs={{0,256},{256,0},{1,257},{257,1},{2,258},{258,2},{3,259},{259,3},{4... | collective-permute-start | bytes 393224 | tf_op jit(solution)/shard_map/ppermute | solution.py:326
  136.4 2.4 %mixing.3.mix_b_ref = bf16[64,128]{1,0:T(8,128)(2,1)S(1)} custom-call(s32[1,2,64,128]{3,2,1,0:T(8,128)S(1)} %copy-done.3, f32[1,2,64,128]{3,2,1,0:T(8,128)S(1)} %copy-done.5), custom_call_target="tpu_custom_call" | custom-call | tf_op jit(solution)/shard_map/mixing/pallas_call | solution.py:42
  138.9 15.4 %collective-permute-done.4 = f32[2,2,64,128]{3,2,1,0:T(8,128)S(1)} collective-permute-done((f32[2,2,64,128]{3,2,1,0:T(8,128)}, f32[2,2,64,128]{3,2,1,0:T(8,128)S(1)}, u32[]{:S(2)}, u32[]{:S(2)}) %collective-permute-start.4) | collective-permute-done | bytes 131104 | tf_op jit(solution)/shard_map/ppermute | solution.py:326
  154.2 0.9 fusion
  155.3 0.8 reshape.100
  156.0 3.8 %all-to-all-done.1.rows_ref = bf16[32,256,128]{2,1,0:T(8,128)(2,1)S(1)} async-done(((bf16[32,256,128]{2,1,0:T(8,128)(2,1)}), bf16[32,256,128]{2,1,0:T(8,128)(2,1)S(1)}, u32[]{:S(2)}, u32[]{:S(2)}) %all-to-all-start.1) | async-done | bytes 2097184 | tf_op jit(solution)/shard_map/all_to_all | solution.py:319
  159.8 1.0 copy-done.4
  160.9 2.5 %final_outputs.1 = (bf16[1,64,4096]{2,1,0:T(8,128)(2,1)}, bf16[1,64,4096]{2,1,0:T(8,128)(2,1)}, f32[1,64,128]{2,1,0:T(8,128)}) custom-call(bf16[32,256,128]{2,1,0:T(8,128)(2,1)S(1)} %all-to-all-done.1.rows_ref, bf16[64,128]{1,0:T(8,128)(2,1)S(1)} %copy-done.6, bf16[64,128]{1,0:T(8,128)(2,1)S(1)} %mixing.3.mix_b_ref, bf16[1,64,4096]{2,1,0:T(8,128)(2,1)S(1)} %copy-done.1, ...), custom_call_target="tpu_custom_call" | custom-call | tf_op jit(solution)/shard_map/final_outputs/pallas_call | solution.py:243
  (36 shorter events, 0.7 us)
Async XLA Ops:
  2.3 19.3 %collective-permute-start = (bf16[16,4096]{1,0:T(8,128)(2,1)S(1)}, bf16[16,4096]{1,0:T(8,128)(2,1)S(1)}, u32[]{:S(2)}, u32[]{:S(2)}) collective-permute-start(bf16[16,4096]{1,0:T(8,128)(2,1)S(1)} %get-tuple-element.22), channel_id=1, source_target_pairs={{0,385},{1,384},{128,257},{129,256},{256,129},{257,128},{384,1},{3... | collective-permute-start | bytes 393224 | tf_op jit(solution)/shard_map/ppermute | solution.py:271
  21.5 0.7 copy-start.9
  51.2 25.9 %collective-permute-start.1 = (bf16[1024,128]{1,0:T(8,128)(2,1)S(1)}, bf16[1024,128]{1,0:T(8,128)(2,1)S(1)}, u32[]{:S(2)}, u32[]{:S(2)}) collective-permute-start(bf16[1024,128]{1,0:T(8,128)(2,1)S(1)} %bitcast.13), channel_id=1, source_target_pairs={{8,0},{10,2},{12,4},{14,6},{0,8},{2,10},{4,12},{6,14},{9,1},{11,3}... | collective-permute-start | bytes 786440 | tf_op jit(solution)/shard_map/ppermute | solution.py:276
  57.8 19.3 %collective-permute-start.2 = (bf16[1024,128]{1,0:T(8,128)(2,1)S(1)}, bf16[1024,128]{1,0:T(8,128)(2,1)S(1)}, u32[]{:S(2)}, u32[]{:S(2)}) collective-permute-start(bf16[1024,128]{1,0:T(8,128)(2,1)S(1)} %bitcast.14), channel_id=1, source_target_pairs={{12,0},{14,2},{0,4},{2,6},{4,8},{6,10},{8,12},{10,14},{13,1},{15,3... | collective-permute-start | bytes 786440 | tf_op jit(solution)/shard_map/ppermute | solution.py:276
  60.2 23.0 %collective-permute-start.3 = (bf16[1024,128]{1,0:T(8,128)(2,1)S(1)}, bf16[1024,128]{1,0:T(8,128)(2,1)S(1)}, u32[]{:S(2)}, u32[]{:S(2)}) collective-permute-start(bf16[1024,128]{1,0:T(8,128)(2,1)S(1)} %bitcast.15), channel_id=1, source_target_pairs={{4,0},{6,2},{8,4},{10,6},{12,8},{14,10},{0,12},{2,14},{5,1},{7,3},... | collective-permute-start | bytes 786440 | tf_op jit(solution)/shard_map/ppermute | solution.py:276
  77.1 12.4 %copy-start.10 = (s32[4]{0:T(128)S(1)}, s32[4]{0:T(128)}, u32[]{:S(2)}) copy-start(s32[4]{0:T(128)} %constant.57.clone) | copy-start | bytes 52
  83.3 37.5 %all-to-all-start.2 = ((bf16[64,64,128]{2,1,0:T(8,128)(2,1)}), bf16[64,64,128]{2,1,0:T(8,128)(2,1)S(1)}, u32[]{:S(2)}, u32[]{:S(2)}) async-start(bf16[64,64,128]{2,1,0:T(8,128)(2,1)} %bitcast.2), calls=%async_computation.2 | async-start | bytes 2097152 | tf_op jit(solution)/shard_map/all_to_all | solution.py:314
  114.7 1.3 copy-start
  120.7 1.0 copy-start.7
  121.7 38.1 %all-to-all-start.1 = ((bf16[32,256,128]{2,1,0:T(8,128)(2,1)}), bf16[32,256,128]{2,1,0:T(8,128)(2,1)S(1)}, u32[]{:S(2)}, u32[]{:S(2)}) async-start(bf16[32,256,128]{2,1,0:T(8,128)(2,1)} %copy-done), calls=%async_computation.1 | async-start | bytes 4194304 | tf_op jit(solution)/shard_map/all_to_all | solution.py:319
  128.6 7.8 %copy-start.3 = (s32[1,2,64,128]{3,2,1,0:T(8,128)S(1)}, s32[1,2,64,128]{3,2,1,0:T(8,128)}, u32[]{:S(2)}) copy-start(s32[1,2,64,128]{3,2,1,0:T(8,128)} %slots_ref.5) | copy-start | bytes 196612
  128.6 7.8 %copy-start.5 = (f32[1,2,64,128]{3,2,1,0:T(8,128)S(1)}, f32[1,2,64,128]{3,2,1,0:T(8,128)}, u32[]{:S(2)}) copy-start(f32[1,2,64,128]{3,2,1,0:T(8,128)} %weights_ref.3) | copy-start | bytes 196612
  128.6 31.2 %copy-start.1 = (bf16[1,64,4096]{2,1,0:T(8,128)(2,1)S(1)}, bf16[1,64,4096]{2,1,0:T(8,128)(2,1)}, u32[]{:S(2)}) copy-start(bf16[1,64,4096]{2,1,0:T(8,128)(2,1)} %gate_a_ref.1) | copy-start | bytes 1572868
  128.6 31.2 %copy-start.2 = (bf16[1,64,4096]{2,1,0:T(8,128)(2,1)S(1)}, bf16[1,64,4096]{2,1,0:T(8,128)(2,1)}, u32[]{:S(2)}) copy-start(bf16[1,64,4096]{2,1,0:T(8,128)(2,1)} %cot_ref.3) | copy-start | bytes 1572868
  128.6 31.2 %copy-start.6 = (bf16[64,128]{1,0:T(8,128)(2,1)S(1)}, bf16[64,128]{1,0:T(8,128)(2,1)}, u32[]{:S(2)}) copy-start(bf16[64,128]{1,0:T(8,128)(2,1)} %mixing.2.mix_ref.mix_a_ref) | copy-start | bytes 49156
  130.1 0.7 copy-start.8
  131.5 22.7 %collective-permute-start.4 = (f32[2,2,64,128]{3,2,1,0:T(8,128)}, f32[2,2,64,128]{3,2,1,0:T(8,128)S(1)}, u32[]{:S(2)}, u32[]{:S(2)}) collective-permute-start(f32[2,2,64,128]{3,2,1,0:T(8,128)} %dynamic-slice_bitcast_fusion), channel_id=1, source_target_pairs={{0,256},{256,0},{1,257},{257,1},{2,258},{258,2},{3,259},{259,3},{4... | collective-permute-start | bytes 393224 | tf_op jit(solution)/shard_map/ppermute | solution.py:326
  159.8 1.0 copy-start.4

commit v7 on v6

--- a/solution.py
+++ b/solution.py
@@ -11,7 +11,7 @@
 GROUP = ("x1", "zl0", "c", "x0", "y0")
 RING = ("y1", "y0")
 ROWS_DEV = 64
-AWAY = (2, -1, 1)
+AWAY = (-1, 1, 2)
 F32 = jnp.float32
 BF16 = jnp.bfloat16
 VMEM = pltpu.CompilerParams(vmem_limit_bytes=40 * 1024 * 1024)
@@ -323,7 +323,7 @@
     mine = lax.axis_index("zl1")
     kept = lax.dynamic_index_in_dim(summed, mine, 0, keepdims=False)
     given = lax.dynamic_index_in_dim(summed, 1 - mine, 0, keepdims=False)
-    total = kept + lax.ppermute(given, "zl1", [(0, 1), (1, 0)])
+    total = kept + lax.ppermute(given.astype(BF16), "zl1", [(0, 1), (1, 0)]).astype(F32)
     grad_table = jnp.transpose(total, (2, 0, 1, 3)).reshape(rows_dev, -1)
 
     mixed, grad_gate, grad_weights = final_outputs(

time: 164 us -> 164 us (level)
  waiting for transfers between devices: 30 us -> 25 us
  starting transfers between devices: 43.4 us -> 48 us
    all_to_all x1, starting transfers between devices: 6.22 us -> 10.3 us  [local(): lax.all_to_all(dense.reshape(owners, rows_dev, -1), TABLE, split_axis=0,...]
    ppermute x3, waiting for transfers between devices: 6.13 us -> 3.38 us  [from_pair(): lax.ppermute(block, RING, [((i + 2 * away) % n_y, i) for i in range(n_y)])]
    ppermute x1, waiting for transfers between devices: 15.4 us -> 13.6 us  [local(): lax.ppermute(given.astype(BF16), 'zl1', [(0, 1), (1, 0)]).astype(F32)]
  transfers between devices with their start and end apart: 7 -> 7, of which waited for: 4 -> 4; matrix products, arithmetic and copies ran while one was open for 3% -> 3% of each run, Pallas kernels for 28% -> 29%
where the time goes in v7:
time: 164 us; the launch traced here: 162 us
  Pallas kernels  50.7 us (31%)
  starting transfers between devices  48 us (29%)
  blocking collectives  27 us (16%)
  waiting for transfers between devices  25 us (15%)
  local copies, waits for them, and re-layouts  8.12 us (5%)
  other arithmetic  2.64 us (2%)
    all_to_all x1, blocking collectives, local(): lax.all_to_all(sent, GROUP, split_axis=0, concat_axis=0, tiled=True)  27 us
    pallas_call x1, Pallas kernels, picked_rows(): pl.pallas_call(pick_kernel, grid=(members,), in_specs=[pl.BlockSpec((1, l...  24.4 us
    ppermute x3, starting transfers between devices, from_pair(): lax.ppermute(block, RING, [((i + 2 * away) % n_y, i) for i in range(n_y)])  13.9 us
    ppermute x1, waiting for transfers between devices, local(): lax.ppermute(given.astype(BF16), 'zl1', [(0, 1), (1, 0)]).astype(F32)  13.6 us
    pallas_call x1, Pallas kernels, dense_rows(): pl.pallas_call(dense_kernel, grid=(rows // tile,), in_specs=[pl.BlockSpec...  11.9 us
    ppermute x1, starting transfers between devices, quarters(): lax.ppermute(quarter(1 - zl0), ('zl1', 'zl0', 'zh'), mirrored)  11.5 us
    all_to_all x1, starting transfers between devices, local(): lax.all_to_all(dense.reshape(owners, rows_dev, -1), TABLE, split_axis=0,...  10.3 us
    all_to_all x1, starting transfers between devices, local(): lax.all_to_all(picked, GROUP, split_axis=0, concat_axis=0, tiled=True)  7.35 us
  transfers between devices with their start and end apart: 7, of which 4 were waited for; matrix products, arithmetic and copies ran while one was open for 3% of the time, Pallas kernels for 29%

profile of v7, /device:TPU:1, one launch (start us, length us, event | category | flops | bytes accessed | tf_op | source)
XLA Modules:
  0.0 162.4 jit_solution(17424892306391104597)
XLA Ops:
  0.6 1.6 %constant_dynamic-slice_fusion = (bf16[16,4096]{1,0:T(8,128)(2,1)S(1)}, bf16[16,4096]{1,0:T(8,128)(2,1)}) fusion(bf16[64,4096]{1,0:T(8,128)(2,1)} %param.11, s32[]{:T(128)S(6)} %select_n.14, s32[]{:T(128)S(6)} %select_n.13), kind=kLoop, calls=%fused_computation.10 | loop fusion | bytes 524296 | tf_op jit(solution)/shard_map/dynamic_slice | solution.py:268
  2.3 11.5 %collective-permute-start = (bf16[16,4096]{1,0:T(8,128)(2,1)S(1)}, bf16[16,4096]{1,0:T(8,128)(2,1)S(1)}, u32[]{:S(2)}, u32[]{:S(2)}) collective-permute-start(bf16[16,4096]{1,0:T(8,128)(2,1)S(1)} %get-tuple-element.22), channel_id=1, source_target_pairs={{0,385},{1,384},{128,257},{129,256},{256,129},{257,128},{384,1},{3... | collective-permute-start | bytes 393224 | tf_op jit(solution)/shard_map/ppermute | solution.py:271
  13.8 3.8 %mixing.2.mix_ref.mix_a_ref = bf16[64,128]{1,0:T(8,128)(2,1)} custom-call(s32[1,2,64,128]{3,2,1,0:T(8,128)} %slots_ref.5, f32[1,2,64,128]{3,2,1,0:T(8,128)} %weights_ref.3), custom_call_target="tpu_custom_call" | custom-call | tf_op jit(solution)/shard_map/mixing/pallas_call | solution.py:42
  17.6 3.9 %outgoing_rows.1.payload_ref = bf16[32,176,128]{2,1,0:T(8,128)(2,1)} custom-call(bf16[1,64,4096]{2,1,0:T(8,128)(2,1)} %gate_a_ref.1, bf16[1,64,4096]{2,1,0:T(8,128)(2,1)} %cot_ref.3, bf16[64,128]{1,0:T(8,128)(2,1)} %mixing.2.mix_ref.mix_a_ref, s32[1,2,1,128]{3,2,1,0:T(1,128)} %ids_ref.1), custom_call_target="tpu_custom_call" | custom-call | tf_op jit(solution)/shard_map/outgoing_rows/pallas_call | solution.py:75
  21.5 0.7 copy-done.9
  22.2 1.7 %table_rows.1 = bf16[32,176,128]{2,1,0:T(8,128)(2,1)} custom-call(bf16[16,4096]{1,0:T(8,128)(2,1)} %get-tuple-element.23.own_ref, bf16[16,4096]{1,0:T(8,128)(2,1)} %copy-done.9, bf16[32,176,128]{2,1,0:T(8,128)(2,1)} %outgoing_rows.1.payload_ref), custom_call_target="tpu_custom_call", output_to_operand_aliasing={{}: (2, {})} | custom-call | tf_op jit(solution)/shard_map/table_rows/pallas_call | solution.py:111
  23.9 27.0 %all_to_all.15.rows_ref = bf16[32,176,128]{2,1,0:T(8,128)(2,1)S(1)} all-to-all(bf16[32,176,128]{2,1,0:T(8,128)(2,1)} %table_rows.1), channel_id=1, replica_groups=mesh['zl1'=2,'zl0'=2,'c'=2,'x1'=2,'x0'=2,'y1'=4,'y0'=2,'zh'=2] {'x1','zl..., dimensions={0} | all-to-all | bytes 2883584 | tf_op jit(solution)/shard_map/all_to_all | solution.py:304
  51.0 0.1 slice.16
  51.1 0.1 slice.17
  51.2 4.2 %collective-permute-start.1 = (bf16[1024,128]{1,0:T(8,128)(2,1)S(1)}, bf16[1024,128]{1,0:T(8,128)(2,1)S(1)}, u32[]{:S(2)}, u32[]{:S(2)}) collective-permute-start(bf16[1024,128]{1,0:T(8,128)(2,1)S(1)} %bitcast.13), channel_id=1, source_target_pairs={{12,0},{14,2},{0,4},{2,6},{4,8},{6,10},{8,12},{10,14},{13,1},{15,3... | collective-permute-start | bytes 786440 | tf_op jit(solution)/shard_map/ppermute | solution.py:276
  55.5 3.2 %collective-permute-start.2 = (bf16[1024,128]{1,0:T(8,128)(2,1)S(1)}, bf16[1024,128]{1,0:T(8,128)(2,1)S(1)}, u32[]{:S(2)}, u32[]{:S(2)}) collective-permute-start(bf16[1024,128]{1,0:T(8,128)(2,1)S(1)} %bitcast.14), channel_id=1, source_target_pairs={{4,0},{6,2},{8,4},{10,6},{12,8},{14,10},{0,12},{2,14},{5,1},{7,3},... | collective-permute-start | bytes 786440 | tf_op jit(solution)/shard_map/ppermute | solution.py:276
  58.6 6.6 %collective-permute-start.3 = (bf16[1024,128]{1,0:T(8,128)(2,1)S(1)}, bf16[1024,128]{1,0:T(8,128)(2,1)S(1)}, u32[]{:S(2)}, u32[]{:S(2)}) collective-permute-start(bf16[1024,128]{1,0:T(8,128)(2,1)S(1)} %bitcast.15), channel_id=1, source_target_pairs={{8,0},{10,2},{12,4},{14,6},{0,8},{2,10},{4,12},{6,14},{9,1},{11,3}... | collective-permute-start | bytes 786440 | tf_op jit(solution)/shard_map/ppermute | solution.py:276
  65.3 11.9 %dense_rows.1 = bf16[4096,128]{1,0:T(8,128)(2,1)} custom-call(f32[32,128]{1,0:T(8,128)S(1)} %bitcast.17, bf16[32,176,128]{2,1,0:T(8,128)(2,1)S(1)} %all_to_all.15.rows_ref), custom_call_target="tpu_custom_call" | custom-call | flops 4294967296 | bytes 1441792 | tf_op jit(solution)/shard_map/dense_rows/pallas_call | solution.py:145
  77.1 3.4 %collective-permute-done.3.refs_3_ = bf16[1024,128]{1,0:T(8,128)(2,1)S(1)} collective-permute-done((bf16[1024,128]{1,0:T(8,128)(2,1)S(1)}, bf16[1024,128]{1,0:T(8,128)(2,1)S(1)}, u32[]{:S(2)}, u32[]{:S(2)}) %collective-permute-start.3) | collective-permute-done | bytes 262176 | tf_op jit(solution)/shard_map/ppermute | solution.py:276
  80.5 10.3 %all-to-all-start.2 = ((bf16[64,64,128]{2,1,0:T(8,128)(2,1)}), bf16[64,64,128]{2,1,0:T(8,128)(2,1)S(1)}, u32[]{:S(2)}, u32[]{:S(2)}) async-start(bf16[64,64,128]{2,1,0:T(8,128)(2,1)} %bitcast.2), calls=%async_computation.2 | async-start | bytes 2097152 | tf_op jit(solution)/shard_map/all_to_all | solution.py:314
  91.1 0.2 add.136
  91.4 0.2 add.137
  91.7 24.4 %picked_rows.1 = bf16[32,256,128]{2,1,0:T(8,128)(2,1)S(1)} custom-call(f32[32,2,128]{2,1,0:T(2,128)S(1)} %multiply_add_fusion.ids_ref, f32[4,1024]{1,0:T(4,128)S(1)} %add_convert_fusion.place_ref, bf16[1024,128]{1,0:T(8,128)(2,1)S(1)} %bitcast.16, bf16[1024,128]{1,0:T(8,128)(2,1)S(1)} %collective-permute-done.1.refs_1_, ...), custom_call_target="tpu_custom_call" | custom-call | flops 8589934592 | bytes 2097152 | tf_op jit(solution)/shard_map/picked_rows/pallas_call | solution.py:183
  116.1 1.3 copy-done
  117.4 4.2 %all-to-all-done.2 = bf16[64,64,128]{2,1,0:T(8,128)(2,1)S(1)} async-done(((bf16[64,64,128]{2,1,0:T(8,128)(2,1)}), bf16[64,64,128]{2,1,0:T(8,128)(2,1)S(1)}, u32[]{:S(2)}, u32[]{:S(2)}) %all-to-all-start.2) | async-done | bytes 1048608 | tf_op jit(solution)/shard_map/all_to_all | solution.py:314
  121.6 1.0 copy-done.7
  122.5 7.3 %all-to-all-start.1 = ((bf16[32,256,128]{2,1,0:T(8,128)(2,1)}), bf16[32,256,128]{2,1,0:T(8,128)(2,1)S(1)}, u32[]{:S(2)}, u32[]{:S(2)}) async-start(bf16[32,256,128]{2,1,0:T(8,128)(2,1)} %copy-done), calls=%async_computation.1 | async-start | bytes 4194304 | tf_op jit(solution)/shard_map/all_to_all | solution.py:319
  130.0 1.5 convert_reduce_fusion
  131.5 0.7 copy-done.8
  132.2 4.9 %collective-permute-start.4 = (bf16[2,2,64,128]{3,2,1,0:T(8,128)(2,1)S(1)}, bf16[2,2,64,128]{3,2,1,0:T(8,128)(2,1)S(1)}, u32[]{:S(2)}, u32[]{:S(2)}) collective-permute-start(bf16[2,2,64,128]{3,2,1,0:T(8,128)(2,1)S(1)} %fusion.1), channel_id=1, source_target_pairs={{0,256},{256,0},{1,257},{257,1},{2,258},{258,2},{3,259},{259,3},{4... | collective-permute-start | bytes 196616 | tf_op jit(solution)/shard_map/ppermute | solution.py:326
  137.1 2.4 %mixing.3.mix_b_ref = bf16[64,128]{1,0:T(8,128)(2,1)S(1)} custom-call(s32[1,2,64,128]{3,2,1,0:T(8,128)S(1)} %copy-done.3, f32[1,2,64,128]{3,2,1,0:T(8,128)S(1)} %copy-done.5), custom_call_target="tpu_custom_call" | custom-call | tf_op jit(solution)/shard_map/mixing/pallas_call | solution.py:42
  139.6 13.6 %collective-permute-done.4 = bf16[2,2,64,128]{3,2,1,0:T(8,128)(2,1)S(1)} collective-permute-done((bf16[2,2,64,128]{3,2,1,0:T(8,128)(2,1)S(1)}, bf16[2,2,64,128]{3,2,1,0:T(8,128)(2,1)S(1)}, u32[]{:S(2)}, u32[]{:S(2)}) %collective-permute-start.4) | collective-permute-done | bytes 65568 | tf_op jit(solution)/shard_map/ppermute | solution.py:326
  153.1 0.9 fusion
  154.2 0.8 reshape.101
  154.9 3.9 %all-to-all-done.1.rows_ref = bf16[32,256,128]{2,1,0:T(8,128)(2,1)S(1)} async-done(((bf16[32,256,128]{2,1,0:T(8,128)(2,1)}), bf16[32,256,128]{2,1,0:T(8,128)(2,1)S(1)}, u32[]{:S(2)}, u32[]{:S(2)}) %all-to-all-start.1) | async-done | bytes 2097184 | tf_op jit(solution)/shard_map/all_to_all | solution.py:319
  158.8 1.0 copy-done.4
  159.8 2.5 %final_outputs.1 = (bf16[1,64,4096]{2,1,0:T(8,128)(2,1)}, bf16[1,64,4096]{2,1,0:T(8,128)(2,1)}, f32[1,64,128]{2,1,0:T(8,128)}) custom-call(bf16[32,256,128]{2,1,0:T(8,128)(2,1)S(1)} %all-to-all-done.1.rows_ref, bf16[64,128]{1,0:T(8,128)(2,1)S(1)} %copy-done.6, bf16[64,128]{1,0:T(8,128)(2,1)S(1)} %mixing.3.mix_b_ref, bf16[1,64,4096]{2,1,0:T(8,128)(2,1)S(1)} %copy-done.1, ...), custom_call_target="tpu_custom_call" | custom-call | tf_op jit(solution)/shard_map/final_outputs/pallas_call | solution.py:243
  (36 shorter events, 0.6 us)
Async XLA Ops:
  2.3 19.3 %collective-permute-start = (bf16[16,4096]{1,0:T(8,128)(2,1)S(1)}, bf16[16,4096]{1,0:T(8,128)(2,1)S(1)}, u32[]{:S(2)}, u32[]{:S(2)}) collective-permute-start(bf16[16,4096]{1,0:T(8,128)(2,1)S(1)} %get-tuple-element.22), channel_id=1, source_target_pairs={{0,385},{1,384},{128,257},{129,256},{256,129},{257,128},{384,1},{3... | collective-permute-start | bytes 393224 | tf_op jit(solution)/shard_map/ppermute | solution.py:271
  21.5 0.7 copy-start.9
  51.2 25.9 %collective-permute-start.1 = (bf16[1024,128]{1,0:T(8,128)(2,1)S(1)}, bf16[1024,128]{1,0:T(8,128)(2,1)S(1)}, u32[]{:S(2)}, u32[]{:S(2)}) collective-permute-start(bf16[1024,128]{1,0:T(8,128)(2,1)S(1)} %bitcast.13), channel_id=1, source_target_pairs={{12,0},{14,2},{0,4},{2,6},{4,8},{6,10},{8,12},{10,14},{13,1},{15,3... | collective-permute-start | bytes 786440 | tf_op jit(solution)/shard_map/ppermute | solution.py:276
  55.5 21.7 %collective-permute-start.2 = (bf16[1024,128]{1,0:T(8,128)(2,1)S(1)}, bf16[1024,128]{1,0:T(8,128)(2,1)S(1)}, u32[]{:S(2)}, u32[]{:S(2)}) collective-permute-start(bf16[1024,128]{1,0:T(8,128)(2,1)S(1)} %bitcast.14), channel_id=1, source_target_pairs={{4,0},{6,2},{8,4},{10,6},{12,8},{14,10},{0,12},{2,14},{5,1},{7,3},... | collective-permute-start | bytes 786440 | tf_op jit(solution)/shard_map/ppermute | solution.py:276
  58.6 21.9 %collective-permute-start.3 = (bf16[1024,128]{1,0:T(8,128)(2,1)S(1)}, bf16[1024,128]{1,0:T(8,128)(2,1)S(1)}, u32[]{:S(2)}, u32[]{:S(2)}) collective-permute-start(bf16[1024,128]{1,0:T(8,128)(2,1)S(1)} %bitcast.15), channel_id=1, source_target_pairs={{8,0},{10,2},{12,4},{14,6},{0,8},{2,10},{4,12},{6,14},{9,1},{11,3}... | collective-permute-start | bytes 786440 | tf_op jit(solution)/shard_map/ppermute | solution.py:276
  77.1 13.7 %copy-start.10 = (s32[4]{0:T(128)S(1)}, s32[4]{0:T(128)}, u32[]{:S(2)}) copy-start(s32[4]{0:T(128)} %constant.57.clone) | copy-start | bytes 52
  80.5 41.0 %all-to-all-start.2 = ((bf16[64,64,128]{2,1,0:T(8,128)(2,1)}), bf16[64,64,128]{2,1,0:T(8,128)(2,1)S(1)}, u32[]{:S(2)}, u32[]{:S(2)}) async-start(bf16[64,64,128]{2,1,0:T(8,128)(2,1)} %bitcast.2), calls=%async_computation.2 | async-start | bytes 2097152 | tf_op jit(solution)/shard_map/all_to_all | solution.py:314
  116.1 1.3 copy-start
  121.5 1.0 copy-start.7
  122.5 36.3 %all-to-all-start.1 = ((bf16[32,256,128]{2,1,0:T(8,128)(2,1)}), bf16[32,256,128]{2,1,0:T(8,128)(2,1)S(1)}, u32[]{:S(2)}, u32[]{:S(2)}) async-start(bf16[32,256,128]{2,1,0:T(8,128)(2,1)} %copy-done), calls=%async_computation.1 | async-start | bytes 4194304 | tf_op jit(solution)/shard_map/all_to_all | solution.py:319
  129.9 7.2 %copy-start.3 = (s32[1,2,64,128]{3,2,1,0:T(8,128)S(1)}, s32[1,2,64,128]{3,2,1,0:T(8,128)}, u32[]{:S(2)}) copy-start(s32[1,2,64,128]{3,2,1,0:T(8,128)} %slots_ref.5) | copy-start | bytes 196612
  129.9 7.2 %copy-start.5 = (f32[1,2,64,128]{3,2,1,0:T(8,128)S(1)}, f32[1,2,64,128]{3,2,1,0:T(8,128)}, u32[]{:S(2)}) copy-start(f32[1,2,64,128]{3,2,1,0:T(8,128)} %weights_ref.3) | copy-start | bytes 196612
  129.9 28.9 %copy-start.1 = (bf16[1,64,4096]{2,1,0:T(8,128)(2,1)S(1)}, bf16[1,64,4096]{2,1,0:T(8,128)(2,1)}, u32[]{:S(2)}) copy-start(bf16[1,64,4096]{2,1,0:T(8,128)(2,1)} %gate_a_ref.1) | copy-start | bytes 1572868
  129.9 28.9 %copy-start.2 = (bf16[1,64,4096]{2,1,0:T(8,128)(2,1)S(1)}, bf16[1,64,4096]{2,1,0:T(8,128)(2,1)}, u32[]{:S(2)}) copy-start(bf16[1,64,4096]{2,1,0:T(8,128)(2,1)} %cot_ref.3) | copy-start | bytes 1572868
  129.9 28.9 %copy-start.6 = (bf16[64,128]{1,0:T(8,128)(2,1)S(1)}, bf16[64,128]{1,0:T(8,128)(2,1)}, u32[]{:S(2)}) copy-start(bf16[64,128]{1,0:T(8,128)(2,1)} %mixing.2.mix_ref.mix_a_ref) | copy-start | bytes 49156
  131.5 0.7 copy-start.8
  132.2 20.9 %collective-permute-start.4 = (bf16[2,2,64,128]{3,2,1,0:T(8,128)(2,1)S(1)}, bf16[2,2,64,128]{3,2,1,0:T(8,128)(2,1)S(1)}, u32[]{:S(2)}, u32[]{:S(2)}) collective-permute-start(bf16[2,2,64,128]{3,2,1,0:T(8,128)(2,1)S(1)} %fusion.1), channel_id=1, source_target_pairs={{0,256},{256,0},{1,257},{257,1},{2,258},{258,2},{3,259},{259,3},{4... | collective-permute-start | bytes 196616 | tf_op jit(solution)/shard_map/ppermute | solution.py:326
  158.8 1.0 copy-start.4
